TPU v7x, 32 devices: a whole 2x2x4 slice. The times are simulated.
32 devices in a mesh: flake: 2 (over y), trow: 16 (over z, x, core).
Axes of the slice: x: 2, y: 2, z: 4, core: 2. Of those that a mesh axis runs over, the one named last changes fastest.
Arguments:
- green: bfloat16 [192, 9, 4, 128, 128], P(('flake', 'trow')), parts along dimension 0, may hold values from -6 to 6
- integrals: bfloat16 [192, 9, 128, 128], P(('flake', 'trow')), parts along dimension 0, may hold values from -2 to 2
- pattern: int32 [192, 9], P(('flake', 'trow')), parts along dimension 0, may hold values from 0 to 1, as said below
- coefficients: bfloat16 [24576, 512], P(('flake', 'trow')), parts along dimension 0, may hold values from -0.0546875 to 0.0546875
Outputs:
- sigma_freq: float32 [2, 128, 1024, 512], P(None, None, ('flake', 'trow')), parts along dimension 2
There are 2 independent parts, one for each index of `flake`. A program takes and returns all parts, laid end to end along the dimension named above; each array names one. Nothing has to cross between parts.
Inputs may be any that keep to these rules, and one draw needn't show every extreme that they name: pattern[r, s] is 1 where tile row r holds the tile of column r + s - 4; the diagonal slot s = 4 is always 1, and tile row 0 has all 9 slots.
All inputs are finite; a program needn't handle non-finite values.
Results may differ from a plain program's by a relative error of at most 0.005.
Values may be sent and summed in bfloat16 or wider, within the bound.
No kernel may reach another device: no remote copies, remote signals or barrier semaphores. Data moves between devices by JAX's collectives and lax.ppermute only.
A program may use at most 192 MiB of HBM per device.

v0:
```python
import functools

import jax
import jax.numpy as jnp
import numpy as np
from jax import lax
from jax.experimental import pallas as pl
from jax.experimental.pallas import tpu as pltpu
from jax.sharding import PartitionSpec as P

TILE = 128
BAND = 4
TAU = 4
PAIRS = TAU // 2
NMO = 512
NW = 128
SLOTS = 9
FREQ_BLOCK = 16
GROUP = 4
MIB = 1 << 20


def tiles_kernel(
    count, pattern, green, integrals, coefficients, near, part, sigma, transposed, gbuf, ibuf, window, order, sems, csems
):
    first = lax.rem(lax.axis_index("trow"), 2) == 0
    inside = count + BAND
    own_at = pl.multiple_of(jnp.where(first, 0, BAND * TILE), TILE)
    near_at = pl.multiple_of(jnp.where(first, count * TILE, 0), TILE)

    def fetch(index):
        row, slot = index // SLOTS, index % SLOTS
        return (
            pltpu.make_async_copy(green.at[row, slot], gbuf.at[index], sems.at[index, 0]),
            pltpu.make_async_copy(integrals.at[row, slot], ibuf.at[index], sems.at[index, 1]),
        )

    def enlist(index, found):
        present = pattern[index // SLOTS, index % SLOTS] != 0

        @pl.when(present)
        def _():
            order[found] = index
            for copy in fetch(index):
                copy.start()

        return found + present.astype(jnp.int32)

    own_copy = pltpu.make_async_copy(coefficients, window.at[pl.ds(own_at, count * TILE)], csems.at[0])
    near_copy = pltpu.make_async_copy(near, window.at[pl.ds(near_at, BAND * TILE)], csems.at[1])
    own_copy.start()
    near_copy.start()
    found = lax.fori_loop(0, count * SLOTS, enlist, jnp.int32(0))
    for extra in range(GROUP - 1):
        order[found + extra] = order[found - 1]
    sigma[...] = jnp.zeros_like(sigma)
    own_copy.wait()
    for row in range(count):
        block = window[pl.ds(pl.multiple_of(own_at + row * TILE, TILE), TILE), :]
        transposed[:, row * TILE : (row + 1) * TILE] = block.T

    @pl.loop(0, pl.cdiv(found, GROUP))
    def _(group):
        indices = [order[group * GROUP + member] for member in range(GROUP)]
        for member, index in enumerate(indices):

            @pl.when(group * GROUP + member < found)
            def _():
                for copy in fetch(index):
                    copy.wait()

        for index in indices:
            paired = jnp.concatenate([gbuf[index, t] * gbuf[index, TAU - 1 - t] for t in range(PAIRS)], axis=0)
            product = jnp.dot(paired, ibuf[index], preferred_element_type=jnp.float32)
            sigma[index // SLOTS, index % SLOTS] = product.astype(jnp.bfloat16)

    near_copy.wait()

    def reduce_rows(low):
        for row in range(count):
            begin, end = max(0, low - row), min(SLOTS, low + inside - row)
            lhs = jnp.concatenate([sigma[row, slot] for slot in range(begin, end)], axis=1)
            rhs = window[(row + begin - low) * TILE : (row + end - low) * TILE, :]
            part[row] = jnp.dot(lhs, rhs, preferred_element_type=jnp.float32)

    @pl.when(first)
    def _():
        reduce_rows(BAND)

    @pl.when(jnp.logical_not(first))
    def _():
        reduce_rows(0)


def tiles(green, integrals, pattern, coefficients, near):
    count = green.shape[0]
    hbm = pl.BlockSpec(memory_space=pltpu.HBM)
    vmem = pl.BlockSpec(memory_space=pltpu.VMEM)
    placed = [pltpu.with_memory_space_constraint(x, pltpu.HBM) for x in (green, integrals, coefficients)]
    return pl.pallas_call(
        functools.partial(tiles_kernel, count),
        out_shape=(
            pltpu.VMEM((count, PAIRS * TILE, NMO), jnp.float32),
            pltpu.VMEM((count, SLOTS, PAIRS * TILE, TILE), jnp.bfloat16),
            pltpu.VMEM((NMO, count * TILE), jnp.bfloat16),
        ),
        in_specs=[pl.BlockSpec(memory_space=pltpu.SMEM), hbm, hbm, hbm, vmem],
        out_specs=(vmem, vmem, vmem),
        scratch_shapes=[
            pltpu.VMEM((count * SLOTS, TAU, TILE, TILE), jnp.bfloat16),
            pltpu.VMEM((count * SLOTS, TILE, TILE), jnp.bfloat16),
            pltpu.VMEM(((count + BAND) * TILE, NMO), jnp.bfloat16),
            pltpu.SMEM((count * SLOTS + GROUP,), jnp.int32),
            pltpu.SemaphoreType.DMA((count * SLOTS, 2)),
            pltpu.SemaphoreType.DMA((2,)),
        ],
        compiler_params=pltpu.CompilerParams(vmem_limit_bytes=24 * MIB),
        cost_estimate=pl.CostEstimate(flops=2_000_000_000, bytes_accessed=12_000_000, transcendentals=0),
        name="tiles",
    )(pattern, *placed, pltpu.with_memory_space_constraint(near, pltpu.VMEM))


def project_kernel(count, split, part, sigma, halo, transposed, *refs):
    outs, half = refs[:-1], refs[-1]
    me = lax.axis_index("trow")
    first = lax.rem(me, 2) == 0

    def store(row, value):
        for t in range(PAIRS):
            half[t, row * TILE : (row + 1) * TILE, :] = value[t * TILE : (t + 1) * TILE].astype(jnp.bfloat16)

    def add_far(low):
        for row in range(count):
            if low:
                slots = range(0, max(0, BAND - row))
                at = row
            else:
                slots = range(min(SLOTS, count + BAND - row), SLOTS)
                at = 0
            value = part[row]
            if slots:
                lhs = jnp.concatenate([sigma[row, slot] for slot in slots], axis=1)
                rhs = halo[at * TILE : (at + len(slots)) * TILE, :]
                value = value + jnp.dot(lhs, rhs, preferred_element_type=jnp.float32)
            store(row, value)

    @pl.when(first)
    def _():
        add_far(BAND)

    @pl.when(jnp.logical_not(first))
    def _():
        add_far(0)

    for k in range(NMO // TILE):
        chunk = lax.bitwise_xor(lax.div(me, 4), k) if split else k
        lhs = transposed[pl.ds(pl.multiple_of(chunk * TILE, TILE), TILE), :]
        for t in range(PAIRS):
            columns = slice(t * NMO, (t + 1) * NMO)
            total = jnp.dot(lhs, half[t], preferred_element_type=jnp.float32)
            if split:
                keep, send = outs
                upper, lower = total[: TILE // 2], total[TILE // 2 :]
                keep[k, :, columns] = jnp.where(first, upper, lower)
                send[k, :, columns] = jnp.where(first, lower, upper).astype(jnp.bfloat16)
            else:
                outs[0][k * TILE : (k + 1) * TILE, columns] = total


def project(part, sigma, halo, transposed, split):
    count = part.shape[0]
    vmem = pl.BlockSpec(memory_space=pltpu.VMEM)
    if split:
        shape = (NMO // TILE, TILE // 2, PAIRS * NMO)
        out_shape = (pltpu.VMEM(shape, jnp.float32), pltpu.VMEM(shape, jnp.bfloat16))
    else:
        out_shape = (jax.ShapeDtypeStruct((NMO, PAIRS * NMO), jnp.float32),)
    return pl.pallas_call(
        functools.partial(project_kernel, count, split),
        out_shape=out_shape,
        in_specs=[vmem] * 4,
        out_specs=tuple(vmem for _ in out_shape),
        scratch_shapes=[pltpu.VMEM((PAIRS, count * TILE, NMO), jnp.bfloat16)],
        compiler_params=pltpu.CompilerParams(vmem_limit_bytes=24 * MIB),
        cost_estimate=pl.CostEstimate(flops=1_600_000_000, bytes_accessed=6_000_000, transcendentals=0),
        name="project",
    )(*[pltpu.with_memory_space_constraint(x, pltpu.VMEM) for x in (part, sigma, halo, transposed)])


def freq_tables():
    point = np.arange(TAU, dtype=np.float32)
    freq = np.arange(NW, dtype=np.float32)
    pi = np.float32(np.pi)
    theta = pi * (np.float32(2.0) * point + np.float32(1.0)) / np.float32(2.0 * TAU)
    nodes = np.float32(0.5) * (np.float32(1.0) - np.cos(theta))
    weights = np.float32(np.pi / (2.0 * TAU)) * np.sin(theta)
    angle = pi * (np.float32(2.0) * freq[:, None] + np.float32(1.0)) * nodes[None, :]
    both = np.concatenate([weights[None, :] * np.cos(angle), weights[None, :] * np.sin(angle)], axis=0)
    folded = both[:, :PAIRS] + both[:, : PAIRS - 1 : -1]
    return folded.astype(np.float32).reshape(-1)


def frequency_kernel(table, mine, other, out, buffer, sems):
    points = [
        mine[:, t * NMO : (t + 1) * NMO] + other[:, t * NMO : (t + 1) * NMO] for t in range(PAIRS)
    ]

    def copy(step):
        rows = pl.ds(step * FREQ_BLOCK, FREQ_BLOCK)
        return pltpu.make_async_copy(buffer.at[rows], out.at[rows], sems.at[step])

    @pl.loop(0, 2 * NW // FREQ_BLOCK)
    def _(step):
        @pl.loop(0, FREQ_BLOCK, unroll=4)
        def _(n):
            at = (step * FREQ_BLOCK + n) * PAIRS
            value = table[at] * points[0]
            for t in range(1, PAIRS):
                value = value + table[at + t] * points[t]
            buffer[step * FREQ_BLOCK + n] = value

        copy(step).start()

    @pl.loop(0, 2 * NW // FREQ_BLOCK)
    def _(step):
        copy(step).wait()


def frequency(mine, other):
    rows = mine.shape[0]
    vmem = pl.BlockSpec(memory_space=pltpu.VMEM)
    out = pl.pallas_call(
        frequency_kernel,
        out_shape=jax.ShapeDtypeStruct((2 * NW, rows, NMO), jnp.float32),
        in_specs=[pl.BlockSpec(memory_space=pltpu.SMEM), vmem, vmem],
        out_specs=pl.BlockSpec(memory_space=pl.ANY),
        scratch_shapes=[
            pltpu.VMEM((2 * NW, rows, NMO), jnp.float32),
            pltpu.SemaphoreType.DMA((2 * NW // FREQ_BLOCK,)),
        ],
        compiler_params=pltpu.CompilerParams(vmem_limit_bytes=24 * MIB),
        cost_estimate=pl.CostEstimate(flops=50_000_000, bytes_accessed=17_000_000, transcendentals=0),
        name="frequency",
    )(jnp.asarray(freq_tables()), mine, other)
    return out.reshape(2, NW, rows, NMO)


def local(devices, green, integrals, pattern, coefficients):
    rows = coefficients.shape[0]
    width = BAND * TILE
    core = lax.rem(lax.axis_index("trow"), 2)
    away = lax.dynamic_slice_in_dim(coefficients, core * (rows - width), width, axis=0)
    pairs = [(i, i + 1) for i in range(1, devices - 1, 2)]
    halo = lax.ppermute(away, "trow", pairs + [(b, a) for a, b in pairs])
    inner = lax.dynamic_slice_in_dim(coefficients, (1 - core) * (rows - width), width, axis=0)
    near = lax.ppermute(inner, "trow", [(i, i ^ 1) for i in range(devices)])
    part, far, transposed = tiles(green, integrals, pattern, coefficients, near)
    if devices != 16:
        (summed,) = project(part, far, halo, transposed, False)
        total = lax.psum_scatter(summed, "trow", scatter_dimension=0, tiled=True)
        return frequency(total, jnp.zeros_like(total))
    keep, send = project(part, far, halo, transposed, True)
    arrived = lax.ppermute(send, "trow", [(i, i ^ 1) for i in range(devices)])
    pieces = [(keep[k] + arrived[k].astype(jnp.float32)).astype(jnp.bfloat16) for k in range(4)]
    got = []
    for k in range(4):
        moves = []
        for i in range(devices):
            z, x, c = i // 4, i // 2 % 2, i % 2
            moves.append((i, ((z ^ k) * 2 + c) * 2 + x))
        got.append(lax.ppermute(pieces[k], "trow", moves))
    total = got[0].astype(jnp.float32)
    for piece in got[1:]:
        total = total + piece.astype(jnp.float32)
    count = total.shape[0] // 2
    mine = lax.dynamic_slice_in_dim(total, core * count, count, axis=0)
    other = lax.dynamic_slice_in_dim(total, (1 - core) * count, count, axis=0)
    other = lax.ppermute(other, "trow", [(i, i ^ 1) for i in range(devices)])
    return frequency(mine, other)


def solution(mesh):
    in_specs = (
        P(("flake", "trow"), None, None, None, None),
        P(("flake", "trow"), None, None, None),
        P(("flake", "trow"), None),
        P(("flake", "trow"), None),
    )
    out_specs = P(None, None, ("flake", "trow"), None)
    return jax.shard_map(
        functools.partial(local, mesh.shape["trow"]),
        mesh=mesh,
        in_specs=in_specs,
        out_specs=out_specs,
        check_vma=False,
    )
```

profile of v0, /device:TPU:0, one launch (start us, length us, event | category | flops | bytes accessed | tf_op | source)
XLA Modules:
  0.0 46.9 jit_solution(11405145352018434348)
XLA Ops:
  0.0 1.3 %constant_dynamic-slice_fusion.2 = (bf16[512,512]{1,0:T(8,128)(2,1)S(1)}, bf16[512,512]{1,0:T(8,128)(2,1)S(1)}) fusion(bf16[768,512]{1,0:T(8,128)(2,1)} %coefficients.1, s32[]{:T(128)S(6)} %select_n.13, s32[]{:T(128)S(6)} %select_n.12), kind=kLoop, calls=%fused_computation.11 | loop fusion | bytes 2097160 | tf_op jit(solution)/shard_map/dynamic_slice | solution.py:252
  1.3 0.5 %collective-permute-start = (bf16[512,512]{1,0:T(8,128)(2,1)S(1)}, bf16[512,512]{1,0:T(8,128)(2,1)S(1)}, u32[]{:S(2)}, u32[]{:S(2)}) collective-permute-start(bf16[512,512]{1,0:T(8,128)(2,1)S(1)} %get-tuple-element.20), channel_id=1, source_target_pairs={{0,1},{1,0},{2,3},{3,2},{4,5},{5,4},{6,7},{7,6},{8,9},{9,8},{10,11... | collective-permute-start | bytes 1572872 | tf_op jit(solution)/shard_map/ppermute | solution.py:256
  1.8 0.7 %collective-permute-start.1 = (bf16[512,512]{1,0:T(8,128)(2,1)S(1)}, bf16[512,512]{1,0:T(8,128)(2,1)S(1)}, u32[]{:S(2)}, u32[]{:S(2)}) collective-permute-start(bf16[512,512]{1,0:T(8,128)(2,1)S(1)} %get-tuple-element.19), channel_id=1, source_target_pairs={{1,2},{3,4},{5,6},{7,8},{9,10},{11,12},{13,14},{2,1},{4,3},{6,5},{... | collective-permute-start | bytes 1572872 | tf_op jit(solution)/shard_map/ppermute | solution.py:254
  2.5 0.8 %collective-permute-done.near = bf16[512,512]{1,0:T(8,128)(2,1)S(1)} collective-permute-done((bf16[512,512]{1,0:T(8,128)(2,1)S(1)}, bf16[512,512]{1,0:T(8,128)(2,1)S(1)}, u32[]{:S(2)}, u32[]{:S(2)}) %collective-permute-start) | collective-permute-done | bytes 524320 | tf_op jit(solution)/shard_map/ppermute | solution.py:256
  3.3 0.7 %copy-done = s32[6,9]{1,0:T(8,128)S(1)} copy-done((s32[6,9]{1,0:T(8,128)S(1)}, s32[6,9]{1,0:T(8,128)}, u32[]{:S(2)}) %copy-start) | copy-done | bytes 240
  4.0 6.8 %tiles.1 = (f32[6,256,512]{2,1,0:T(8,128)S(1)}, bf16[6,9,256,128]{3,2,1,0:T(8,128)(2,1)S(1)}, bf16[512,768]{1,0:T(8,128)(2,1)S(1)}) custom-call(s32[6,9]{1,0:T(8,128)S(1)} %copy-done, bf16[6,9,4,128,128]{4,3,2,1,0:T(8,128)(2,1)} %green.1, bf16[6,9,128,128]{3,2,1,0:T(8,128)(2,1)} %integrals.1, bf16[768,512]{1,0:T(8,128)(2,1)} %coefficients.1, ...), custom_call_target="tpu_custom_call" | custom-call | flops 2000000000 | bytes 12000000 | tf_op jit(solution)/shard_map/tiles/pallas_call | solution.py:100
  10.8 0.0 collective-permute-done.1.halo
  10.8 0.0 copy-start.1
  10.8 1.6 %project.1 = (f32[4,64,1024]{2,1,0:T(8,128)S(1)}, bf16[4,64,1024]{2,1,0:T(8,128)(2,1)S(1)}) custom-call(f32[6,256,512]{2,1,0:T(8,128)S(1)} %get-tuple-element.10.part, bf16[6,9,256,128]{3,2,1,0:T(8,128)(2,1)S(1)} %get-tuple-element.11.sigma, bf16[512,512]{1,0:T(8,128)(2,1)S(1)} %collective-permute-done.1.halo, bf16[512,768]{1,0:T(8,128)(2,1)S(1)} %get-tuple-element.12.transposed), custom_call_target="tpu_custom_call" | custom-call | flops 1600000000 | bytes 6000000 | tf_op jit(solution)/shard_map/project/pallas_call | solution.py:178
  12.4 7.3 %collective-permute-start.2 = (bf16[4,64,1024]{2,1,0:T(8,128)(2,1)S(1)}, bf16[4,64,1024]{2,1,0:T(8,128)(2,1)S(1)}, u32[]{:S(2)}, u32[]{:S(2)}) collective-permute-start(bf16[4,64,1024]{2,1,0:T(8,128)(2,1)S(1)} %get-tuple-element.14), channel_id=1, source_target_pairs={{0,1},{1,0},{2,3},{3,2},{4,5},{5,4},{6,7},{7,6},{8,9},{9,8},{10,11... | collective-permute-start | bytes 1572872 | tf_op jit(solution)/shard_map/ppermute | solution.py:263
  19.7 1.5 %collective-permute-done.2 = bf16[4,64,1024]{2,1,0:T(8,128)(2,1)S(1)} collective-permute-done((bf16[4,64,1024]{2,1,0:T(8,128)(2,1)S(1)}, bf16[4,64,1024]{2,1,0:T(8,128)(2,1)S(1)}, u32[]{:S(2)}, u32[]{:S(2)}) %collective-permute-start.2) | collective-permute-done | bytes 524320 | tf_op jit(solution)/shard_map/ppermute | solution.py:263
  21.3 0.1 fusion
  21.4 0.7 %collective-permute-start.3 = (bf16[64,1024]{1,0:T(8,128)(2,1)S(1)}, bf16[64,1024]{1,0:T(8,128)(2,1)S(1)}, u32[]{:S(2)}, u32[]{:S(2)}) collective-permute-start(bf16[64,1024]{1,0:T(8,128)(2,1)S(1)} %get-tuple-element.15), channel_id=1, source_target_pairs={{0,0},{1,2},{2,1},{3,3},{4,4},{5,6},{6,5},{7,7},{8,8},{9,10},{10,9... | collective-permute-start | bytes 393224 | tf_op jit(solution)/shard_map/ppermute | solution.py:271
  22.1 5.0 %collective-permute-start.6 = (bf16[64,1024]{1,0:T(8,128)(2,1)S(1)}, bf16[64,1024]{1,0:T(8,128)(2,1)S(1)}, u32[]{:S(2)}, u32[]{:S(2)}) collective-permute-start(bf16[64,1024]{1,0:T(8,128)(2,1)S(1)} %get-tuple-element.16), channel_id=1, source_target_pairs={{0,12},{1,14},{2,13},{3,15},{4,8},{5,10},{6,9},{7,11},{8,4},{9,6},... | collective-permute-start | bytes 393224 | tf_op jit(solution)/shard_map/ppermute | solution.py:271
  27.1 0.0 collective-permute-start.5
  27.1 0.6 %collective-permute-start.4 = (bf16[64,1024]{1,0:T(8,128)(2,1)S(1)}, bf16[64,1024]{1,0:T(8,128)(2,1)S(1)}, u32[]{:S(2)}, u32[]{:S(2)}) collective-permute-start(bf16[64,1024]{1,0:T(8,128)(2,1)S(1)} %get-tuple-element.18), channel_id=1, source_target_pairs={{0,4},{1,6},{2,5},{3,7},{4,0},{5,2},{6,1},{7,3},{8,12},{9,14},{10,... | collective-permute-start | bytes 393224 | tf_op jit(solution)/shard_map/ppermute | solution.py:271
  27.8 0.0 collective-permute-done.3
  27.8 2.4 %collective-permute-done.6 = bf16[64,1024]{1,0:T(8,128)(2,1)S(1)} collective-permute-done((bf16[64,1024]{1,0:T(8,128)(2,1)S(1)}, bf16[64,1024]{1,0:T(8,128)(2,1)S(1)}, u32[]{:S(2)}, u32[]{:S(2)}) %collective-permute-start.6) | collective-permute-done | bytes 131104 | tf_op jit(solution)/shard_map/ppermute | solution.py:271
  30.2 8.4 %collective-permute-done.5 = bf16[64,1024]{1,0:T(8,128)(2,1)S(1)} collective-permute-done((bf16[64,1024]{1,0:T(8,128)(2,1)S(1)}, bf16[64,1024]{1,0:T(8,128)(2,1)S(1)}, u32[]{:S(2)}, u32[]{:S(2)}) %collective-permute-start.5) | collective-permute-done | bytes 131104 | tf_op jit(solution)/shard_map/ppermute | solution.py:271
  38.6 0.0 collective-permute-done.4
  38.6 0.1 convert_add_fusion
  38.7 0.6 %collective-permute-start.7 = (f32[32,1024]{1,0:T(8,128)S(1)}, f32[32,1024]{1,0:T(8,128)S(1)}, u32[]{:S(2)}, u32[]{:S(2)}) collective-permute-start(f32[32,1024]{1,0:T(8,128)S(1)} %get-tuple-element.21), channel_id=1, source_target_pairs={{0,1},{1,0},{2,3},{3,2},{4,5},{5,4},{6,7},{7,6},{8,9},{9,8},{10,11... | collective-permute-start | bytes 393224 | tf_op jit(solution)/shard_map/ppermute | solution.py:278
  39.3 1.0 %collective-permute-done.7.other = f32[32,1024]{1,0:T(8,128)S(1)} collective-permute-done((f32[32,1024]{1,0:T(8,128)S(1)}, f32[32,1024]{1,0:T(8,128)S(1)}, u32[]{:S(2)}, u32[]{:S(2)}) %collective-permute-start.7) | collective-permute-done | bytes 131104 | tf_op jit(solution)/shard_map/ppermute | solution.py:278
  40.3 6.7 %frequency.1 = f32[256,32,512]{2,1,0:T(8,128)} custom-call(f32[512]{0:T(512)S(1)} %copy-done.1, f32[32,1024]{1,0:T(8,128)S(1)} %get-tuple-element.22.mine, f32[32,1024]{1,0:T(8,128)S(1)} %collective-permute-done.7.other), custom_call_target="tpu_custom_call" | custom-call | flops 50000000 | bytes 17000000 | tf_op jit(solution)/shard_map/frequency/pallas_call | solution.py:232
  (3 shorter events, 0.0 us)
Async XLA Ops:
  1.3 2.1 %collective-permute-start = (bf16[512,512]{1,0:T(8,128)(2,1)S(1)}, bf16[512,512]{1,0:T(8,128)(2,1)S(1)}, u32[]{:S(2)}, u32[]{:S(2)}) collective-permute-start(bf16[512,512]{1,0:T(8,128)(2,1)S(1)} %get-tuple-element.20), channel_id=1, source_target_pairs={{0,1},{1,0},{2,3},{3,2},{4,5},{5,4},{6,7},{7,6},{8,9},{9,8},{10,11... | collective-permute-start | bytes 1572872 | tf_op jit(solution)/shard_map/ppermute | solution.py:256
  1.8 9.0 %collective-permute-start.1 = (bf16[512,512]{1,0:T(8,128)(2,1)S(1)}, bf16[512,512]{1,0:T(8,128)(2,1)S(1)}, u32[]{:S(2)}, u32[]{:S(2)}) collective-permute-start(bf16[512,512]{1,0:T(8,128)(2,1)S(1)} %get-tuple-element.19), channel_id=1, source_target_pairs={{1,2},{3,4},{5,6},{7,8},{9,10},{11,12},{13,14},{2,1},{4,3},{6,5},{... | collective-permute-start | bytes 1572872 | tf_op jit(solution)/shard_map/ppermute | solution.py:254
  3.3 0.7 %copy-start = (s32[6,9]{1,0:T(8,128)S(1)}, s32[6,9]{1,0:T(8,128)}, u32[]{:S(2)}) copy-start(s32[6,9]{1,0:T(8,128)} %pattern.1) | copy-start | bytes 652
  10.8 29.4 %copy-start.1 = (f32[512]{0:T(512)S(1)}, f32[512]{0:T(512)}, u32[]{:S(2)}) copy-start(f32[512]{0:T(512)} %constant.21.clone.table) | copy-start | bytes 6148
  12.4 8.8 %collective-permute-start.2 = (bf16[4,64,1024]{2,1,0:T(8,128)(2,1)S(1)}, bf16[4,64,1024]{2,1,0:T(8,128)(2,1)S(1)}, u32[]{:S(2)}, u32[]{:S(2)}) collective-permute-start(bf16[4,64,1024]{2,1,0:T(8,128)(2,1)S(1)} %get-tuple-element.14), channel_id=1, source_target_pairs={{0,1},{1,0},{2,3},{3,2},{4,5},{5,4},{6,7},{7,6},{8,9},{9,8},{10,11... | collective-permute-start | bytes 1572872 | tf_op jit(solution)/shard_map/ppermute | solution.py:263
  21.4 6.3 %collective-permute-start.3 = (bf16[64,1024]{1,0:T(8,128)(2,1)S(1)}, bf16[64,1024]{1,0:T(8,128)(2,1)S(1)}, u32[]{:S(2)}, u32[]{:S(2)}) collective-permute-start(bf16[64,1024]{1,0:T(8,128)(2,1)S(1)} %get-tuple-element.15), channel_id=1, source_target_pairs={{0,0},{1,2},{2,1},{3,3},{4,4},{5,6},{6,5},{7,7},{8,8},{9,10},{10,9... | collective-permute-start | bytes 393224 | tf_op jit(solution)/shard_map/ppermute | solution.py:271
  22.1 8.1 %collective-permute-start.6 = (bf16[64,1024]{1,0:T(8,128)(2,1)S(1)}, bf16[64,1024]{1,0:T(8,128)(2,1)S(1)}, u32[]{:S(2)}, u32[]{:S(2)}) collective-permute-start(bf16[64,1024]{1,0:T(8,128)(2,1)S(1)} %get-tuple-element.16), channel_id=1, source_target_pairs={{0,12},{1,14},{2,13},{3,15},{4,8},{5,10},{6,9},{7,11},{8,4},{9,6},... | collective-permute-start | bytes 393224 | tf_op jit(solution)/shard_map/ppermute | solution.py:271
  27.1 11.4 %collective-permute-start.5 = (bf16[64,1024]{1,0:T(8,128)(2,1)S(1)}, bf16[64,1024]{1,0:T(8,128)(2,1)S(1)}, u32[]{:S(2)}, u32[]{:S(2)}) collective-permute-start(bf16[64,1024]{1,0:T(8,128)(2,1)S(1)} %get-tuple-element.17), channel_id=1, source_target_pairs={{0,8},{1,10},{2,9},{3,11},{4,12},{5,14},{6,13},{7,15},{8,0},{9,2},... | collective-permute-start | bytes 393224 | tf_op jit(solution)/shard_map/ppermute | solution.py:271
  27.1 11.4 %collective-permute-start.4 = (bf16[64,1024]{1,0:T(8,128)(2,1)S(1)}, bf16[64,1024]{1,0:T(8,128)(2,1)S(1)}, u32[]{:S(2)}, u32[]{:S(2)}) collective-permute-start(bf16[64,1024]{1,0:T(8,128)(2,1)S(1)} %get-tuple-element.18), channel_id=1, source_target_pairs={{0,4},{1,6},{2,5},{3,7},{4,0},{5,2},{6,1},{7,3},{8,12},{9,14},{10,... | collective-permute-start | bytes 393224 | tf_op jit(solution)/shard_map/ppermute | solution.py:271
  38.7 1.6 %collective-permute-start.7 = (f32[32,1024]{1,0:T(8,128)S(1)}, f32[32,1024]{1,0:T(8,128)S(1)}, u32[]{:S(2)}, u32[]{:S(2)}) collective-permute-start(f32[32,1024]{1,0:T(8,128)S(1)} %get-tuple-element.21), channel_id=1, source_target_pairs={{0,1},{1,0},{2,3},{3,2},{4,5},{5,4},{6,7},{7,6},{8,9},{9,8},{10,11... | collective-permute-start | bytes 393224 | tf_op jit(solution)/shard_map/ppermute | solution.py:278
where the time goes:
time: 47.1 us; the launch traced here: 46.9 us
  starting transfers between devices  15.4 us (33%)
  Pallas kernels  15.1 us (32%)
  waiting for transfers between devices  14.2 us (30%)
  local copies, waits for them, and re-layouts  1.99 us (4%)
    ppermute x4, waiting for transfers between devices, local(): got.append(lax.ppermute(pieces[k], 'trow', moves))  10.8 us
    ppermute x1, starting transfers between devices, local(): arrived = lax.ppermute(send, 'trow', [(i, i ^ 1) for i in range(devices)])  7.3 us
    pallas_call x1, Pallas kernels, tiles(): pl.pallas_call(functools.partial(tiles_kernel, count), out_shape=(pltpu.V...  6.8 us
    pallas_call x1, Pallas kernels, frequency(): pl.pallas_call(frequency_kernel, out_shape=jax.ShapeDtypeStruct((2 * NW,...  6.67 us
    ppermute x4, starting transfers between devices, local(): got.append(lax.ppermute(pieces[k], 'trow', moves))  6.34 us
    pallas_call x1, Pallas kernels, project(): pl.pallas_call(functools.partial(project_kernel, count, split), out_shape...  1.59 us
    ppermute x1, waiting for transfers between devices, local(): arrived = lax.ppermute(send, 'trow', [(i, i ^ 1) for i in range(devices)])  1.54 us
    dynamic_slice x1, local copies, waits for them, and re-layouts, local(): lax.dynamic_slice_in_dim(coefficients, core * (rows - width), width, axis=0)  1.27 us
  transfers between devices with their start and end apart: 8, of which 5 were waited for; matrix products, arithmetic and copies ran while one was open for 0% of the time, Pallas kernels for 14%

commit v1 on v0

v1 whole, which is shorter than its diff:
```python
import functools

import jax
import jax.numpy as jnp
import numpy as np
from jax import lax
from jax.experimental import pallas as pl
from jax.experimental.pallas import tpu as pltpu
from jax.sharding import PartitionSpec as P

TILE = 128
BAND = 4
TAU = 4
PAIRS = TAU // 2
NMO = 512
NW = 128
SLOTS = 9
FREQ_BLOCK = 16
GROUP = 4
CHUNKS = 2
COLUMNS = NMO // CHUNKS
MIB = 1 << 20


def sides(count, row):
    return range(0, max(0, BAND - row)), range(max(0, BAND - row), min(SLOTS, count + BAND - row)), range(
        min(SLOTS, count + BAND - row), SLOTS
    )


def contract(sigma, row, slots, block, begin):
    lhs = jnp.concatenate([sigma[row, slot] for slot in slots], axis=1)
    rhs = block[begin * TILE : (begin + len(slots)) * TILE, :]
    return jnp.dot(lhs, rhs, preferred_element_type=jnp.float32)


def tiles_kernel(
    count,
    mask,
    green,
    integrals,
    coefficients,
    part,
    sigma,
    transposed,
    gbuf,
    ibuf,
    own,
    pattern,
    order,
    sems,
    csem,
):
    def fetch(index):
        row, slot = index // SLOTS, index % SLOTS
        return (
            pltpu.make_async_copy(green.at[row, slot], gbuf.at[index], sems.at[index, 0]),
            pltpu.make_async_copy(integrals.at[row, slot], ibuf.at[index], sems.at[index, 1]),
        )

    def enlist(index, found):
        present = pattern[index // SLOTS, index % SLOTS] != 0

        @pl.when(present)
        def _():
            order[found] = index
            for copy in fetch(index):
                copy.start()

        return found + present.astype(jnp.int32)

    mask_copy = pltpu.make_async_copy(mask, pattern, csem.at[0])
    own_copy = pltpu.make_async_copy(coefficients, own, csem.at[1])
    mask_copy.start()
    own_copy.start()
    sigma[...] = jnp.zeros_like(sigma)
    mask_copy.wait()
    found = lax.fori_loop(0, count * SLOTS, enlist, jnp.int32(0))
    for extra in range(GROUP - 1):
        order[found + extra] = order[found - 1]
    own_copy.wait()
    for row in range(count):
        rows = slice(row * TILE, (row + 1) * TILE)
        transposed[:, rows] = own[rows, :].T

    @pl.loop(0, pl.cdiv(found, GROUP))
    def _(group):
        indices = [order[group * GROUP + member] for member in range(GROUP)]
        for member, index in enumerate(indices):

            @pl.when(group * GROUP + member < found)
            def _():
                for copy in fetch(index):
                    copy.wait()

        for index in indices:
            paired = jnp.concatenate([gbuf[index, t] * gbuf[index, TAU - 1 - t] for t in range(PAIRS)], axis=0)
            product = jnp.dot(paired, ibuf[index], preferred_element_type=jnp.float32)
            sigma[index // SLOTS, index % SLOTS] = product.astype(jnp.bfloat16)

    for row in range(count):
        _, slots, _ = sides(count, row)
        part[row] = contract(sigma, row, slots, own, row + slots[0] - BAND)


def tiles(green, integrals, pattern, coefficients):
    count = green.shape[0]
    hbm = pl.BlockSpec(memory_space=pltpu.HBM)
    vmem = pl.BlockSpec(memory_space=pltpu.VMEM)
    placed = [pltpu.with_memory_space_constraint(x, pltpu.HBM) for x in (pattern, green, integrals, coefficients)]
    return pl.pallas_call(
        functools.partial(tiles_kernel, count),
        out_shape=(
            pltpu.VMEM((count, PAIRS * TILE, NMO), jnp.float32),
            pltpu.VMEM((count, SLOTS, PAIRS * TILE, TILE), jnp.bfloat16),
            pltpu.VMEM((NMO, count * TILE), jnp.bfloat16),
        ),
        in_specs=[hbm] * 4,
        out_specs=(vmem,) * 3,
        scratch_shapes=[
            pltpu.VMEM((count * SLOTS, TAU, TILE, TILE), jnp.bfloat16),
            pltpu.VMEM((count * SLOTS, TILE, TILE), jnp.bfloat16),
            pltpu.VMEM((count * TILE, NMO), jnp.bfloat16),
            pltpu.SMEM((count, SLOTS), jnp.int32),
            pltpu.SMEM((count * SLOTS + GROUP,), jnp.int32),
            pltpu.SemaphoreType.DMA((count * SLOTS, 2)),
            pltpu.SemaphoreType.DMA((2,)),
        ],
        compiler_params=pltpu.CompilerParams(vmem_limit_bytes=24 * MIB),
        cost_estimate=pl.CostEstimate(flops=2_000_000_000, bytes_accessed=12_000_000, transcendentals=0),
        name="tiles",
    )(*placed)


def beside(count, row, left, sigma, block):
    before, _, after = sides(count, row)
    slots = before if left else after
    if not slots:
        return None
    return contract(sigma, row, slots, block, row if left else row + slots[0] - BAND - count)


def project_kernel(count, split, piece, *refs):
    part, sigma, near, halo, transposed = refs[:5]
    outs, half = refs[5:-1], refs[-1]
    me = lax.axis_index("trow")
    first = lax.rem(me, 2) == 0
    columns = slice(piece * COLUMNS, (piece + 1) * COLUMNS)

    def finish(far_left):
        for row in range(count):
            value = part[row, :, columns]
            for left, block in ((not far_left, near), (far_left, halo)):
                term = beside(count, row, left, sigma, block)
                value = value if term is None else value + term
            for t in range(PAIRS):
                half[row * TILE : (row + 1) * TILE, t * COLUMNS : (t + 1) * COLUMNS] = value[
                    t * TILE : (t + 1) * TILE
                ].astype(jnp.bfloat16)

    @pl.when(first)
    def _():
        finish(True)

    @pl.when(jnp.logical_not(first))
    def _():
        finish(False)

    for k in range(NMO // TILE):
        block = lax.bitwise_xor(lax.div(me, 4), k) if split else k
        lhs = transposed[pl.ds(pl.multiple_of(block * TILE, TILE), TILE), :]
        total = jnp.dot(lhs, half[...], preferred_element_type=jnp.float32)
        if not split:
            outs[0][k * TILE : (k + 1) * TILE] = total
            continue
        keep, send = outs
        quarter = TILE // 4
        quarters = [total[q * quarter : (q + 1) * quarter] for q in range(4)]
        low_x = lax.rem(lax.div(me, 2), 2) == 0
        mine = [jnp.where(first, quarters[2 * x], quarters[2 * x + 1]) for x in range(2)]
        other = [jnp.where(first, quarters[2 * x + 1], quarters[2 * x]) for x in range(2)]
        for ref, pair in ((keep, mine), (send, other)):
            ref[2 * k] = jnp.where(low_x, pair[0], pair[1]).astype(ref.dtype)
            ref[2 * k + 1] = jnp.where(low_x, pair[1], pair[0]).astype(ref.dtype)


def project(part, sigma, near, halo, transposed, split, piece):
    count = part.shape[0]
    operands = (part, sigma, near, halo, transposed)
    vmem = pl.BlockSpec(memory_space=pltpu.VMEM)
    if split:
        shape = (8, NMO // 16, PAIRS * COLUMNS)
        out_shape = (pltpu.VMEM(shape, jnp.float32), pltpu.VMEM(shape, jnp.bfloat16))
    else:
        out_shape = (jax.ShapeDtypeStruct((NMO, PAIRS * COLUMNS), jnp.float32),)
    return pl.pallas_call(
        functools.partial(project_kernel, count, split, piece),
        out_shape=out_shape,
        in_specs=[vmem] * len(operands),
        out_specs=tuple(vmem for _ in out_shape),
        scratch_shapes=[pltpu.VMEM((count * TILE, PAIRS * COLUMNS), jnp.bfloat16)],
        compiler_params=pltpu.CompilerParams(vmem_limit_bytes=16 * MIB),
        cost_estimate=pl.CostEstimate(flops=800_000_000, bytes_accessed=3_000_000, transcendentals=0),
        name="project",
    )(*[pltpu.with_memory_space_constraint(x, pltpu.VMEM) for x in operands])


def freq_tables():
    point = np.arange(TAU, dtype=np.float32)
    freq = np.arange(NW, dtype=np.float32)
    pi = np.float32(np.pi)
    theta = pi * (np.float32(2.0) * point + np.float32(1.0)) / np.float32(2.0 * TAU)
    nodes = np.float32(0.5) * (np.float32(1.0) - np.cos(theta))
    weights = np.float32(np.pi / (2.0 * TAU)) * np.sin(theta)
    angle = pi * (np.float32(2.0) * freq[:, None] + np.float32(1.0)) * nodes[None, :]
    both = np.concatenate([weights[None, :] * np.cos(angle), weights[None, :] * np.sin(angle)], axis=0)
    folded = both[:, :PAIRS] + both[:, : PAIRS - 1 : -1]
    return folded.astype(np.float32).reshape(-1)


def frequency_kernel(terms, table, *refs):
    out, buffer, sems = refs[terms:]
    summed = refs[0][...]
    for ref in refs[1:terms]:
        summed = summed + ref[...].astype(jnp.float32)
    points = [
        jnp.concatenate(
            [summed[:, (piece * PAIRS + t) * COLUMNS : (piece * PAIRS + t + 1) * COLUMNS] for piece in range(CHUNKS)],
            axis=1,
        )
        for t in range(PAIRS)
    ]

    def copy(step):
        rows = pl.ds(step * FREQ_BLOCK, FREQ_BLOCK)
        return pltpu.make_async_copy(buffer.at[rows], out.at[rows], sems.at[step])

    @pl.loop(0, 2 * NW // FREQ_BLOCK)
    def _(step):
        @pl.loop(0, FREQ_BLOCK, unroll=4)
        def _(n):
            at = (step * FREQ_BLOCK + n) * PAIRS
            value = table[at] * points[0]
            for t in range(1, PAIRS):
                value = value + table[at + t] * points[t]
            buffer[step * FREQ_BLOCK + n] = value

        copy(step).start()

    @pl.loop(0, 2 * NW // FREQ_BLOCK)
    def _(step):
        copy(step).wait()


def frequency(*terms):
    rows = terms[0].shape[0]
    vmem = pl.BlockSpec(memory_space=pltpu.VMEM)
    out = pl.pallas_call(
        functools.partial(frequency_kernel, len(terms)),
        out_shape=jax.ShapeDtypeStruct((2 * NW, rows, NMO), jnp.float32),
        in_specs=[pl.BlockSpec(memory_space=pltpu.SMEM)] + [vmem] * len(terms),
        out_specs=pl.BlockSpec(memory_space=pl.ANY),
        scratch_shapes=[
            pltpu.VMEM((2 * NW, rows, NMO), jnp.float32),
            pltpu.SemaphoreType.DMA((2 * NW // FREQ_BLOCK,)),
        ],
        compiler_params=pltpu.CompilerParams(vmem_limit_bytes=24 * MIB),
        cost_estimate=pl.CostEstimate(flops=50_000_000, bytes_accessed=17_000_000, transcendentals=0),
        name="frequency",
    )(jnp.asarray(freq_tables()), *terms)
    return out.reshape(2, NW, rows, NMO)


def local(devices, green, integrals, pattern, coefficients):
    rows = coefficients.shape[0]
    width = BAND * TILE
    core = lax.rem(lax.axis_index("trow"), 2)
    partner = [(i, i ^ 1) for i in range(devices)]
    pairs = [(i, i + 1) for i in range(1, devices - 1, 2)]
    pairs += [(b, a) for a, b in pairs]
    halos, nears = [], []
    for piece in range(CHUNKS):
        away = lax.dynamic_slice(coefficients, (core * (rows - width), piece * COLUMNS), (width, COLUMNS))
        halos.append(lax.ppermute(away, "trow", pairs))
        inner = lax.dynamic_slice(coefficients, ((1 - core) * (rows - width), piece * COLUMNS), (width, COLUMNS))
        nears.append(lax.ppermute(inner, "trow", partner))
    part, sigma, transposed = tiles(green, integrals, pattern, coefficients)
    if devices != 16:
        summed = jnp.concatenate(
            [project(part, sigma, nears[piece], halos[piece], transposed, False, piece)[0] for piece in range(CHUNKS)], axis=1
        )
        return frequency(lax.psum_scatter(summed, "trow", scatter_dimension=0, tiled=True))
    keeps, arrived = [], []
    for piece in range(CHUNKS):
        keep, send = project(part, sigma, nears[piece], halos[piece], transposed, True, piece)
        keeps.append(keep)
        arrived.append(lax.ppermute(send, "trow", partner))
    sums = [
        jnp.concatenate([keep[k] + other[k].astype(jnp.float32) for keep, other in zip(keeps, arrived)], axis=1)
        for k in range(8)
    ]
    terms = [sums[0]]
    for k in (6, 7, 4, 5, 2, 3, 1):
        moves = [(i, i ^ (2 * k)) for i in range(devices)]
        terms.append(lax.ppermute(sums[k].astype(jnp.bfloat16), "trow", moves))
    return frequency(*terms)


def solution(mesh):
    in_specs = (
        P(("flake", "trow"), None, None, None, None),
        P(("flake", "trow"), None, None, None),
        P(("flake", "trow"), None),
        P(("flake", "trow"), None),
    )
    out_specs = P(None, None, ("flake", "trow"), None)
    return jax.shard_map(
        functools.partial(local, mesh.shape["trow"]),
        mesh=mesh,
        in_specs=in_specs,
        out_specs=out_specs,
        check_vma=False,
    )
```

time: 47.1 us -> 45.1 us (0.958)
  waiting for transfers between devices: 14.2 us -> 6.76 us
  starting transfers between devices: 15.4 us -> 21.2 us
  local copies, waits for them, and re-layouts: 1.99 us -> 1.26 us
    ppermute x8 -> x13, waiting for transfers between devices: 14.2 us -> 6.76 us  [the longest x7 5.67 us: local(): terms.append(lax.ppermute(sums[k].astype(jnp.bfloat16), 'trow', moves))]
    ppermute x8 -> x13, starting transfers between devices: 15.4 us -> 21.2 us  [the longest x7 11.9 us: local(): terms.append(lax.ppermute(sums[k].astype(jnp.bfloat16), 'trow', moves))]
    pallas_call x2 -> x3, Pallas kernels: 8.27 us -> 9.11 us  [the longest x1 6.73 us: frequency(): pl.pallas_call(functools.partial(frequency_kernel, len(terms)), out_shape...]
    unnamed x4 -> x2, local copies, waits for them, and re-layouts: 0.69 us -> 0.01 us
    pallas_call x1, Pallas kernels: 6.8 us -> 6.24 us  [tiles(): pl.pallas_call(functools.partial(tiles_kernel, count), out_shape=(pltpu.V...]
    dynamic_slice x2 -> x1, local copies, waits for them, and re-layouts: 1.29 us -> 1.25 us  [local(): lax.dynamic_slice(coefficients, (core * (rows - width), piece * COLUMNS),...]
  transfers between devices with their start and end apart: 8 -> 13, of which waited for: 5 -> 6; matrix products, arithmetic and copies ran while one was open for 0% -> 0% of each run, Pallas kernels for 14% -> 19%
where the time goes in v1:
time: 45.1 us; the launch traced here: 44.9 us
  starting transfers between devices  21.2 us (47%)
  Pallas kernels  15.4 us (34%)
  waiting for transfers between devices  6.76 us (15%)
  local copies, waits for them, and re-layouts  1.26 us (3%)
    ppermute x7, starting transfers between devices, local(): terms.append(lax.ppermute(sums[k].astype(jnp.bfloat16), 'trow', moves))  11.9 us
    ppermute x2, starting transfers between devices, local(): nears.append(lax.ppermute(inner, 'trow', partner))  7.31 us
    pallas_call x1, Pallas kernels, frequency(): pl.pallas_call(functools.partial(frequency_kernel, len(terms)), out_shape...  6.73 us
    pallas_call x1, Pallas kernels, tiles(): pl.pallas_call(functools.partial(tiles_kernel, count), out_shape=(pltpu.V...  6.24 us
    ppermute x7, waiting for transfers between devices, local(): terms.append(lax.ppermute(sums[k].astype(jnp.bfloat16), 'trow', moves))  5.67 us
    pallas_call x2, Pallas kernels, project(): pl.pallas_call(functools.partial(project_kernel, count, split, piece), ou...  2.39 us
    ppermute x2, starting transfers between devices, local(): halos.append(lax.ppermute(away, 'trow', pairs))  1.34 us
    dynamic_slice x1, local copies, waits for them, and re-layouts, local(): lax.dynamic_slice(coefficients, (core * (rows - width), piece * COLUMNS),...  1.25 us
  transfers between devices with their start and end apart: 13, of which 6 were waited for; matrix products, arithmetic and copies ran while one was open for 0% of the time, Pallas kernels for 19%

profile of v1, /device:TPU:0, one launch (start us, length us, event | category | flops | bytes accessed | tf_op | source)
XLA Modules:
  0.0 44.9 jit_solution(4368659120170140453)
XLA Ops:
  0.0 1.3 %constant_dynamic-slice_fusion.2 = (bf16[512,256]{1,0:T(8,128)(2,1)S(1)}, bf16[512,256]{1,0:T(8,128)(2,1)S(1)}, bf16[512,256]{1,0:T(8,128)(2,1)S(1)}, bf16[512,256]{1,0:T(8,128)(2,1)S(1)}) fusion(bf16[768,512]{1,0:T(8,128)(2,1)} %coefficients.1, s32[]{:T(128)S(6)} %select_n.9, s32[]{:T(128)S(6)} %select_n.8), kind=kLoop, calls=%fused_computation.40 | loop fusion | bytes 2097160 | tf_op jit(solution)/shard_map/dynamic_slice | solution.py:283
  1.3 0.7 %collective-permute-start.4 = (bf16[512,256]{1,0:T(8,128)(2,1)S(1)}, bf16[512,256]{1,0:T(8,128)(2,1)S(1)}, u32[]{:S(2)}, u32[]{:S(2)}) collective-permute-start(bf16[512,256]{1,0:T(8,128)(2,1)S(1)} %get-tuple-element.37), channel_id=1, source_target_pairs={{1,2},{3,4},{5,6},{7,8},{9,10},{11,12},{13,14},{2,1},{4,3},{6,5},{... | collective-permute-start | bytes 786440 | tf_op jit(solution)/shard_map/ppermute | solution.py:284
  1.9 4.3 %collective-permute-start.3 = (bf16[512,256]{1,0:T(8,128)(2,1)S(1)}, bf16[512,256]{1,0:T(8,128)(2,1)S(1)}, u32[]{:S(2)}, u32[]{:S(2)}) collective-permute-start(bf16[512,256]{1,0:T(8,128)(2,1)S(1)} %get-tuple-element.38), channel_id=1, source_target_pairs={{0,1},{1,0},{2,3},{3,2},{4,5},{5,4},{6,7},{7,6},{8,9},{9,8},{10,11... | collective-permute-start | bytes 786440 | tf_op jit(solution)/shard_map/ppermute | solution.py:286
  6.3 0.7 %collective-permute-start.1 = (bf16[512,256]{1,0:T(8,128)(2,1)S(1)}, bf16[512,256]{1,0:T(8,128)(2,1)S(1)}, u32[]{:S(2)}, u32[]{:S(2)}) collective-permute-start(bf16[512,256]{1,0:T(8,128)(2,1)S(1)} %get-tuple-element.35), channel_id=1, source_target_pairs={{1,2},{3,4},{5,6},{7,8},{9,10},{11,12},{13,14},{2,1},{4,3},{6,5},{... | collective-permute-start | bytes 786440 | tf_op jit(solution)/shard_map/ppermute | solution.py:284
  7.0 3.0 %collective-permute-start = (bf16[512,256]{1,0:T(8,128)(2,1)S(1)}, bf16[512,256]{1,0:T(8,128)(2,1)S(1)}, u32[]{:S(2)}, u32[]{:S(2)}) collective-permute-start(bf16[512,256]{1,0:T(8,128)(2,1)S(1)} %get-tuple-element.36), channel_id=1, source_target_pairs={{0,1},{1,0},{2,3},{3,2},{4,5},{5,4},{6,7},{7,6},{8,9},{9,8},{10,11... | collective-permute-start | bytes 786440 | tf_op jit(solution)/shard_map/ppermute | solution.py:286
  9.9 6.2 %tiles.1 = (f32[6,256,512]{2,1,0:T(8,128)S(1)}, bf16[6,9,256,128]{3,2,1,0:T(8,128)(2,1)S(1)}, bf16[512,768]{1,0:T(8,128)(2,1)S(1)}) custom-call(s32[6,9]{1,0:T(8,128)} %mask.1, bf16[6,9,4,128,128]{4,3,2,1,0:T(8,128)(2,1)} %green.1, bf16[6,9,128,128]{3,2,1,0:T(8,128)(2,1)} %integrals.1, bf16[768,512]{1,0:T(8,128)(2,1)} %coefficients.1), custom_call_target="tpu_custom_call" | custom-call | flops 2000000000 | bytes 12000000 | tf_op jit(solution)/shard_map/tiles/pallas_call | solution.py:111
  16.2 1.2 %project.3 = (f32[8,32,512]{2,1,0:T(8,128)S(1)}, bf16[8,32,512]{2,1,0:T(8,128)(2,1)S(1)}) custom-call(f32[6,256,512]{2,1,0:T(8,128)S(1)} %get-tuple-element.12.refs_0_, bf16[6,9,256,128]{3,2,1,0:T(8,128)(2,1)S(1)} %get-tuple-element.13.refs_1_, bf16[512,256]{1,0:T(8,128)(2,1)S(1)} %collective-permute-done.3.refs_2_, ...), custom_call_target="tpu_custom_call" | custom-call | flops 800000000 | bytes 3000000 | tf_op jit(solution)/shard_map/project/pallas_call | solution.py:196
  17.4 0.1 collective-permute-start.5
  17.5 1.2 %project.2 = (f32[8,32,512]{2,1,0:T(8,128)S(1)}, bf16[8,32,512]{2,1,0:T(8,128)(2,1)S(1)}) custom-call(f32[6,256,512]{2,1,0:T(8,128)S(1)} %get-tuple-element.12.refs_0_, bf16[6,9,256,128]{3,2,1,0:T(8,128)(2,1)S(1)} %get-tuple-element.13.refs_1_, bf16[512,256]{1,0:T(8,128)(2,1)S(1)} %collective-permute-done.refs_2_, ...), custom_call_target="tpu_custom_call" | custom-call | flops 800000000 | bytes 3000000 | tf_op jit(solution)/shard_map/project/pallas_call | solution.py:196
  18.7 0.5 %collective-permute-start.2 = (bf16[8,32,512]{2,1,0:T(8,128)(2,1)S(1)}, bf16[8,32,512]{2,1,0:T(8,128)(2,1)S(1)}, u32[]{:S(2)}, u32[]{:S(2)}) collective-permute-start(bf16[8,32,512]{2,1,0:T(8,128)(2,1)S(1)} %get-tuple-element.16), channel_id=1, source_target_pairs={{0,1},{1,0},{2,3},{3,2},{4,5},{5,4},{6,7},{7,6},{8,9},{9,8},{10,11... | collective-permute-start | bytes 786440 | tf_op jit(solution)/shard_map/ppermute | solution.py:297
  19.2 0.1 fusion.13
  19.3 1.1 %collective-permute-done.2 = bf16[8,32,512]{2,1,0:T(8,128)(2,1)S(1)} collective-permute-done((bf16[8,32,512]{2,1,0:T(8,128)(2,1)S(1)}, bf16[8,32,512]{2,1,0:T(8,128)(2,1)S(1)}, u32[]{:S(2)}, u32[]{:S(2)}) %collective-permute-start.2) | collective-permute-done | bytes 262176 | tf_op jit(solution)/shard_map/ppermute | solution.py:297
  20.5 4.4 %collective-permute-start.6 = (bf16[32,1024]{1,0:T(8,128)(2,1)S(1)}, bf16[32,1024]{1,0:T(8,128)(2,1)S(1)}, u32[]{:S(2)}, u32[]{:S(2)}) collective-permute-start(bf16[32,1024]{1,0:T(8,128)(2,1)S(1)} %pad_maximum_fusion.1), channel_id=1, source_target_pairs={{0,12},{1,13},{2,14},{3,15},{4,8},{5,9},{6,10},{7,11},{8,4},{9,5},... | collective-permute-start | bytes 196616 | tf_op jit(solution)/shard_map/ppermute | solution.py:305
  24.9 1.6 %collective-permute-start.7 = (bf16[32,1024]{1,0:T(8,128)(2,1)S(1)}, bf16[32,1024]{1,0:T(8,128)(2,1)S(1)}, u32[]{:S(2)}, u32[]{:S(2)}) collective-permute-start(bf16[32,1024]{1,0:T(8,128)(2,1)S(1)} %pad_maximum_fusion.2), channel_id=1, source_target_pairs={{0,14},{1,15},{2,12},{3,13},{4,10},{5,11},{6,8},{7,9},{8,6},{9,7},... | collective-permute-start | bytes 196616 | tf_op jit(solution)/shard_map/ppermute | solution.py:305
  26.5 0.8 %collective-permute-start.8 = (bf16[32,1024]{1,0:T(8,128)(2,1)S(1)}, bf16[32,1024]{1,0:T(8,128)(2,1)S(1)}, u32[]{:S(2)}, u32[]{:S(2)}) collective-permute-start(bf16[32,1024]{1,0:T(8,128)(2,1)S(1)} %pad_maximum_fusion.3), channel_id=1, source_target_pairs={{0,8},{1,9},{2,10},{3,11},{4,12},{5,13},{6,14},{7,15},{8,0},{9,1},... | collective-permute-start | bytes 196616 | tf_op jit(solution)/shard_map/ppermute | solution.py:305
  27.3 1.5 %collective-permute-start.9 = (bf16[32,1024]{1,0:T(8,128)(2,1)S(1)}, bf16[32,1024]{1,0:T(8,128)(2,1)S(1)}, u32[]{:S(2)}, u32[]{:S(2)}) collective-permute-start(bf16[32,1024]{1,0:T(8,128)(2,1)S(1)} %pad_maximum_fusion.4), channel_id=1, source_target_pairs={{0,10},{1,11},{2,8},{3,9},{4,14},{5,15},{6,12},{7,13},{8,2},{9,3},... | collective-permute-start | bytes 196616 | tf_op jit(solution)/shard_map/ppermute | solution.py:305
  28.8 1.5 %collective-permute-start.10 = (bf16[32,1024]{1,0:T(8,128)(2,1)S(1)}, bf16[32,1024]{1,0:T(8,128)(2,1)S(1)}, u32[]{:S(2)}, u32[]{:S(2)}) collective-permute-start(bf16[32,1024]{1,0:T(8,128)(2,1)S(1)} %pad_maximum_fusion.5), channel_id=1, source_target_pairs={{0,4},{1,5},{2,6},{3,7},{4,0},{5,1},{6,2},{7,3},{8,12},{9,13},{10,... | collective-permute-start | bytes 196616 | tf_op jit(solution)/shard_map/ppermute | solution.py:305
  30.3 2.2 %collective-permute-start.11 = (bf16[32,1024]{1,0:T(8,128)(2,1)S(1)}, bf16[32,1024]{1,0:T(8,128)(2,1)S(1)}, u32[]{:S(2)}, u32[]{:S(2)}) collective-permute-start(bf16[32,1024]{1,0:T(8,128)(2,1)S(1)} %pad_maximum_fusion.6), channel_id=1, source_target_pairs={{0,6},{1,7},{2,4},{3,5},{4,2},{5,3},{6,0},{7,1},{8,14},{9,15},{10,... | collective-permute-start | bytes 196616 | tf_op jit(solution)/shard_map/ppermute | solution.py:305
  32.5 0.2 collective-permute-done.7.refs_2_
  32.7 3.2 %collective-permute-done.8.refs_3_ = bf16[32,1024]{1,0:T(8,128)(2,1)S(1)} collective-permute-done((bf16[32,1024]{1,0:T(8,128)(2,1)S(1)}, bf16[32,1024]{1,0:T(8,128)(2,1)S(1)}, u32[]{:S(2)}, u32[]{:S(2)}) %collective-permute-start.8) | collective-permute-done | bytes 65568 | tf_op jit(solution)/shard_map/ppermute | solution.py:305
  35.8 2.1 %collective-permute-done.9.refs_4_ = bf16[32,1024]{1,0:T(8,128)(2,1)S(1)} collective-permute-done((bf16[32,1024]{1,0:T(8,128)(2,1)S(1)}, bf16[32,1024]{1,0:T(8,128)(2,1)S(1)}, u32[]{:S(2)}, u32[]{:S(2)}) %collective-permute-start.9) | collective-permute-done | bytes 65568 | tf_op jit(solution)/shard_map/ppermute | solution.py:305
  38.0 0.1 collective-permute-done.11.refs_6_
  38.1 0.1 collective-permute-done.12.refs_7_
  38.2 6.7 %frequency.1 = f32[256,32,512]{2,1,0:T(8,128)} custom-call(f32[512]{0:T(512)S(1)} %copy-done, f32[32,1024]{1,0:T(8,128)S(1)} %pad_maximum_fusion.refs_0_, bf16[32,1024]{1,0:T(8,128)(2,1)S(1)} %collective-permute-done.6.refs_1_, bf16[32,1024]{1,0:T(8,128)(2,1)S(1)} %collective-permute-done.7.refs_2_, bf16[32,1024]{1,0:T(8,128)(2,1)S(1)} %collective-permute-done.8.refs_3_, ...), custom_call_target="tpu_custom_call" | custom-call | flops 50000000 | bytes 17000000 | tf_op jit(solution)/shard_map/frequency/pallas_call | solution.py:258
  (19 shorter events, 0.1 us)
Async XLA Ops:
  1.3 14.9 %collective-permute-start.4 = (bf16[512,256]{1,0:T(8,128)(2,1)S(1)}, bf16[512,256]{1,0:T(8,128)(2,1)S(1)}, u32[]{:S(2)}, u32[]{:S(2)}) collective-permute-start(bf16[512,256]{1,0:T(8,128)(2,1)S(1)} %get-tuple-element.37), channel_id=1, source_target_pairs={{1,2},{3,4},{5,6},{7,8},{9,10},{11,12},{13,14},{2,1},{4,3},{6,5},{... | collective-permute-start | bytes 786440 | tf_op jit(solution)/shard_map/ppermute | solution.py:284
  1.9 14.2 %collective-permute-start.3 = (bf16[512,256]{1,0:T(8,128)(2,1)S(1)}, bf16[512,256]{1,0:T(8,128)(2,1)S(1)}, u32[]{:S(2)}, u32[]{:S(2)}) collective-permute-start(bf16[512,256]{1,0:T(8,128)(2,1)S(1)} %get-tuple-element.38), channel_id=1, source_target_pairs={{0,1},{1,0},{2,3},{3,2},{4,5},{5,4},{6,7},{7,6},{8,9},{9,8},{10,11... | collective-permute-start | bytes 786440 | tf_op jit(solution)/shard_map/ppermute | solution.py:286
  6.3 11.2 %collective-permute-start.1 = (bf16[512,256]{1,0:T(8,128)(2,1)S(1)}, bf16[512,256]{1,0:T(8,128)(2,1)S(1)}, u32[]{:S(2)}, u32[]{:S(2)}) collective-permute-start(bf16[512,256]{1,0:T(8,128)(2,1)S(1)} %get-tuple-element.35), channel_id=1, source_target_pairs={{1,2},{3,4},{5,6},{7,8},{9,10},{11,12},{13,14},{2,1},{4,3},{6,5},{... | collective-permute-start | bytes 786440 | tf_op jit(solution)/shard_map/ppermute | solution.py:284
  7.0 10.5 %collective-permute-start = (bf16[512,256]{1,0:T(8,128)(2,1)S(1)}, bf16[512,256]{1,0:T(8,128)(2,1)S(1)}, u32[]{:S(2)}, u32[]{:S(2)}) collective-permute-start(bf16[512,256]{1,0:T(8,128)(2,1)S(1)} %get-tuple-element.36), channel_id=1, source_target_pairs={{0,1},{1,0},{2,3},{3,2},{4,5},{5,4},{6,7},{7,6},{8,9},{9,8},{10,11... | collective-permute-start | bytes 786440 | tf_op jit(solution)/shard_map/ppermute | solution.py:286
  17.4 20.8 %copy-start = (f32[512]{0:T(512)S(1)}, f32[512]{0:T(512)}, u32[]{:S(2)}) copy-start(f32[512]{0:T(512)} %constant.17.clone.table) | copy-start | bytes 6148
  17.4 1.8 %collective-permute-start.5 = (bf16[8,32,512]{2,1,0:T(8,128)(2,1)S(1)}, bf16[8,32,512]{2,1,0:T(8,128)(2,1)S(1)}, u32[]{:S(2)}, u32[]{:S(2)}) collective-permute-start(bf16[8,32,512]{2,1,0:T(8,128)(2,1)S(1)} %get-tuple-element.18), channel_id=1, source_target_pairs={{0,1},{1,0},{2,3},{3,2},{4,5},{5,4},{6,7},{7,6},{8,9},{9,8},{10,11... | collective-permute-start | bytes 786440 | tf_op jit(solution)/shard_map/ppermute | solution.py:297
  18.7 1.7 %collective-permute-start.2 = (bf16[8,32,512]{2,1,0:T(8,128)(2,1)S(1)}, bf16[8,32,512]{2,1,0:T(8,128)(2,1)S(1)}, u32[]{:S(2)}, u32[]{:S(2)}) collective-permute-start(bf16[8,32,512]{2,1,0:T(8,128)(2,1)S(1)} %get-tuple-element.16), channel_id=1, source_target_pairs={{0,1},{1,0},{2,3},{3,2},{4,5},{5,4},{6,7},{7,6},{8,9},{9,8},{10,11... | collective-permute-start | bytes 786440 | tf_op jit(solution)/shard_map/ppermute | solution.py:297
  20.5 9.8 %collective-permute-start.6 = (bf16[32,1024]{1,0:T(8,128)(2,1)S(1)}, bf16[32,1024]{1,0:T(8,128)(2,1)S(1)}, u32[]{:S(2)}, u32[]{:S(2)}) collective-permute-start(bf16[32,1024]{1,0:T(8,128)(2,1)S(1)} %pad_maximum_fusion.1), channel_id=1, source_target_pairs={{0,12},{1,13},{2,14},{3,15},{4,8},{5,9},{6,10},{7,11},{8,4},{9,5},... | collective-permute-start | bytes 196616 | tf_op jit(solution)/shard_map/ppermute | solution.py:305
  24.9 7.7 %collective-permute-start.7 = (bf16[32,1024]{1,0:T(8,128)(2,1)S(1)}, bf16[32,1024]{1,0:T(8,128)(2,1)S(1)}, u32[]{:S(2)}, u32[]{:S(2)}) collective-permute-start(bf16[32,1024]{1,0:T(8,128)(2,1)S(1)} %pad_maximum_fusion.2), channel_id=1, source_target_pairs={{0,14},{1,15},{2,12},{3,13},{4,10},{5,11},{6,8},{7,9},{8,6},{9,7},... | collective-permute-start | bytes 196616 | tf_op jit(solution)/shard_map/ppermute | solution.py:305
  26.5 9.3 %collective-permute-start.8 = (bf16[32,1024]{1,0:T(8,128)(2,1)S(1)}, bf16[32,1024]{1,0:T(8,128)(2,1)S(1)}, u32[]{:S(2)}, u32[]{:S(2)}) collective-permute-start(bf16[32,1024]{1,0:T(8,128)(2,1)S(1)} %pad_maximum_fusion.3), channel_id=1, source_target_pairs={{0,8},{1,9},{2,10},{3,11},{4,12},{5,13},{6,14},{7,15},{8,0},{9,1},... | collective-permute-start | bytes 196616 | tf_op jit(solution)/shard_map/ppermute | solution.py:305
  27.3 10.6 %collective-permute-start.9 = (bf16[32,1024]{1,0:T(8,128)(2,1)S(1)}, bf16[32,1024]{1,0:T(8,128)(2,1)S(1)}, u32[]{:S(2)}, u32[]{:S(2)}) collective-permute-start(bf16[32,1024]{1,0:T(8,128)(2,1)S(1)} %pad_maximum_fusion.4), channel_id=1, source_target_pairs={{0,10},{1,11},{2,8},{3,9},{4,14},{5,15},{6,12},{7,13},{8,2},{9,3},... | collective-permute-start | bytes 196616 | tf_op jit(solution)/shard_map/ppermute | solution.py:305
  28.8 9.1 %collective-permute-start.10 = (bf16[32,1024]{1,0:T(8,128)(2,1)S(1)}, bf16[32,1024]{1,0:T(8,128)(2,1)S(1)}, u32[]{:S(2)}, u32[]{:S(2)}) collective-permute-start(bf16[32,1024]{1,0:T(8,128)(2,1)S(1)} %pad_maximum_fusion.5), channel_id=1, source_target_pairs={{0,4},{1,5},{2,6},{3,7},{4,0},{5,1},{6,2},{7,3},{8,12},{9,13},{10,... | collective-permute-start | bytes 196616 | tf_op jit(solution)/shard_map/ppermute | solution.py:305
  30.3 7.8 %collective-permute-start.11 = (bf16[32,1024]{1,0:T(8,128)(2,1)S(1)}, bf16[32,1024]{1,0:T(8,128)(2,1)S(1)}, u32[]{:S(2)}, u32[]{:S(2)}) collective-permute-start(bf16[32,1024]{1,0:T(8,128)(2,1)S(1)} %pad_maximum_fusion.6), channel_id=1, source_target_pairs={{0,6},{1,7},{2,4},{3,5},{4,2},{5,3},{6,0},{7,1},{8,14},{9,15},{10,... | collective-permute-start | bytes 196616 | tf_op jit(solution)/shard_map/ppermute | solution.py:305
  32.6 5.5 %collective-permute-start.12 = (bf16[32,1024]{1,0:T(8,128)(2,1)S(1)}, bf16[32,1024]{1,0:T(8,128)(2,1)S(1)}, u32[]{:S(2)}, u32[]{:S(2)}) collective-permute-start(bf16[32,1024]{1,0:T(8,128)(2,1)S(1)} %pad_maximum_fusion.7), channel_id=1, source_target_pairs={{0,2},{1,3},{2,0},{3,1},{4,6},{5,7},{6,4},{7,5},{8,10},{9,11},{10,... | collective-permute-start | bytes 196616 | tf_op jit(solution)/shard_map/ppermute | solution.py:305

commit v2 on v1

--- a/solution.py
+++ b/solution.py
@@ -36,6 +36,7 @@
 
 def tiles_kernel(
     count,
+    split,
     mask,
     green,
     integrals,
@@ -46,6 +47,7 @@
     gbuf,
     ibuf,
     own,
+    turned,
     pattern,
     order,
     sems,
@@ -81,7 +83,13 @@
     own_copy.wait()
     for row in range(count):
         rows = slice(row * TILE, (row + 1) * TILE)
-        transposed[:, rows] = own[rows, :].T
+        (turned if split else transposed)[:, rows] = own[rows, :].T
+    if split:
+        place = lax.axis_index("trow")
+        size = NMO // 16
+        for k in range(16):
+            owner = lax.bitwise_xor(place, 2 * (k % 8) + k // 8)
+            transposed[k * size : (k + 1) * size, :] = turned[pl.ds(pl.multiple_of(owner * size, size), size), :]
 
     @pl.loop(0, pl.cdiv(found, GROUP))
     def _(group):
@@ -103,13 +111,13 @@
         part[row] = contract(sigma, row, slots, own, row + slots[0] - BAND)
 
 
-def tiles(green, integrals, pattern, coefficients):
+def tiles(green, integrals, pattern, coefficients, split):
     count = green.shape[0]
     hbm = pl.BlockSpec(memory_space=pltpu.HBM)
     vmem = pl.BlockSpec(memory_space=pltpu.VMEM)
     placed = [pltpu.with_memory_space_constraint(x, pltpu.HBM) for x in (pattern, green, integrals, coefficients)]
     return pl.pallas_call(
-        functools.partial(tiles_kernel, count),
+        functools.partial(tiles_kernel, count, split),
         out_shape=(
             pltpu.VMEM((count, PAIRS * TILE, NMO), jnp.float32),
             pltpu.VMEM((count, SLOTS, PAIRS * TILE, TILE), jnp.bfloat16),
@@ -121,6 +129,7 @@
             pltpu.VMEM((count * SLOTS, TAU, TILE, TILE), jnp.bfloat16),
             pltpu.VMEM((count * SLOTS, TILE, TILE), jnp.bfloat16),
             pltpu.VMEM((count * TILE, NMO), jnp.bfloat16),
+            pltpu.VMEM((NMO, count * TILE), jnp.bfloat16),
             pltpu.SMEM((count, SLOTS), jnp.int32),
             pltpu.SMEM((count * SLOTS + GROUP,), jnp.int32),
             pltpu.SemaphoreType.DMA((count * SLOTS, 2)),
@@ -132,7 +141,7 @@
     )(*placed)
 
 
-def beside(count, row, left, sigma, block):
+def outer(count, row, left, sigma, block):
     before, _, after = sides(count, row)
     slots = before if left else after
     if not slots:
@@ -141,17 +150,15 @@
 
 
 def project_kernel(count, split, piece, *refs):
-    part, sigma, near, halo, transposed = refs[:5]
-    outs, half = refs[5:-1], refs[-1]
-    me = lax.axis_index("trow")
-    first = lax.rem(me, 2) == 0
+    part, sigma, near, halo, transposed, out, half = refs
+    first = lax.rem(lax.axis_index("trow"), 2) == 0
     columns = slice(piece * COLUMNS, (piece + 1) * COLUMNS)
 
     def finish(far_left):
         for row in range(count):
             value = part[row, :, columns]
             for left, block in ((not far_left, near), (far_left, halo)):
-                term = beside(count, row, left, sigma, block)
+                term = outer(count, row, left, sigma, block)
                 value = value if term is None else value + term
             for t in range(PAIRS):
                 half[row * TILE : (row + 1) * TILE, t * COLUMNS : (t + 1) * COLUMNS] = value[
@@ -166,22 +173,8 @@
     def _():
         finish(False)
 
-    for k in range(NMO // TILE):
-        block = lax.bitwise_xor(lax.div(me, 4), k) if split else k
-        lhs = transposed[pl.ds(pl.multiple_of(block * TILE, TILE), TILE), :]
-        total = jnp.dot(lhs, half[...], preferred_element_type=jnp.float32)
-        if not split:
-            outs[0][k * TILE : (k + 1) * TILE] = total
-            continue
-        keep, send = outs
-        quarter = TILE // 4
-        quarters = [total[q * quarter : (q + 1) * quarter] for q in range(4)]
-        low_x = lax.rem(lax.div(me, 2), 2) == 0
-        mine = [jnp.where(first, quarters[2 * x], quarters[2 * x + 1]) for x in range(2)]
-        other = [jnp.where(first, quarters[2 * x + 1], quarters[2 * x]) for x in range(2)]
-        for ref, pair in ((keep, mine), (send, other)):
-            ref[2 * k] = jnp.where(low_x, pair[0], pair[1]).astype(ref.dtype)
-            ref[2 * k + 1] = jnp.where(low_x, pair[1], pair[0]).astype(ref.dtype)
+    rows = slice(NMO // 2, NMO) if split else slice(0, NMO)
+    out[...] = jnp.dot(transposed[rows, :], half[...], preferred_element_type=jnp.float32).astype(out.dtype)
 
 
 def project(part, sigma, near, halo, transposed, split, piece):
@@ -189,20 +182,35 @@
     operands = (part, sigma, near, halo, transposed)
     vmem = pl.BlockSpec(memory_space=pltpu.VMEM)
     if split:
-        shape = (8, NMO // 16, PAIRS * COLUMNS)
-        out_shape = (pltpu.VMEM(shape, jnp.float32), pltpu.VMEM(shape, jnp.bfloat16))
+        out_shape = pltpu.VMEM((NMO // 2, PAIRS * COLUMNS), jnp.bfloat16)
     else:
-        out_shape = (jax.ShapeDtypeStruct((NMO, PAIRS * COLUMNS), jnp.float32),)
+        out_shape = jax.ShapeDtypeStruct((NMO, PAIRS * COLUMNS), jnp.float32)
     return pl.pallas_call(
         functools.partial(project_kernel, count, split, piece),
-        out_shape=out_shape,
+        out_shape=(out_shape, pltpu.VMEM((count * TILE, PAIRS * COLUMNS), jnp.bfloat16)),
         in_specs=[vmem] * len(operands),
-        out_specs=tuple(vmem for _ in out_shape),
-        scratch_shapes=[pltpu.VMEM((count * TILE, PAIRS * COLUMNS), jnp.bfloat16)],
+        out_specs=(vmem, vmem),
         compiler_params=pltpu.CompilerParams(vmem_limit_bytes=16 * MIB),
-        cost_estimate=pl.CostEstimate(flops=800_000_000, bytes_accessed=3_000_000, transcendentals=0),
+        cost_estimate=pl.CostEstimate(flops=500_000_000, bytes_accessed=3_000_000, transcendentals=0),
         name="project",
     )(*[pltpu.with_memory_space_constraint(x, pltpu.VMEM) for x in operands])
+
+
+def keep_kernel(half, transposed, out):
+    out[...] = jnp.dot(transposed[: NMO // 2, :], half[...], preferred_element_type=jnp.float32)
+
+
+def project_own(half, transposed):
+    vmem = pl.BlockSpec(memory_space=pltpu.VMEM)
+    return pl.pallas_call(
+        keep_kernel,
+        out_shape=pltpu.VMEM((NMO // 2, half.shape[1]), jnp.float32),
+        in_specs=[vmem, vmem],
+        out_specs=vmem,
+        compiler_params=pltpu.CompilerParams(vmem_limit_bytes=16 * MIB),
+        cost_estimate=pl.CostEstimate(flops=400_000_000, bytes_accessed=2_000_000, transcendentals=0),
+        name="project_own",
+    )(*[pltpu.with_memory_space_constraint(x, pltpu.VMEM) for x in (half, transposed)])
 
 
 def freq_tables():
@@ -284,7 +292,7 @@
         halos.append(lax.ppermute(away, "trow", pairs))
         inner = lax.dynamic_slice(coefficients, ((1 - core) * (rows - width), piece * COLUMNS), (width, COLUMNS))
         nears.append(lax.ppermute(inner, "trow", partner))
-    part, sigma, transposed = tiles(green, integrals, pattern, coefficients)
+    part, sigma, transposed = tiles(green, integrals, pattern, coefficients, devices == 16)
     if devices != 16:
         summed = jnp.concatenate(
             [project(part, sigma, nears[piece], halos[piece], transposed, False, piece)[0] for piece in range(CHUNKS)], axis=1
@@ -292,17 +300,25 @@
         return frequency(lax.psum_scatter(summed, "trow", scatter_dimension=0, tiled=True))
     keeps, arrived = [], []
     for piece in range(CHUNKS):
-        keep, send = project(part, sigma, nears[piece], halos[piece], transposed, True, piece)
-        keeps.append(keep)
+        send, half = project(part, sigma, nears[piece], halos[piece], transposed, True, piece)
         arrived.append(lax.ppermute(send, "trow", partner))
+        keeps.append(project_own(half, transposed))
+    size = NMO // 16
+    both = list(zip(keeps, arrived))
     sums = [
-        jnp.concatenate([keep[k] + other[k].astype(jnp.float32) for keep, other in zip(keeps, arrived)], axis=1)
+        jnp.concatenate(
+            [keep[k * size : (k + 1) * size] + other[k * size : (k + 1) * size].astype(jnp.float32) for keep, other in both],
+            axis=1,
+        )
         for k in range(8)
     ]
-    terms = [sums[0]]
-    for k in (6, 7, 4, 5, 2, 3, 1):
-        moves = [(i, i ^ (2 * k)) for i in range(devices)]
-        terms.append(lax.ppermute(sums[k].astype(jnp.bfloat16), "trow", moves))
+    cast = [value.astype(jnp.bfloat16) for value in sums]
+    flip = {k: [(i, i ^ (2 * k)) for i in range(devices)] for k in range(1, 8)}
+    far = [lax.ppermute(cast[k], "trow", flip[k]) for k in (6, 7)]
+    beside = lax.ppermute(jnp.stack([cast[1], cast[3]]), "trow", flip[1])
+    far += [lax.ppermute(cast[k], "trow", flip[k]) for k in (4, 5)]
+    onward = (sums[2] + beside[1].astype(jnp.float32)).astype(jnp.bfloat16)
+    terms = [sums[0], beside[0]] + far + [lax.ppermute(onward, "trow", flip[2])]
     return frequency(*terms)
 
 

time: 45.1 us -> 44.5 us (0.987)
  waiting for transfers between devices: 6.76 us -> 5.22 us
  Pallas kernels: 15.4 us -> 16.1 us
    pallas_call x1 -> x3, Pallas kernels: 6.24 us -> 7.49 us  [the longest x1 6.77 us: tiles(): pl.pallas_call(functools.partial(tiles_kernel, count, split), out_shape=(...]
    ppermute x7 -> x6, waiting for transfers between devices: 5.67 us -> 4.88 us  [the longest x1 2.49 us: local(): beside = lax.ppermute(jnp.stack([cast[1], cast[3]]), 'trow', flip[1])]
    ppermute x2, waiting for transfers between devices: 1.08 us -> 0.34 us  [local(): arrived.append(lax.ppermute(send, 'trow', partner))]
    pallas_call x2, Pallas kernels: 2.39 us -> 1.91 us  [project(): pl.pallas_call(functools.partial(project_kernel, count, split, piece), ou...]
    ppermute x7 -> x6, starting transfers between devices: 11.9 us -> 12.1 us  [the longest x2 5.75 us: local(): far = [lax.ppermute(cast[k], 'trow', flip[k]) for k in (6, 7)]]
  transfers between devices with their start and end apart: 13 -> 12, of which waited for: 6 -> 4; matrix products, arithmetic and copies ran while one was open for 0% -> 0% of each run, Pallas kernels for 19% -> 21%
where the time goes in v2:
time: 44.5 us; the launch traced here: 44.3 us
  starting transfers between devices  21.4 us (48%)
  Pallas kernels  16.1 us (36%)
  waiting for transfers between devices  5.22 us (12%)
  local copies, waits for them, and re-layouts  1.26 us (3%)
    ppermute x2, starting transfers between devices, local(): nears.append(lax.ppermute(inner, 'trow', partner))  7.31 us
    pallas_call x1, Pallas kernels, tiles(): pl.pallas_call(functools.partial(tiles_kernel, count, split), out_shape=(...  6.77 us
    pallas_call x1, Pallas kernels, frequency(): pl.pallas_call(functools.partial(frequency_kernel, len(terms)), out_shape...  6.72 us
    ppermute x2, starting transfers between devices, local(): far = [lax.ppermute(cast[k], 'trow', flip[k]) for k in (6, 7)]  5.75 us
    ppermute x2, starting transfers between devices, local(): far += [lax.ppermute(cast[k], 'trow', flip[k]) for k in (4, 5)]  4.34 us
    ppermute x1, waiting for transfers between devices, local(): beside = lax.ppermute(jnp.stack([cast[1], cast[3]]), 'trow', flip[1])  2.49 us
    ppermute x2, waiting for transfers between devices, local(): far += [lax.ppermute(cast[k], 'trow', flip[k]) for k in (4, 5)]  2.38 us
    ppermute x1, starting transfers between devices, local(): terms = [sums[0], beside[0]] + far + [lax.ppermute(onward, 'trow', flip[2])]  1.93 us
  transfers between devices with their start and end apart: 12, of which 4 were waited for; matrix products, arithmetic and copies ran while one was open for 0% of the time, Pallas kernels for 21%

profile of v2, /device:TPU:0, one launch (start us, length us, event | category | flops | bytes accessed | tf_op | source)
XLA Modules:
  0.0 44.3 jit_solution(4736044500266353073)
XLA Ops:
  0.0 1.3 %constant_dynamic-slice_fusion.2 = (bf16[512,256]{1,0:T(8,128)(2,1)S(1)}, bf16[512,256]{1,0:T(8,128)(2,1)S(1)}, bf16[512,256]{1,0:T(8,128)(2,1)S(1)}, bf16[512,256]{1,0:T(8,128)(2,1)S(1)}) fusion(bf16[768,512]{1,0:T(8,128)(2,1)} %coefficients.1, s32[]{:T(128)S(6)} %select_n.9, s32[]{:T(128)S(6)} %select_n.8), kind=kLoop, calls=%fused_computation.44 | loop fusion | bytes 2097160 | tf_op jit(solution)/shard_map/dynamic_slice | solution.py:291
  1.3 0.7 %collective-permute-start.4 = (bf16[512,256]{1,0:T(8,128)(2,1)S(1)}, bf16[512,256]{1,0:T(8,128)(2,1)S(1)}, u32[]{:S(2)}, u32[]{:S(2)}) collective-permute-start(bf16[512,256]{1,0:T(8,128)(2,1)S(1)} %get-tuple-element.37), channel_id=1, source_target_pairs={{1,2},{3,4},{5,6},{7,8},{9,10},{11,12},{13,14},{2,1},{4,3},{6,5},{... | collective-permute-start | bytes 786440 | tf_op jit(solution)/shard_map/ppermute | solution.py:292
  1.9 4.3 %collective-permute-start.3 = (bf16[512,256]{1,0:T(8,128)(2,1)S(1)}, bf16[512,256]{1,0:T(8,128)(2,1)S(1)}, u32[]{:S(2)}, u32[]{:S(2)}) collective-permute-start(bf16[512,256]{1,0:T(8,128)(2,1)S(1)} %get-tuple-element.38), channel_id=1, source_target_pairs={{0,1},{1,0},{2,3},{3,2},{4,5},{5,4},{6,7},{7,6},{8,9},{9,8},{10,11... | collective-permute-start | bytes 786440 | tf_op jit(solution)/shard_map/ppermute | solution.py:294
  6.3 0.7 %collective-permute-start.1 = (bf16[512,256]{1,0:T(8,128)(2,1)S(1)}, bf16[512,256]{1,0:T(8,128)(2,1)S(1)}, u32[]{:S(2)}, u32[]{:S(2)}) collective-permute-start(bf16[512,256]{1,0:T(8,128)(2,1)S(1)} %get-tuple-element.35), channel_id=1, source_target_pairs={{1,2},{3,4},{5,6},{7,8},{9,10},{11,12},{13,14},{2,1},{4,3},{6,5},{... | collective-permute-start | bytes 786440 | tf_op jit(solution)/shard_map/ppermute | solution.py:292
  7.0 3.0 %collective-permute-start = (bf16[512,256]{1,0:T(8,128)(2,1)S(1)}, bf16[512,256]{1,0:T(8,128)(2,1)S(1)}, u32[]{:S(2)}, u32[]{:S(2)}) collective-permute-start(bf16[512,256]{1,0:T(8,128)(2,1)S(1)} %get-tuple-element.36), channel_id=1, source_target_pairs={{0,1},{1,0},{2,3},{3,2},{4,5},{5,4},{6,7},{7,6},{8,9},{9,8},{10,11... | collective-permute-start | bytes 786440 | tf_op jit(solution)/shard_map/ppermute | solution.py:294
  9.9 6.8 %tiles.1 = (f32[6,256,512]{2,1,0:T(8,128)S(1)}, bf16[6,9,256,128]{3,2,1,0:T(8,128)(2,1)S(1)}, bf16[512,768]{1,0:T(8,128)(2,1)S(1)}) custom-call(s32[6,9]{1,0:T(8,128)} %mask.1, bf16[6,9,4,128,128]{4,3,2,1,0:T(8,128)(2,1)} %green.1, bf16[6,9,128,128]{3,2,1,0:T(8,128)(2,1)} %integrals.1, bf16[768,512]{1,0:T(8,128)(2,1)} %coefficients.1), custom_call_target="tpu_custom_call" | custom-call | flops 2000000000 | bytes 12000000 | tf_op jit(solution)/shard_map/tiles/pallas_call | solution.py:119
  16.7 1.0 %project.3 = (bf16[256,512]{1,0:T(8,128)(2,1)S(1)}, bf16[768,512]{1,0:T(8,128)(2,1)S(1)}) custom-call(f32[6,256,512]{2,1,0:T(8,128)S(1)} %get-tuple-element.12.refs_0_, bf16[6,9,256,128]{3,2,1,0:T(8,128)(2,1)S(1)} %get-tuple-element.13.refs_1_, bf16[512,256]{1,0:T(8,128)(2,1)S(1)} %collective-permute-done.3.refs_2_, ...), custom_call_target="tpu_custom_call" | custom-call | flops 500000000 | bytes 3000000 | tf_op jit(solution)/shard_map/project/pallas_call | solution.py:188
  17.7 0.1 collective-permute-start.5
  17.8 1.0 %project.2 = (bf16[256,512]{1,0:T(8,128)(2,1)S(1)}, bf16[768,512]{1,0:T(8,128)(2,1)S(1)}) custom-call(f32[6,256,512]{2,1,0:T(8,128)S(1)} %get-tuple-element.12.refs_0_, bf16[6,9,256,128]{3,2,1,0:T(8,128)(2,1)S(1)} %get-tuple-element.13.refs_1_, bf16[512,256]{1,0:T(8,128)(2,1)S(1)} %collective-permute-done.refs_2_, ...), custom_call_target="tpu_custom_call" | custom-call | flops 500000000 | bytes 3000000 | tf_op jit(solution)/shard_map/project/pallas_call | solution.py:188
  18.7 0.5 %collective-permute-start.2 = (bf16[256,512]{1,0:T(8,128)(2,1)S(1)}, bf16[256,512]{1,0:T(8,128)(2,1)S(1)}, u32[]{:S(2)}, u32[]{:S(2)}) collective-permute-start(bf16[256,512]{1,0:T(8,128)(2,1)S(1)} %get-tuple-element.16), channel_id=1, source_target_pairs={{0,1},{1,0},{2,3},{3,2},{4,5},{5,4},{6,7},{7,6},{8,9},{9,8},{10,11... | collective-permute-start | bytes 786440 | tf_op jit(solution)/shard_map/ppermute | solution.py:304
  19.3 0.4 project_own.2
  19.7 0.4 project_own.3
  20.0 0.1 slice_add_fusion
  20.1 0.3 collective-permute-done.2
  20.5 4.1 %collective-permute-start.7 = (bf16[32,1024]{1,0:T(8,128)(2,1)S(1)}, bf16[32,1024]{1,0:T(8,128)(2,1)S(1)}, u32[]{:S(2)}, u32[]{:S(2)}) collective-permute-start(bf16[32,1024]{1,0:T(8,128)(2,1)S(1)} %pad_maximum_fusion.1), channel_id=1, source_target_pairs={{0,12},{1,13},{2,14},{3,15},{4,8},{5,9},{6,10},{7,11},{8,4},{9,5},... | collective-permute-start | bytes 196616 | tf_op jit(solution)/shard_map/ppermute | solution.py:317
  24.7 1.6 %collective-permute-start.8 = (bf16[32,1024]{1,0:T(8,128)(2,1)S(1)}, bf16[32,1024]{1,0:T(8,128)(2,1)S(1)}, u32[]{:S(2)}, u32[]{:S(2)}) collective-permute-start(bf16[32,1024]{1,0:T(8,128)(2,1)S(1)} %pad_maximum_fusion.2), channel_id=1, source_target_pairs={{0,14},{1,15},{2,12},{3,13},{4,10},{5,11},{6,8},{7,9},{8,6},{9,7},... | collective-permute-start | bytes 196616 | tf_op jit(solution)/shard_map/ppermute | solution.py:317
  26.3 0.8 %collective-permute-start.9 = (bf16[32,1024]{1,0:T(8,128)(2,1)S(1)}, bf16[32,1024]{1,0:T(8,128)(2,1)S(1)}, u32[]{:S(2)}, u32[]{:S(2)}) collective-permute-start(bf16[32,1024]{1,0:T(8,128)(2,1)S(1)} %pad_maximum_fusion.3), channel_id=1, source_target_pairs={{0,8},{1,9},{2,10},{3,11},{4,12},{5,13},{6,14},{7,15},{8,0},{9,1},... | collective-permute-start | bytes 196616 | tf_op jit(solution)/shard_map/ppermute | solution.py:319
  27.1 0.1 collective-permute-start.6
  27.2 3.5 %collective-permute-start.10 = (bf16[32,1024]{1,0:T(8,128)(2,1)S(1)}, bf16[32,1024]{1,0:T(8,128)(2,1)S(1)}, u32[]{:S(2)}, u32[]{:S(2)}) collective-permute-start(bf16[32,1024]{1,0:T(8,128)(2,1)S(1)} %pad_maximum_fusion.4), channel_id=1, source_target_pairs={{0,10},{1,11},{2,8},{3,9},{4,14},{5,15},{6,12},{7,13},{8,2},{9,3},... | collective-permute-start | bytes 196616 | tf_op jit(solution)/shard_map/ppermute | solution.py:319
  30.8 2.5 %collective-permute-done.6 = bf16[2,32,1024]{2,1,0:T(8,128)(2,1)S(1)} collective-permute-done((bf16[2,32,1024]{2,1,0:T(8,128)(2,1)S(1)}, bf16[2,32,1024]{2,1,0:T(8,128)(2,1)S(1)}, u32[]{:S(2)}, u32[]{:S(2)}) %collective-permute-start.6) | collective-permute-done | bytes 131104 | tf_op jit(solution)/shard_map/ppermute | solution.py:318
  33.3 1.9 %collective-permute-start.11 = (bf16[32,1024]{1,0:T(8,128)(2,1)S(1)}, bf16[32,1024]{1,0:T(8,128)(2,1)S(1)}, u32[]{:S(2)}, u32[]{:S(2)}) collective-permute-start(bf16[32,1024]{1,0:T(8,128)(2,1)S(1)} %fusion), channel_id=1, source_target_pairs={{0,4},{1,5},{2,6},{3,7},{4,0},{5,1},{6,2},{7,3},{8,12},{9,13},{10,... | collective-permute-start | bytes 196616 | tf_op jit(solution)/shard_map/ppermute | solution.py:321
  35.2 0.4 collective-permute-done.9.refs_4_
  35.6 2.0 %collective-permute-done.10.refs_5_ = bf16[32,1024]{1,0:T(8,128)(2,1)S(1)} collective-permute-done((bf16[32,1024]{1,0:T(8,128)(2,1)S(1)}, bf16[32,1024]{1,0:T(8,128)(2,1)S(1)}, u32[]{:S(2)}, u32[]{:S(2)}) %collective-permute-start.10) | collective-permute-done | bytes 65568 | tf_op jit(solution)/shard_map/ppermute | solution.py:319
  37.6 6.7 %frequency.1 = f32[256,32,512]{2,1,0:T(8,128)} custom-call(f32[512]{0:T(512)S(1)} %copy-done, f32[32,1024]{1,0:T(8,128)S(1)} %pad_maximum_fusion.refs_0_, bf16[32,1024]{1,0:T(8,128)(2,1)S(1)} %slice_bitcast_fusion.1.refs_1_, bf16[32,1024]{1,0:T(8,128)(2,1)S(1)} %collective-permute-done.7.refs_2_, bf16[32,1024]{1,0:T(8,128)(2,1)S(1)} %collective-permute-done.8.refs_3_, ...), custom_call_target="tpu_custom_call" | custom-call | flops 50000000 | bytes 17000000 | tf_op jit(solution)/shard_map/frequency/pallas_call | solution.py:266
  (19 shorter events, 0.2 us)
Async XLA Ops:
  1.3 15.4 %collective-permute-start.4 = (bf16[512,256]{1,0:T(8,128)(2,1)S(1)}, bf16[512,256]{1,0:T(8,128)(2,1)S(1)}, u32[]{:S(2)}, u32[]{:S(2)}) collective-permute-start(bf16[512,256]{1,0:T(8,128)(2,1)S(1)} %get-tuple-element.37), channel_id=1, source_target_pairs={{1,2},{3,4},{5,6},{7,8},{9,10},{11,12},{13,14},{2,1},{4,3},{6,5},{... | collective-permute-start | bytes 786440 | tf_op jit(solution)/shard_map/ppermute | solution.py:292
  1.9 14.8 %collective-permute-start.3 = (bf16[512,256]{1,0:T(8,128)(2,1)S(1)}, bf16[512,256]{1,0:T(8,128)(2,1)S(1)}, u32[]{:S(2)}, u32[]{:S(2)}) collective-permute-start(bf16[512,256]{1,0:T(8,128)(2,1)S(1)} %get-tuple-element.38), channel_id=1, source_target_pairs={{0,1},{1,0},{2,3},{3,2},{4,5},{5,4},{6,7},{7,6},{8,9},{9,8},{10,11... | collective-permute-start | bytes 786440 | tf_op jit(solution)/shard_map/ppermute | solution.py:294
  6.3 11.5 %collective-permute-start.1 = (bf16[512,256]{1,0:T(8,128)(2,1)S(1)}, bf16[512,256]{1,0:T(8,128)(2,1)S(1)}, u32[]{:S(2)}, u32[]{:S(2)}) collective-permute-start(bf16[512,256]{1,0:T(8,128)(2,1)S(1)} %get-tuple-element.35), channel_id=1, source_target_pairs={{1,2},{3,4},{5,6},{7,8},{9,10},{11,12},{13,14},{2,1},{4,3},{6,5},{... | collective-permute-start | bytes 786440 | tf_op jit(solution)/shard_map/ppermute | solution.py:292
  7.0 10.8 %collective-permute-start = (bf16[512,256]{1,0:T(8,128)(2,1)S(1)}, bf16[512,256]{1,0:T(8,128)(2,1)S(1)}, u32[]{:S(2)}, u32[]{:S(2)}) collective-permute-start(bf16[512,256]{1,0:T(8,128)(2,1)S(1)} %get-tuple-element.36), channel_id=1, source_target_pairs={{0,1},{1,0},{2,3},{3,2},{4,5},{5,4},{6,7},{7,6},{8,9},{9,8},{10,11... | collective-permute-start | bytes 786440 | tf_op jit(solution)/shard_map/ppermute | solution.py:294
  17.7 2.3 %collective-permute-start.5 = (bf16[256,512]{1,0:T(8,128)(2,1)S(1)}, bf16[256,512]{1,0:T(8,128)(2,1)S(1)}, u32[]{:S(2)}, u32[]{:S(2)}) collective-permute-start(bf16[256,512]{1,0:T(8,128)(2,1)S(1)} %get-tuple-element.18), channel_id=1, source_target_pairs={{0,1},{1,0},{2,3},{3,2},{4,5},{5,4},{6,7},{7,6},{8,9},{9,8},{10,11... | collective-permute-start | bytes 786440 | tf_op jit(solution)/shard_map/ppermute | solution.py:304
  18.7 1.7 %collective-permute-start.2 = (bf16[256,512]{1,0:T(8,128)(2,1)S(1)}, bf16[256,512]{1,0:T(8,128)(2,1)S(1)}, u32[]{:S(2)}, u32[]{:S(2)}) collective-permute-start(bf16[256,512]{1,0:T(8,128)(2,1)S(1)} %get-tuple-element.16), channel_id=1, source_target_pairs={{0,1},{1,0},{2,3},{3,2},{4,5},{5,4},{6,7},{7,6},{8,9},{9,8},{10,11... | collective-permute-start | bytes 786440 | tf_op jit(solution)/shard_map/ppermute | solution.py:304
  19.3 18.3 %copy-start = (f32[512]{0:T(512)S(1)}, f32[512]{0:T(512)}, u32[]{:S(2)}) copy-start(f32[512]{0:T(512)} %constant.17.clone.table) | copy-start | bytes 6148
  20.5 14.7 %collective-permute-start.7 = (bf16[32,1024]{1,0:T(8,128)(2,1)S(1)}, bf16[32,1024]{1,0:T(8,128)(2,1)S(1)}, u32[]{:S(2)}, u32[]{:S(2)}) collective-permute-start(bf16[32,1024]{1,0:T(8,128)(2,1)S(1)} %pad_maximum_fusion.1), channel_id=1, source_target_pairs={{0,12},{1,13},{2,14},{3,15},{4,8},{5,9},{6,10},{7,11},{8,4},{9,5},... | collective-permute-start | bytes 196616 | tf_op jit(solution)/shard_map/ppermute | solution.py:317
  24.7 10.6 %collective-permute-start.8 = (bf16[32,1024]{1,0:T(8,128)(2,1)S(1)}, bf16[32,1024]{1,0:T(8,128)(2,1)S(1)}, u32[]{:S(2)}, u32[]{:S(2)}) collective-permute-start(bf16[32,1024]{1,0:T(8,128)(2,1)S(1)} %pad_maximum_fusion.2), channel_id=1, source_target_pairs={{0,14},{1,15},{2,12},{3,13},{4,10},{5,11},{6,8},{7,9},{8,6},{9,7},... | collective-permute-start | bytes 196616 | tf_op jit(solution)/shard_map/ppermute | solution.py:317
  26.3 9.3 %collective-permute-start.9 = (bf16[32,1024]{1,0:T(8,128)(2,1)S(1)}, bf16[32,1024]{1,0:T(8,128)(2,1)S(1)}, u32[]{:S(2)}, u32[]{:S(2)}) collective-permute-start(bf16[32,1024]{1,0:T(8,128)(2,1)S(1)} %pad_maximum_fusion.3), channel_id=1, source_target_pairs={{0,8},{1,9},{2,10},{3,11},{4,12},{5,13},{6,14},{7,15},{8,0},{9,1},... | collective-permute-start | bytes 196616 | tf_op jit(solution)/shard_map/ppermute | solution.py:319
  27.1 6.2 %collective-permute-start.6 = (bf16[2,32,1024]{2,1,0:T(8,128)(2,1)S(1)}, bf16[2,32,1024]{2,1,0:T(8,128)(2,1)S(1)}, u32[]{:S(2)}, u32[]{:S(2)}) collective-permute-start(bf16[2,32,1024]{2,1,0:T(8,128)(2,1)S(1)} %maximum_maximum_fusion), channel_id=1, source_target_pairs={{0,2},{1,3},{2,0},{3,1},{4,6},{5,7},{6,4},{7,5},{8,10},{9,11},{10,... | collective-permute-start | bytes 393224 | tf_op jit(solution)/shard_map/ppermute | solution.py:318
  27.2 10.4 %collective-permute-start.10 = (bf16[32,1024]{1,0:T(8,128)(2,1)S(1)}, bf16[32,1024]{1,0:T(8,128)(2,1)S(1)}, u32[]{:S(2)}, u32[]{:S(2)}) collective-permute-start(bf16[32,1024]{1,0:T(8,128)(2,1)S(1)} %pad_maximum_fusion.4), channel_id=1, source_target_pairs={{0,10},{1,11},{2,8},{3,9},{4,14},{5,15},{6,12},{7,13},{8,2},{9,3},... | collective-permute-start | bytes 196616 | tf_op jit(solution)/shard_map/ppermute | solution.py:319
  33.3 4.3 %collective-permute-start.11 = (bf16[32,1024]{1,0:T(8,128)(2,1)S(1)}, bf16[32,1024]{1,0:T(8,128)(2,1)S(1)}, u32[]{:S(2)}, u32[]{:S(2)}) collective-permute-start(bf16[32,1024]{1,0:T(8,128)(2,1)S(1)} %fusion), channel_id=1, source_target_pairs={{0,4},{1,5},{2,6},{3,7},{4,0},{5,1},{6,2},{7,3},{8,12},{9,13},{10,... | collective-permute-start | bytes 196616 | tf_op jit(solution)/shard_map/ppermute | solution.py:321

commit v3 on v2

--- a/solution.py
+++ b/solution.py
@@ -15,7 +15,9 @@
 NMO = 512
 NW = 128
 SLOTS = 9
-FREQ_BLOCK = 16
+FREQ_STEP = 4
+FREQ_EDGES = [0, 2, 4, 8, 16, *range(32, 2 * NW + 1, 32)]
+FREQ_BLOCKS = list(zip(FREQ_EDGES, FREQ_EDGES[1:]))
 GROUP = 4
 CHUNKS = 2
 COLUMNS = NMO // CHUNKS
@@ -223,7 +225,7 @@
     angle = pi * (np.float32(2.0) * freq[:, None] + np.float32(1.0)) * nodes[None, :]
     both = np.concatenate([weights[None, :] * np.cos(angle), weights[None, :] * np.sin(angle)], axis=0)
     folded = both[:, :PAIRS] + both[:, : PAIRS - 1 : -1]
-    return folded.astype(np.float32).reshape(-1)
+    return np.repeat(folded.astype(np.float32).reshape(-1, 1), TILE, axis=1)
 
 
 def frequency_kernel(terms, table, *refs):
@@ -239,25 +241,26 @@
         for t in range(PAIRS)
     ]
 
-    def copy(step):
-        rows = pl.ds(step * FREQ_BLOCK, FREQ_BLOCK)
-        return pltpu.make_async_copy(buffer.at[rows], out.at[rows], sems.at[step])
-
-    @pl.loop(0, 2 * NW // FREQ_BLOCK)
-    def _(step):
-        @pl.loop(0, FREQ_BLOCK, unroll=4)
-        def _(n):
-            at = (step * FREQ_BLOCK + n) * PAIRS
-            value = table[at] * points[0]
-            for t in range(1, PAIRS):
-                value = value + table[at + t] * points[t]
-            buffer[step * FREQ_BLOCK + n] = value
-
-        copy(step).start()
-
-    @pl.loop(0, 2 * NW // FREQ_BLOCK)
-    def _(step):
-        copy(step).wait()
+    def number(at):
+        return jnp.concatenate([table[pl.ds(at, 1), :]] * (NMO // TILE), axis=1)
+
+    def transform(n):
+        value = number(n * PAIRS) * points[0]
+        for t in range(1, PAIRS):
+            value = value + number(n * PAIRS + t) * points[t]
+        buffer[n] = value
+
+    copies = []
+    for index, (begin, end) in enumerate(FREQ_BLOCKS):
+        if end - begin <= FREQ_STEP:
+            for n in range(begin, end):
+                transform(n)
+        else:
+            pl.loop(begin, end, unroll=FREQ_STEP)(transform)
+        copies.append(pltpu.make_async_copy(buffer.at[begin:end], out.at[begin:end], sems.at[index]))
+        copies[-1].start()
+    for copy in copies:
+        copy.wait()
 
 
 def frequency(*terms):
@@ -266,16 +269,16 @@
     out = pl.pallas_call(
         functools.partial(frequency_kernel, len(terms)),
         out_shape=jax.ShapeDtypeStruct((2 * NW, rows, NMO), jnp.float32),
-        in_specs=[pl.BlockSpec(memory_space=pltpu.SMEM)] + [vmem] * len(terms),
+        in_specs=[vmem] * (1 + len(terms)),
         out_specs=pl.BlockSpec(memory_space=pl.ANY),
         scratch_shapes=[
             pltpu.VMEM((2 * NW, rows, NMO), jnp.float32),
-            pltpu.SemaphoreType.DMA((2 * NW // FREQ_BLOCK,)),
+            pltpu.SemaphoreType.DMA((len(FREQ_BLOCKS),)),
         ],
         compiler_params=pltpu.CompilerParams(vmem_limit_bytes=24 * MIB),
         cost_estimate=pl.CostEstimate(flops=50_000_000, bytes_accessed=17_000_000, transcendentals=0),
         name="frequency",
-    )(jnp.asarray(freq_tables()), *terms)
+    )(*[pltpu.with_memory_space_constraint(x, pltpu.VMEM) for x in (jnp.asarray(freq_tables()), *terms)])
     return out.reshape(2, NW, rows, NMO)
 
 
@@ -314,11 +317,11 @@
     ]
     cast = [value.astype(jnp.bfloat16) for value in sums]
     flip = {k: [(i, i ^ (2 * k)) for i in range(devices)] for k in range(1, 8)}
-    far = [lax.ppermute(cast[k], "trow", flip[k]) for k in (6, 7)]
-    beside = lax.ppermute(jnp.stack([cast[1], cast[3]]), "trow", flip[1])
-    far += [lax.ppermute(cast[k], "trow", flip[k]) for k in (4, 5)]
-    onward = (sums[2] + beside[1].astype(jnp.float32)).astype(jnp.bfloat16)
-    terms = [sums[0], beside[0]] + far + [lax.ppermute(onward, "trow", flip[2])]
+    beside = lax.ppermute(jnp.stack([cast[k] for k in (1, 3, 7)]), "trow", flip[1])
+    straight = {k: lax.ppermute(cast[k], "trow", flip[k]) for k in (4, 5)}
+    own = sums[0] + beside[0].astype(jnp.float32)
+    merged = {k: lax.ppermute((sums[k] + beside[at].astype(jnp.float32)).astype(jnp.bfloat16), "trow", flip[k]) for at, k in ((1, 2), (2, 6))}
+    terms = [own] + [straight[k] for k in (4, 5)] + [merged[k] for k in (2, 6)]
     return frequency(*terms)
 
 

time: 44.5 us -> 42.4 us (0.953)
  starting transfers between devices: 21.4 us -> 19.5 us
  Pallas kernels: 16.1 us -> 14.9 us
  waiting for transfers between devices: 5.22 us -> 6.24 us
    ppermute x6 -> x5, starting transfers between devices: 12.1 us -> 10 us  [the longest x2 4.62 us: local(): lax.ppermute((sums[k] + beside[at].astype(jnp.float32)).astype(jnp.bfloat...]
    ppermute x6 -> x5, waiting for transfers between devices: 4.88 us -> 5.89 us  [the longest x2 3.29 us: local(): lax.ppermute((sums[k] + beside[at].astype(jnp.float32)).astype(jnp.bfloat...]
    pallas_call x1, Pallas kernels: 6.72 us -> 6 us  [frequency(): pl.pallas_call(functools.partial(frequency_kernel, len(terms)), out_shape...]
    pallas_call x1, Pallas kernels: 6.77 us -> 6.29 us  [tiles(): pl.pallas_call(functools.partial(tiles_kernel, count, split), out_shape=(...]
  transfers between devices with their start and end apart: 12 -> 11, of which waited for: 4 -> 4; matrix products, arithmetic and copies ran while one was open for 0% -> 0% of each run, Pallas kernels for 21% -> 21%
where the time goes in v3:
time: 42.4 us; the launch traced here: 42.2 us
  starting transfers between devices  19.5 us (46%)
  Pallas kernels  14.9 us (35%)
  waiting for transfers between devices  6.24 us (15%)
  local copies, waits for them, and re-layouts  1.26 us (3%)
    ppermute x2, starting transfers between devices, local(): nears.append(lax.ppermute(inner, 'trow', partner))  7.31 us
    pallas_call x1, Pallas kernels, tiles(): pl.pallas_call(functools.partial(tiles_kernel, count, split), out_shape=(...  6.29 us
    pallas_call x1, Pallas kernels, frequency(): pl.pallas_call(functools.partial(frequency_kernel, len(terms)), out_shape...  6 us
    ppermute x2, starting transfers between devices, local(): lax.ppermute((sums[k] + beside[at].astype(jnp.float32)).astype(jnp.bfloat...  4.62 us
    ppermute x2, waiting for transfers between devices, local(): lax.ppermute((sums[k] + beside[at].astype(jnp.float32)).astype(jnp.bfloat...  3.29 us
    ppermute x1, starting transfers between devices, local(): lax.ppermute(jnp.stack([cast[k] for k in (1, 3, 7)]), 'trow', flip[1])  2.8 us
    ppermute x1, waiting for transfers between devices, local(): lax.ppermute(jnp.stack([cast[k] for k in (1, 3, 7)]), 'trow', flip[1])  2.6 us
    ppermute x2, starting transfers between devices, local(): straight = {k: lax.ppermute(cast[k], 'trow', flip[k]) for k in (4, 5)}  2.59 us
  transfers between devices with their start and end apart: 11, of which 4 were waited for; matrix products, arithmetic and copies ran while one was open for 0% of the time, Pallas kernels for 21%

profile of v3, /device:TPU:0, one launch (start us, length us, event | category | flops | bytes accessed | tf_op | source)
XLA Modules:
  0.0 42.2 jit_solution(14662743805057054994)
XLA Ops:
  0.0 1.3 %constant_dynamic-slice_fusion.2 = (bf16[512,256]{1,0:T(8,128)(2,1)S(1)}, bf16[512,256]{1,0:T(8,128)(2,1)S(1)}, bf16[512,256]{1,0:T(8,128)(2,1)S(1)}, bf16[512,256]{1,0:T(8,128)(2,1)S(1)}) fusion(bf16[768,512]{1,0:T(8,128)(2,1)} %coefficients.1, s32[]{:T(128)S(6)} %select_n.9, s32[]{:T(128)S(6)} %select_n.8), kind=kLoop, calls=%fused_computation.45 | loop fusion | bytes 2097160 | tf_op jit(solution)/shard_map/dynamic_slice | solution.py:294
  1.3 0.7 %collective-permute-start.4 = (bf16[512,256]{1,0:T(8,128)(2,1)S(1)}, bf16[512,256]{1,0:T(8,128)(2,1)S(1)}, u32[]{:S(2)}, u32[]{:S(2)}) collective-permute-start(bf16[512,256]{1,0:T(8,128)(2,1)S(1)} %get-tuple-element.37), channel_id=1, source_target_pairs={{1,2},{3,4},{5,6},{7,8},{9,10},{11,12},{13,14},{2,1},{4,3},{6,5},{... | collective-permute-start | bytes 786440 | tf_op jit(solution)/shard_map/ppermute | solution.py:295
  1.9 4.3 %collective-permute-start.3 = (bf16[512,256]{1,0:T(8,128)(2,1)S(1)}, bf16[512,256]{1,0:T(8,128)(2,1)S(1)}, u32[]{:S(2)}, u32[]{:S(2)}) collective-permute-start(bf16[512,256]{1,0:T(8,128)(2,1)S(1)} %get-tuple-element.38), channel_id=1, source_target_pairs={{0,1},{1,0},{2,3},{3,2},{4,5},{5,4},{6,7},{7,6},{8,9},{9,8},{10,11... | collective-permute-start | bytes 786440 | tf_op jit(solution)/shard_map/ppermute | solution.py:297
  6.3 0.7 %collective-permute-start.1 = (bf16[512,256]{1,0:T(8,128)(2,1)S(1)}, bf16[512,256]{1,0:T(8,128)(2,1)S(1)}, u32[]{:S(2)}, u32[]{:S(2)}) collective-permute-start(bf16[512,256]{1,0:T(8,128)(2,1)S(1)} %get-tuple-element.35), channel_id=1, source_target_pairs={{1,2},{3,4},{5,6},{7,8},{9,10},{11,12},{13,14},{2,1},{4,3},{6,5},{... | collective-permute-start | bytes 786440 | tf_op jit(solution)/shard_map/ppermute | solution.py:295
  7.0 3.0 %collective-permute-start = (bf16[512,256]{1,0:T(8,128)(2,1)S(1)}, bf16[512,256]{1,0:T(8,128)(2,1)S(1)}, u32[]{:S(2)}, u32[]{:S(2)}) collective-permute-start(bf16[512,256]{1,0:T(8,128)(2,1)S(1)} %get-tuple-element.36), channel_id=1, source_target_pairs={{0,1},{1,0},{2,3},{3,2},{4,5},{5,4},{6,7},{7,6},{8,9},{9,8},{10,11... | collective-permute-start | bytes 786440 | tf_op jit(solution)/shard_map/ppermute | solution.py:297
  9.9 6.3 %tiles.1 = (f32[6,256,512]{2,1,0:T(8,128)S(1)}, bf16[6,9,256,128]{3,2,1,0:T(8,128)(2,1)S(1)}, bf16[512,768]{1,0:T(8,128)(2,1)S(1)}) custom-call(s32[6,9]{1,0:T(8,128)} %mask.1, bf16[6,9,4,128,128]{4,3,2,1,0:T(8,128)(2,1)} %green.1, bf16[6,9,128,128]{3,2,1,0:T(8,128)(2,1)} %integrals.1, bf16[768,512]{1,0:T(8,128)(2,1)} %coefficients.1), custom_call_target="tpu_custom_call" | custom-call | flops 2000000000 | bytes 12000000 | tf_op jit(solution)/shard_map/tiles/pallas_call | solution.py:121
  16.3 1.0 %project.3 = (bf16[256,512]{1,0:T(8,128)(2,1)S(1)}, bf16[768,512]{1,0:T(8,128)(2,1)S(1)}) custom-call(f32[6,256,512]{2,1,0:T(8,128)S(1)} %get-tuple-element.12.refs_0_, bf16[6,9,256,128]{3,2,1,0:T(8,128)(2,1)S(1)} %get-tuple-element.13.refs_1_, bf16[512,256]{1,0:T(8,128)(2,1)S(1)} %collective-permute-done.3.refs_2_, ...), custom_call_target="tpu_custom_call" | custom-call | flops 500000000 | bytes 3000000 | tf_op jit(solution)/shard_map/project/pallas_call | solution.py:190
  17.2 0.3 collective-permute-start.5
  17.5 0.9 %project.2 = (bf16[256,512]{1,0:T(8,128)(2,1)S(1)}, bf16[768,512]{1,0:T(8,128)(2,1)S(1)}) custom-call(f32[6,256,512]{2,1,0:T(8,128)S(1)} %get-tuple-element.12.refs_0_, bf16[6,9,256,128]{3,2,1,0:T(8,128)(2,1)S(1)} %get-tuple-element.13.refs_1_, bf16[512,256]{1,0:T(8,128)(2,1)S(1)} %collective-permute-done.refs_2_, ...), custom_call_target="tpu_custom_call" | custom-call | flops 500000000 | bytes 3000000 | tf_op jit(solution)/shard_map/project/pallas_call | solution.py:190
  18.5 0.5 %collective-permute-start.2 = (bf16[256,512]{1,0:T(8,128)(2,1)S(1)}, bf16[256,512]{1,0:T(8,128)(2,1)S(1)}, u32[]{:S(2)}, u32[]{:S(2)}) collective-permute-start(bf16[256,512]{1,0:T(8,128)(2,1)S(1)} %get-tuple-element.16), channel_id=1, source_target_pairs={{0,1},{1,0},{2,3},{3,2},{4,5},{5,4},{6,7},{7,6},{8,9},{9,8},{10,11... | collective-permute-start | bytes 786440 | tf_op jit(solution)/shard_map/ppermute | solution.py:307
  19.0 0.4 project_own.2
  19.3 0.4 project_own.3
  19.7 0.1 slice_add_fusion
  19.8 0.3 collective-permute-done.2
  20.1 0.1 slice_add_fusion.1
  20.2 2.8 %collective-permute-start.6 = (bf16[3,32,1024]{2,1,0:T(8,128)(2,1)S(1)}, bf16[3,32,1024]{2,1,0:T(8,128)(2,1)S(1)}, u32[]{:S(2)}, u32[]{:S(2)}) collective-permute-start(bf16[3,32,1024]{2,1,0:T(8,128)(2,1)S(1)} %maximum_maximum_fusion), channel_id=1, source_target_pairs={{0,2},{1,3},{2,0},{3,1},{4,6},{5,7},{6,4},{7,5},{8,10},{9,11},{10,... | collective-permute-start | bytes 589832 | tf_op jit(solution)/shard_map/ppermute | solution.py:320
  23.0 2.6 %collective-permute-start.7 = (bf16[32,1024]{1,0:T(8,128)(2,1)S(1)}, bf16[32,1024]{1,0:T(8,128)(2,1)S(1)}, u32[]{:S(2)}, u32[]{:S(2)}) collective-permute-start(bf16[32,1024]{1,0:T(8,128)(2,1)S(1)} %pad_maximum_fusion), channel_id=1, source_target_pairs={{0,8},{1,9},{2,10},{3,11},{4,12},{5,13},{6,14},{7,15},{8,0},{9,1},... | collective-permute-start | bytes 196616 | tf_op jit(solution)/shard_map/ppermute | solution.py:321
  25.6 0.0 collective-permute-start.8
  25.6 2.6 %collective-permute-done.6 = bf16[3,32,1024]{2,1,0:T(8,128)(2,1)S(1)} collective-permute-done((bf16[3,32,1024]{2,1,0:T(8,128)(2,1)S(1)}, bf16[3,32,1024]{2,1,0:T(8,128)(2,1)S(1)}, u32[]{:S(2)}, u32[]{:S(2)}) %collective-permute-start.6) | collective-permute-done | bytes 196640 | tf_op jit(solution)/shard_map/ppermute | solution.py:320
  28.3 3.7 %collective-permute-start.10 = (bf16[32,1024]{1,0:T(8,128)(2,1)S(1)}, bf16[32,1024]{1,0:T(8,128)(2,1)S(1)}, u32[]{:S(2)}, u32[]{:S(2)}) collective-permute-start(bf16[32,1024]{1,0:T(8,128)(2,1)S(1)} %get-tuple-element.39), channel_id=1, source_target_pairs={{0,12},{1,13},{2,14},{3,15},{4,8},{5,9},{6,10},{7,11},{8,4},{9,5},... | collective-permute-start | bytes 196616 | tf_op jit(solution)/shard_map/ppermute | solution.py:323
  31.9 1.0 %collective-permute-start.9 = (bf16[32,1024]{1,0:T(8,128)(2,1)S(1)}, bf16[32,1024]{1,0:T(8,128)(2,1)S(1)}, u32[]{:S(2)}, u32[]{:S(2)}) collective-permute-start(bf16[32,1024]{1,0:T(8,128)(2,1)S(1)} %get-tuple-element.40), channel_id=1, source_target_pairs={{0,4},{1,5},{2,6},{3,7},{4,0},{5,1},{6,2},{7,3},{8,12},{9,13},{10,... | collective-permute-start | bytes 196616 | tf_op jit(solution)/shard_map/ppermute | solution.py:323
  32.9 1.6 %collective-permute-done.10.refs_4_ = bf16[32,1024]{1,0:T(8,128)(2,1)S(1)} collective-permute-done((bf16[32,1024]{1,0:T(8,128)(2,1)S(1)}, bf16[32,1024]{1,0:T(8,128)(2,1)S(1)}, u32[]{:S(2)}, u32[]{:S(2)}) %collective-permute-start.10) | collective-permute-done | bytes 65568 | tf_op jit(solution)/shard_map/ppermute | solution.py:323
  34.5 1.7 %collective-permute-done.9.refs_3_ = bf16[32,1024]{1,0:T(8,128)(2,1)S(1)} collective-permute-done((bf16[32,1024]{1,0:T(8,128)(2,1)S(1)}, bf16[32,1024]{1,0:T(8,128)(2,1)S(1)}, u32[]{:S(2)}, u32[]{:S(2)}) %collective-permute-start.9) | collective-permute-done | bytes 65568 | tf_op jit(solution)/shard_map/ppermute | solution.py:323
  36.2 6.0 %frequency.1 = f32[256,32,512]{2,1,0:T(8,128)} custom-call(f32[512,128]{1,0:T(8,128)S(1)} %copy-done, f32[32,1024]{1,0:T(8,128)S(1)} %get-tuple-element.41.refs_0_, bf16[32,1024]{1,0:T(8,128)(2,1)S(1)} %collective-permute-done.7.refs_1_, bf16[32,1024]{1,0:T(8,128)(2,1)S(1)} %collective-permute-done.8.refs_2_, ...), custom_call_target="tpu_custom_call" | custom-call | flops 50000000 | bytes 17000000 | tf_op jit(solution)/shard_map/frequency/pallas_call | solution.py:269
  (13 shorter events, 0.1 us)
Async XLA Ops:
  1.3 15.0 %collective-permute-start.4 = (bf16[512,256]{1,0:T(8,128)(2,1)S(1)}, bf16[512,256]{1,0:T(8,128)(2,1)S(1)}, u32[]{:S(2)}, u32[]{:S(2)}) collective-permute-start(bf16[512,256]{1,0:T(8,128)(2,1)S(1)} %get-tuple-element.37), channel_id=1, source_target_pairs={{1,2},{3,4},{5,6},{7,8},{9,10},{11,12},{13,14},{2,1},{4,3},{6,5},{... | collective-permute-start | bytes 786440 | tf_op jit(solution)/shard_map/ppermute | solution.py:295
  1.9 14.3 %collective-permute-start.3 = (bf16[512,256]{1,0:T(8,128)(2,1)S(1)}, bf16[512,256]{1,0:T(8,128)(2,1)S(1)}, u32[]{:S(2)}, u32[]{:S(2)}) collective-permute-start(bf16[512,256]{1,0:T(8,128)(2,1)S(1)} %get-tuple-element.38), channel_id=1, source_target_pairs={{0,1},{1,0},{2,3},{3,2},{4,5},{5,4},{6,7},{7,6},{8,9},{9,8},{10,11... | collective-permute-start | bytes 786440 | tf_op jit(solution)/shard_map/ppermute | solution.py:297
  6.3 11.2 %collective-permute-start.1 = (bf16[512,256]{1,0:T(8,128)(2,1)S(1)}, bf16[512,256]{1,0:T(8,128)(2,1)S(1)}, u32[]{:S(2)}, u32[]{:S(2)}) collective-permute-start(bf16[512,256]{1,0:T(8,128)(2,1)S(1)} %get-tuple-element.35), channel_id=1, source_target_pairs={{1,2},{3,4},{5,6},{7,8},{9,10},{11,12},{13,14},{2,1},{4,3},{6,5},{... | collective-permute-start | bytes 786440 | tf_op jit(solution)/shard_map/ppermute | solution.py:295
  7.0 10.6 %collective-permute-start = (bf16[512,256]{1,0:T(8,128)(2,1)S(1)}, bf16[512,256]{1,0:T(8,128)(2,1)S(1)}, u32[]{:S(2)}, u32[]{:S(2)}) collective-permute-start(bf16[512,256]{1,0:T(8,128)(2,1)S(1)} %get-tuple-element.36), channel_id=1, source_target_pairs={{0,1},{1,0},{2,3},{3,2},{4,5},{5,4},{6,7},{7,6},{8,9},{9,8},{10,11... | collective-permute-start | bytes 786440 | tf_op jit(solution)/shard_map/ppermute | solution.py:297
  17.2 2.5 %collective-permute-start.5 = (bf16[256,512]{1,0:T(8,128)(2,1)S(1)}, bf16[256,512]{1,0:T(8,128)(2,1)S(1)}, u32[]{:S(2)}, u32[]{:S(2)}) collective-permute-start(bf16[256,512]{1,0:T(8,128)(2,1)S(1)} %get-tuple-element.18), channel_id=1, source_target_pairs={{0,1},{1,0},{2,3},{3,2},{4,5},{5,4},{6,7},{7,6},{8,9},{9,8},{10,11... | collective-permute-start | bytes 786440 | tf_op jit(solution)/shard_map/ppermute | solution.py:307
  18.5 1.6 %collective-permute-start.2 = (bf16[256,512]{1,0:T(8,128)(2,1)S(1)}, bf16[256,512]{1,0:T(8,128)(2,1)S(1)}, u32[]{:S(2)}, u32[]{:S(2)}) collective-permute-start(bf16[256,512]{1,0:T(8,128)(2,1)S(1)} %get-tuple-element.16), channel_id=1, source_target_pairs={{0,1},{1,0},{2,3},{3,2},{4,5},{5,4},{6,7},{7,6},{8,9},{9,8},{10,11... | collective-permute-start | bytes 786440 | tf_op jit(solution)/shard_map/ppermute | solution.py:307
  19.0 17.2 %copy-start = (f32[512,128]{1,0:T(8,128)S(1)}, f32[512,128]{1,0:T(8,128)}, u32[]{:S(2)}) copy-start(f32[512,128]{1,0:T(8,128)} %constant.17.clone.table) | copy-start | bytes 786436
  20.2 8.0 %collective-permute-start.6 = (bf16[3,32,1024]{2,1,0:T(8,128)(2,1)S(1)}, bf16[3,32,1024]{2,1,0:T(8,128)(2,1)S(1)}, u32[]{:S(2)}, u32[]{:S(2)}) collective-permute-start(bf16[3,32,1024]{2,1,0:T(8,128)(2,1)S(1)} %maximum_maximum_fusion), channel_id=1, source_target_pairs={{0,2},{1,3},{2,0},{3,1},{4,6},{5,7},{6,4},{7,5},{8,10},{9,11},{10,... | collective-permute-start | bytes 589832 | tf_op jit(solution)/shard_map/ppermute | solution.py:320
  23.0 9.9 %collective-permute-start.7 = (bf16[32,1024]{1,0:T(8,128)(2,1)S(1)}, bf16[32,1024]{1,0:T(8,128)(2,1)S(1)}, u32[]{:S(2)}, u32[]{:S(2)}) collective-permute-start(bf16[32,1024]{1,0:T(8,128)(2,1)S(1)} %pad_maximum_fusion), channel_id=1, source_target_pairs={{0,8},{1,9},{2,10},{3,11},{4,12},{5,13},{6,14},{7,15},{8,0},{9,1},... | collective-permute-start | bytes 196616 | tf_op jit(solution)/shard_map/ppermute | solution.py:321
  25.6 7.3 %collective-permute-start.8 = (bf16[32,1024]{1,0:T(8,128)(2,1)S(1)}, bf16[32,1024]{1,0:T(8,128)(2,1)S(1)}, u32[]{:S(2)}, u32[]{:S(2)}) collective-permute-start(bf16[32,1024]{1,0:T(8,128)(2,1)S(1)} %pad_maximum_fusion.1), channel_id=1, source_target_pairs={{0,10},{1,11},{2,8},{3,9},{4,14},{5,15},{6,12},{7,13},{8,2},{9,3},... | collective-permute-start | bytes 196616 | tf_op jit(solution)/shard_map/ppermute | solution.py:321
  28.3 6.3 %collective-permute-start.10 = (bf16[32,1024]{1,0:T(8,128)(2,1)S(1)}, bf16[32,1024]{1,0:T(8,128)(2,1)S(1)}, u32[]{:S(2)}, u32[]{:S(2)}) collective-permute-start(bf16[32,1024]{1,0:T(8,128)(2,1)S(1)} %get-tuple-element.39), channel_id=1, source_target_pairs={{0,12},{1,13},{2,14},{3,15},{4,8},{5,9},{6,10},{7,11},{8,4},{9,5},... | collective-permute-start | bytes 196616 | tf_op jit(solution)/shard_map/ppermute | solution.py:323
  31.9 4.3 %collective-permute-start.9 = (bf16[32,1024]{1,0:T(8,128)(2,1)S(1)}, bf16[32,1024]{1,0:T(8,128)(2,1)S(1)}, u32[]{:S(2)}, u32[]{:S(2)}) collective-permute-start(bf16[32,1024]{1,0:T(8,128)(2,1)S(1)} %get-tuple-element.40), channel_id=1, source_target_pairs={{0,4},{1,5},{2,6},{3,7},{4,0},{5,1},{6,2},{7,3},{8,12},{9,13},{10,... | collective-permute-start | bytes 196616 | tf_op jit(solution)/shard_map/ppermute | solution.py:323

commit v4 on v3

--- a/solution.py
+++ b/solution.py
@@ -317,11 +317,18 @@
     ]
     cast = [value.astype(jnp.bfloat16) for value in sums]
     flip = {k: [(i, i ^ (2 * k)) for i in range(devices)] for k in range(1, 8)}
-    beside = lax.ppermute(jnp.stack([cast[k] for k in (1, 3, 7)]), "trow", flip[1])
-    straight = {k: lax.ppermute(cast[k], "trow", flip[k]) for k in (4, 5)}
-    own = sums[0] + beside[0].astype(jnp.float32)
-    merged = {k: lax.ppermute((sums[k] + beside[at].astype(jnp.float32)).astype(jnp.bfloat16), "trow", flip[k]) for at, k in ((1, 2), (2, 6))}
-    terms = [own] + [straight[k] for k in (4, 5)] + [merged[k] for k in (2, 6)]
+    parts = []
+    for keep, other in both:
+        blocks = [
+            keep[k * size : (k + 1) * size] + other[k * size : (k + 1) * size].astype(jnp.float32) for k in (1, 3, 5)
+        ]
+        parts.append(lax.ppermute(jnp.stack(blocks).astype(jnp.bfloat16), "trow", flip[1]))
+    beside = jnp.concatenate(lax.optimization_barrier(parts), axis=2).astype(jnp.float32)
+    straight = [lax.ppermute(cast[k], "trow", flip[k]) for k in (6, 7)]
+    merged = [
+        lax.ppermute((sums[k] + beside[at]).astype(jnp.bfloat16), "trow", flip[k]) for at, k in ((1, 2), (2, 4))
+    ]
+    terms = [sums[0] + beside[0], *straight, *merged]
     return frequency(*terms)
 
 

time: 42.4 us -> 41.7 us (0.983)
  waiting for transfers between devices: 6.24 us -> 5.3 us
  Pallas kernels: 14.9 us -> 15.4 us
    ppermute x5 -> x6, waiting for transfers between devices: 5.89 us -> 5.29 us  [the longest x2 2.1 us: local(): straight = [lax.ppermute(cast[k], 'trow', flip[k]) for k in (6, 7)]]
    pallas_call x1, Pallas kernels: 6.29 us -> 6.77 us  [tiles(): pl.pallas_call(functools.partial(tiles_kernel, count, split), out_shape=(...]
    ppermute x5 -> x6, starting transfers between devices: 10 us -> 9.89 us  [the longest x2 3.98 us: local(): lax.ppermute(jnp.stack(blocks).astype(jnp.bfloat16), 'trow', flip[1])]
  transfers between devices with their start and end apart: 11 -> 12, of which waited for: 4 -> 4; matrix products, arithmetic and copies ran while one was open for 0% -> 1% of each run, Pallas kernels for 21% -> 23%
where the time goes in v4:
time: 41.7 us; the launch traced here: 41.5 us
  starting transfers between devices  19.1 us (46%)
  Pallas kernels  15.4 us (37%)
  waiting for transfers between devices  5.3 us (13%)
  local copies, waits for them, and re-layouts  1.26 us (3%)
    ppermute x2, starting transfers between devices, local(): nears.append(lax.ppermute(inner, 'trow', partner))  7.31 us
    pallas_call x1, Pallas kernels, tiles(): pl.pallas_call(functools.partial(tiles_kernel, count, split), out_shape=(...  6.77 us
    pallas_call x1, Pallas kernels, frequency(): pl.pallas_call(functools.partial(frequency_kernel, len(terms)), out_shape...  6 us
    ppermute x2, starting transfers between devices, local(): lax.ppermute(jnp.stack(blocks).astype(jnp.bfloat16), 'trow', flip[1])  3.98 us
    ppermute x2, starting transfers between devices, local(): straight = [lax.ppermute(cast[k], 'trow', flip[k]) for k in (6, 7)]  3.57 us
    ppermute x2, starting transfers between devices, local(): lax.ppermute((sums[k] + beside[at]).astype(jnp.bfloat16), 'trow', flip[k])  2.34 us
    ppermute x2, waiting for transfers between devices, local(): straight = [lax.ppermute(cast[k], 'trow', flip[k]) for k in (6, 7)]  2.1 us
    pallas_call x2, Pallas kernels, project(): pl.pallas_call(functools.partial(project_kernel, count, split, piece), ou...  1.91 us
  transfers between devices with their start and end apart: 12, of which 4 were waited for; matrix products, arithmetic and copies ran while one was open for 1% of the time, Pallas kernels for 23%

profile of v4, /device:TPU:0, one launch (start us, length us, event | category | flops | bytes accessed | tf_op | source)
XLA Modules:
  0.0 41.5 jit_solution(5461696990970272118)
XLA Ops:
  0.0 1.3 %constant_dynamic-slice_fusion = (bf16[512,256]{1,0:T(8,128)(2,1)S(1)}, bf16[512,256]{1,0:T(8,128)(2,1)S(1)}, bf16[512,256]{1,0:T(8,128)(2,1)S(1)}, bf16[512,256]{1,0:T(8,128)(2,1)S(1)}) fusion(bf16[768,512]{1,0:T(8,128)(2,1)} %coefficients.1, s32[]{:T(128)S(6)} %select_n.9, s32[]{:T(128)S(6)} %select_n.8), kind=kLoop, calls=%fused_computation.45 | loop fusion | bytes 2097160 | tf_op jit(solution)/shard_map/dynamic_slice | solution.py:294
  1.3 0.7 %collective-permute-start.4 = (bf16[512,256]{1,0:T(8,128)(2,1)S(1)}, bf16[512,256]{1,0:T(8,128)(2,1)S(1)}, u32[]{:S(2)}, u32[]{:S(2)}) collective-permute-start(bf16[512,256]{1,0:T(8,128)(2,1)S(1)} %get-tuple-element.39), channel_id=1, source_target_pairs={{1,2},{3,4},{5,6},{7,8},{9,10},{11,12},{13,14},{2,1},{4,3},{6,5},{... | collective-permute-start | bytes 786440 | tf_op jit(solution)/shard_map/ppermute | solution.py:295
  1.9 4.3 %collective-permute-start.3 = (bf16[512,256]{1,0:T(8,128)(2,1)S(1)}, bf16[512,256]{1,0:T(8,128)(2,1)S(1)}, u32[]{:S(2)}, u32[]{:S(2)}) collective-permute-start(bf16[512,256]{1,0:T(8,128)(2,1)S(1)} %get-tuple-element.42), channel_id=1, source_target_pairs={{0,1},{1,0},{2,3},{3,2},{4,5},{5,4},{6,7},{7,6},{8,9},{9,8},{10,11... | collective-permute-start | bytes 786440 | tf_op jit(solution)/shard_map/ppermute | solution.py:297
  6.3 0.7 %collective-permute-start.1 = (bf16[512,256]{1,0:T(8,128)(2,1)S(1)}, bf16[512,256]{1,0:T(8,128)(2,1)S(1)}, u32[]{:S(2)}, u32[]{:S(2)}) collective-permute-start(bf16[512,256]{1,0:T(8,128)(2,1)S(1)} %get-tuple-element.40), channel_id=1, source_target_pairs={{1,2},{3,4},{5,6},{7,8},{9,10},{11,12},{13,14},{2,1},{4,3},{6,5},{... | collective-permute-start | bytes 786440 | tf_op jit(solution)/shard_map/ppermute | solution.py:295
  7.0 3.0 %collective-permute-start = (bf16[512,256]{1,0:T(8,128)(2,1)S(1)}, bf16[512,256]{1,0:T(8,128)(2,1)S(1)}, u32[]{:S(2)}, u32[]{:S(2)}) collective-permute-start(bf16[512,256]{1,0:T(8,128)(2,1)S(1)} %get-tuple-element.41), channel_id=1, source_target_pairs={{0,1},{1,0},{2,3},{3,2},{4,5},{5,4},{6,7},{7,6},{8,9},{9,8},{10,11... | collective-permute-start | bytes 786440 | tf_op jit(solution)/shard_map/ppermute | solution.py:297
  9.9 6.8 %tiles.1 = (f32[6,256,512]{2,1,0:T(8,128)S(1)}, bf16[6,9,256,128]{3,2,1,0:T(8,128)(2,1)S(1)}, bf16[512,768]{1,0:T(8,128)(2,1)S(1)}) custom-call(s32[6,9]{1,0:T(8,128)} %mask.1, bf16[6,9,4,128,128]{4,3,2,1,0:T(8,128)(2,1)} %green.1, bf16[6,9,128,128]{3,2,1,0:T(8,128)(2,1)} %integrals.1, bf16[768,512]{1,0:T(8,128)(2,1)} %coefficients.1), custom_call_target="tpu_custom_call" | custom-call | flops 2000000000 | bytes 12000000 | tf_op jit(solution)/shard_map/tiles/pallas_call | solution.py:121
  16.7 1.0 %project.3 = (bf16[256,512]{1,0:T(8,128)(2,1)S(1)}, bf16[768,512]{1,0:T(8,128)(2,1)S(1)}) custom-call(f32[6,256,512]{2,1,0:T(8,128)S(1)} %get-tuple-element.14.refs_0_, bf16[6,9,256,128]{3,2,1,0:T(8,128)(2,1)S(1)} %get-tuple-element.15.refs_1_, bf16[512,256]{1,0:T(8,128)(2,1)S(1)} %collective-permute-done.3.refs_2_, ...), custom_call_target="tpu_custom_call" | custom-call | flops 500000000 | bytes 3000000 | tf_op jit(solution)/shard_map/project/pallas_call | solution.py:190
  17.7 0.1 collective-permute-start.5
  17.8 1.0 %project.2 = (bf16[256,512]{1,0:T(8,128)(2,1)S(1)}, bf16[768,512]{1,0:T(8,128)(2,1)S(1)}) custom-call(f32[6,256,512]{2,1,0:T(8,128)S(1)} %get-tuple-element.14.refs_0_, bf16[6,9,256,128]{3,2,1,0:T(8,128)(2,1)S(1)} %get-tuple-element.15.refs_1_, bf16[512,256]{1,0:T(8,128)(2,1)S(1)} %collective-permute-done.refs_2_, ...), custom_call_target="tpu_custom_call" | custom-call | flops 500000000 | bytes 3000000 | tf_op jit(solution)/shard_map/project/pallas_call | solution.py:190
  18.7 0.5 %collective-permute-start.2 = (bf16[256,512]{1,0:T(8,128)(2,1)S(1)}, bf16[256,512]{1,0:T(8,128)(2,1)S(1)}, u32[]{:S(2)}, u32[]{:S(2)}) collective-permute-start(bf16[256,512]{1,0:T(8,128)(2,1)S(1)} %get-tuple-element.18), channel_id=1, source_target_pairs={{0,1},{1,0},{2,3},{3,2},{4,5},{5,4},{6,7},{7,6},{8,9},{9,8},{10,11... | collective-permute-start | bytes 786440 | tf_op jit(solution)/shard_map/ppermute | solution.py:307
  19.3 0.4 project_own.2
  19.7 0.4 project_own.3
  20.0 0.1 slice_add_fusion
  20.1 2.1 %collective-permute-start.7 = (bf16[3,32,512]{2,1,0:T(8,128)(2,1)S(1)}, bf16[3,32,512]{2,1,0:T(8,128)(2,1)S(1)}, u32[]{:S(2)}, u32[]{:S(2)}) collective-permute-start(bf16[3,32,512]{2,1,0:T(8,128)(2,1)S(1)} %pad_maximum_fusion.1), channel_id=1, source_target_pairs={{0,2},{1,3},{2,0},{3,1},{4,6},{5,7},{6,4},{7,5},{8,10},{9,11},{10,... | collective-permute-start | bytes 294920 | tf_op jit(solution)/shard_map/ppermute | solution.py:325
  22.4 2.3 %collective-permute-start.8 = (bf16[32,1024]{1,0:T(8,128)(2,1)S(1)}, bf16[32,1024]{1,0:T(8,128)(2,1)S(1)}, u32[]{:S(2)}, u32[]{:S(2)}) collective-permute-start(bf16[32,1024]{1,0:T(8,128)(2,1)S(1)} %pad_maximum_fusion.2), channel_id=1, source_target_pairs={{0,12},{1,13},{2,14},{3,15},{4,8},{5,9},{6,10},{7,11},{8,4},{9,5},... | collective-permute-start | bytes 196616 | tf_op jit(solution)/shard_map/ppermute | solution.py:327
  24.7 1.8 %collective-permute-start.6 = (bf16[3,32,512]{2,1,0:T(8,128)(2,1)S(1)}, bf16[3,32,512]{2,1,0:T(8,128)(2,1)S(1)}, u32[]{:S(2)}, u32[]{:S(2)}) collective-permute-start(bf16[3,32,512]{2,1,0:T(8,128)(2,1)S(1)} %pad_maximum_fusion), channel_id=1, source_target_pairs={{0,2},{1,3},{2,0},{3,1},{4,6},{5,7},{6,4},{7,5},{8,10},{9,11},{10,... | collective-permute-start | bytes 294920 | tf_op jit(solution)/shard_map/ppermute | solution.py:325
  26.5 1.3 %collective-permute-start.9 = (bf16[32,1024]{1,0:T(8,128)(2,1)S(1)}, bf16[32,1024]{1,0:T(8,128)(2,1)S(1)}, u32[]{:S(2)}, u32[]{:S(2)}) collective-permute-start(bf16[32,1024]{1,0:T(8,128)(2,1)S(1)} %pad_maximum_fusion.3), channel_id=1, source_target_pairs={{0,14},{1,15},{2,12},{3,13},{4,10},{5,11},{6,8},{7,9},{8,6},{9,7},... | collective-permute-start | bytes 196616 | tf_op jit(solution)/shard_map/ppermute | solution.py:327
  27.8 1.7 %collective-permute-done.6 = bf16[3,32,512]{2,1,0:T(8,128)(2,1)S(1)} collective-permute-done((bf16[3,32,512]{2,1,0:T(8,128)(2,1)S(1)}, bf16[3,32,512]{2,1,0:T(8,128)(2,1)S(1)}, u32[]{:S(2)}, u32[]{:S(2)}) %collective-permute-start.6) | collective-permute-done | bytes 98336 | tf_op jit(solution)/shard_map/ppermute | solution.py:325
  29.6 1.3 %collective-permute-start.11 = (bf16[32,1024]{1,0:T(8,128)(2,1)S(1)}, bf16[32,1024]{1,0:T(8,128)(2,1)S(1)}, u32[]{:S(2)}, u32[]{:S(2)}) collective-permute-start(bf16[32,1024]{1,0:T(8,128)(2,1)S(1)} %get-tuple-element.43), channel_id=1, source_target_pairs={{0,8},{1,9},{2,10},{3,11},{4,12},{5,13},{6,14},{7,15},{8,0},{9,1},... | collective-permute-start | bytes 196616 | tf_op jit(solution)/shard_map/ppermute | solution.py:329
  30.9 1.0 %collective-permute-start.10 = (bf16[32,1024]{1,0:T(8,128)(2,1)S(1)}, bf16[32,1024]{1,0:T(8,128)(2,1)S(1)}, u32[]{:S(2)}, u32[]{:S(2)}) collective-permute-start(bf16[32,1024]{1,0:T(8,128)(2,1)S(1)} %get-tuple-element.44), channel_id=1, source_target_pairs={{0,4},{1,5},{2,6},{3,7},{4,0},{5,1},{6,2},{7,3},{8,12},{9,13},{10,... | collective-permute-start | bytes 196616 | tf_op jit(solution)/shard_map/ppermute | solution.py:329
  32.0 2.1 %collective-permute-done.9.refs_2_ = bf16[32,1024]{1,0:T(8,128)(2,1)S(1)} collective-permute-done((bf16[32,1024]{1,0:T(8,128)(2,1)S(1)}, bf16[32,1024]{1,0:T(8,128)(2,1)S(1)}, u32[]{:S(2)}, u32[]{:S(2)}) %collective-permute-start.9) | collective-permute-done | bytes 65568 | tf_op jit(solution)/shard_map/ppermute | solution.py:327
  34.0 0.8 %collective-permute-done.11.refs_4_ = bf16[32,1024]{1,0:T(8,128)(2,1)S(1)} collective-permute-done((bf16[32,1024]{1,0:T(8,128)(2,1)S(1)}, bf16[32,1024]{1,0:T(8,128)(2,1)S(1)}, u32[]{:S(2)}, u32[]{:S(2)}) %collective-permute-start.11) | collective-permute-done | bytes 65568 | tf_op jit(solution)/shard_map/ppermute | solution.py:329
  34.9 0.7 %collective-permute-done.10.refs_3_ = bf16[32,1024]{1,0:T(8,128)(2,1)S(1)} collective-permute-done((bf16[32,1024]{1,0:T(8,128)(2,1)S(1)}, bf16[32,1024]{1,0:T(8,128)(2,1)S(1)}, u32[]{:S(2)}, u32[]{:S(2)}) %collective-permute-start.10) | collective-permute-done | bytes 65568 | tf_op jit(solution)/shard_map/ppermute | solution.py:329
  35.5 6.0 %frequency.1 = f32[256,32,512]{2,1,0:T(8,128)} custom-call(f32[512,128]{1,0:T(8,128)S(1)} %copy-done, f32[32,1024]{1,0:T(8,128)S(1)} %get-tuple-element.45.refs_0_, bf16[32,1024]{1,0:T(8,128)(2,1)S(1)} %collective-permute-done.8.refs_1_, bf16[32,1024]{1,0:T(8,128)(2,1)S(1)} %collective-permute-done.9.refs_2_, ...), custom_call_target="tpu_custom_call" | custom-call | flops 50000000 | bytes 17000000 | tf_op jit(solution)/shard_map/frequency/pallas_call | solution.py:269
  (17 shorter events, 0.2 us)
Async XLA Ops:
  1.3 15.4 %collective-permute-start.4 = (bf16[512,256]{1,0:T(8,128)(2,1)S(1)}, bf16[512,256]{1,0:T(8,128)(2,1)S(1)}, u32[]{:S(2)}, u32[]{:S(2)}) collective-permute-start(bf16[512,256]{1,0:T(8,128)(2,1)S(1)} %get-tuple-element.39), channel_id=1, source_target_pairs={{1,2},{3,4},{5,6},{7,8},{9,10},{11,12},{13,14},{2,1},{4,3},{6,5},{... | collective-permute-start | bytes 786440 | tf_op jit(solution)/shard_map/ppermute | solution.py:295
  1.9 14.8 %collective-permute-start.3 = (bf16[512,256]{1,0:T(8,128)(2,1)S(1)}, bf16[512,256]{1,0:T(8,128)(2,1)S(1)}, u32[]{:S(2)}, u32[]{:S(2)}) collective-permute-start(bf16[512,256]{1,0:T(8,128)(2,1)S(1)} %get-tuple-element.42), channel_id=1, source_target_pairs={{0,1},{1,0},{2,3},{3,2},{4,5},{5,4},{6,7},{7,6},{8,9},{9,8},{10,11... | collective-permute-start | bytes 786440 | tf_op jit(solution)/shard_map/ppermute | solution.py:297
  6.3 11.5 %collective-permute-start.1 = (bf16[512,256]{1,0:T(8,128)(2,1)S(1)}, bf16[512,256]{1,0:T(8,128)(2,1)S(1)}, u32[]{:S(2)}, u32[]{:S(2)}) collective-permute-start(bf16[512,256]{1,0:T(8,128)(2,1)S(1)} %get-tuple-element.40), channel_id=1, source_target_pairs={{1,2},{3,4},{5,6},{7,8},{9,10},{11,12},{13,14},{2,1},{4,3},{6,5},{... | collective-permute-start | bytes 786440 | tf_op jit(solution)/shard_map/ppermute | solution.py:295
  7.0 10.8 %collective-permute-start = (bf16[512,256]{1,0:T(8,128)(2,1)S(1)}, bf16[512,256]{1,0:T(8,128)(2,1)S(1)}, u32[]{:S(2)}, u32[]{:S(2)}) collective-permute-start(bf16[512,256]{1,0:T(8,128)(2,1)S(1)} %get-tuple-element.41), channel_id=1, source_target_pairs={{0,1},{1,0},{2,3},{3,2},{4,5},{5,4},{6,7},{7,6},{8,9},{9,8},{10,11... | collective-permute-start | bytes 786440 | tf_op jit(solution)/shard_map/ppermute | solution.py:297
  17.7 2.3 %collective-permute-start.5 = (bf16[256,512]{1,0:T(8,128)(2,1)S(1)}, bf16[256,512]{1,0:T(8,128)(2,1)S(1)}, u32[]{:S(2)}, u32[]{:S(2)}) collective-permute-start(bf16[256,512]{1,0:T(8,128)(2,1)S(1)} %get-tuple-element.20), channel_id=1, source_target_pairs={{0,1},{1,0},{2,3},{3,2},{4,5},{5,4},{6,7},{7,6},{8,9},{9,8},{10,11... | collective-permute-start | bytes 786440 | tf_op jit(solution)/shard_map/ppermute | solution.py:307
  18.7 3.5 %collective-permute-start.2 = (bf16[256,512]{1,0:T(8,128)(2,1)S(1)}, bf16[256,512]{1,0:T(8,128)(2,1)S(1)}, u32[]{:S(2)}, u32[]{:S(2)}) collective-permute-start(bf16[256,512]{1,0:T(8,128)(2,1)S(1)} %get-tuple-element.18), channel_id=1, source_target_pairs={{0,1},{1,0},{2,3},{3,2},{4,5},{5,4},{6,7},{7,6},{8,9},{9,8},{10,11... | collective-permute-start | bytes 786440 | tf_op jit(solution)/shard_map/ppermute | solution.py:307
  19.6 15.9 %copy-start = (f32[512,128]{1,0:T(8,128)S(1)}, f32[512,128]{1,0:T(8,128)}, u32[]{:S(2)}) copy-start(f32[512,128]{1,0:T(8,128)} %constant.17.clone.table) | copy-start | bytes 786436
  20.1 7.7 %collective-permute-start.7 = (bf16[3,32,512]{2,1,0:T(8,128)(2,1)S(1)}, bf16[3,32,512]{2,1,0:T(8,128)(2,1)S(1)}, u32[]{:S(2)}, u32[]{:S(2)}) collective-permute-start(bf16[3,32,512]{2,1,0:T(8,128)(2,1)S(1)} %pad_maximum_fusion.1), channel_id=1, source_target_pairs={{0,2},{1,3},{2,0},{3,1},{4,6},{5,7},{6,4},{7,5},{8,10},{9,11},{10,... | collective-permute-start | bytes 294920 | tf_op jit(solution)/shard_map/ppermute | solution.py:325
  22.4 9.6 %collective-permute-start.8 = (bf16[32,1024]{1,0:T(8,128)(2,1)S(1)}, bf16[32,1024]{1,0:T(8,128)(2,1)S(1)}, u32[]{:S(2)}, u32[]{:S(2)}) collective-permute-start(bf16[32,1024]{1,0:T(8,128)(2,1)S(1)} %pad_maximum_fusion.2), channel_id=1, source_target_pairs={{0,12},{1,13},{2,14},{3,15},{4,8},{5,9},{6,10},{7,11},{8,4},{9,5},... | collective-permute-start | bytes 196616 | tf_op jit(solution)/shard_map/ppermute | solution.py:327
  24.7 4.8 %collective-permute-start.6 = (bf16[3,32,512]{2,1,0:T(8,128)(2,1)S(1)}, bf16[3,32,512]{2,1,0:T(8,128)(2,1)S(1)}, u32[]{:S(2)}, u32[]{:S(2)}) collective-permute-start(bf16[3,32,512]{2,1,0:T(8,128)(2,1)S(1)} %pad_maximum_fusion), channel_id=1, source_target_pairs={{0,2},{1,3},{2,0},{3,1},{4,6},{5,7},{6,4},{7,5},{8,10},{9,11},{10,... | collective-permute-start | bytes 294920 | tf_op jit(solution)/shard_map/ppermute | solution.py:325
  26.5 7.5 %collective-permute-start.9 = (bf16[32,1024]{1,0:T(8,128)(2,1)S(1)}, bf16[32,1024]{1,0:T(8,128)(2,1)S(1)}, u32[]{:S(2)}, u32[]{:S(2)}) collective-permute-start(bf16[32,1024]{1,0:T(8,128)(2,1)S(1)} %pad_maximum_fusion.3), channel_id=1, source_target_pairs={{0,14},{1,15},{2,12},{3,13},{4,10},{5,11},{6,8},{7,9},{8,6},{9,7},... | collective-permute-start | bytes 196616 | tf_op jit(solution)/shard_map/ppermute | solution.py:327
  29.6 5.3 %collective-permute-start.11 = (bf16[32,1024]{1,0:T(8,128)(2,1)S(1)}, bf16[32,1024]{1,0:T(8,128)(2,1)S(1)}, u32[]{:S(2)}, u32[]{:S(2)}) collective-permute-start(bf16[32,1024]{1,0:T(8,128)(2,1)S(1)} %get-tuple-element.43), channel_id=1, source_target_pairs={{0,8},{1,9},{2,10},{3,11},{4,12},{5,13},{6,14},{7,15},{8,0},{9,1},... | collective-permute-start | bytes 196616 | tf_op jit(solution)/shard_map/ppermute | solution.py:329
  30.9 4.6 %collective-permute-start.10 = (bf16[32,1024]{1,0:T(8,128)(2,1)S(1)}, bf16[32,1024]{1,0:T(8,128)(2,1)S(1)}, u32[]{:S(2)}, u32[]{:S(2)}) collective-permute-start(bf16[32,1024]{1,0:T(8,128)(2,1)S(1)} %get-tuple-element.44), channel_id=1, source_target_pairs={{0,4},{1,5},{2,6},{3,7},{4,0},{5,1},{6,2},{7,3},{8,12},{9,13},{10,... | collective-permute-start | bytes 196616 | tf_op jit(solution)/shard_map/ppermute | solution.py:329

commit v5 on v4

--- a/solution.py
+++ b/solution.py
@@ -151,15 +151,47 @@
     return contract(sigma, row, slots, block, row if left else row + slots[0] - BAND - count)
 
 
-def project_kernel(count, split, piece, *refs):
-    part, sigma, near, halo, transposed, out, half = refs
+def prepare_kernel(count, piece, part, sigma, near, total):
     first = lax.rem(lax.axis_index("trow"), 2) == 0
     columns = slice(piece * COLUMNS, (piece + 1) * COLUMNS)
 
+    def add(left):
+        for row in range(count):
+            value = part[row, :, columns]
+            term = outer(count, row, left, sigma, near)
+            total[row] = value if term is None else value + term
+
+    @pl.when(first)
+    def _():
+        add(False)
+
+    @pl.when(jnp.logical_not(first))
+    def _():
+        add(True)
+
+
+def prepare(part, sigma, near, piece):
+    count = part.shape[0]
+    vmem = pl.BlockSpec(memory_space=pltpu.VMEM)
+    return pl.pallas_call(
+        functools.partial(prepare_kernel, count, piece),
+        out_shape=pltpu.VMEM((count, PAIRS * TILE, COLUMNS), jnp.float32),
+        in_specs=[vmem] * 3,
+        out_specs=vmem,
+        compiler_params=pltpu.CompilerParams(vmem_limit_bytes=16 * MIB),
+        cost_estimate=pl.CostEstimate(flops=200_000_000, bytes_accessed=2_000_000, transcendentals=0),
+        name="prepare",
+    )(*[pltpu.with_memory_space_constraint(x, pltpu.VMEM) for x in (part, sigma, near)])
+
+
+def project_kernel(count, split, *refs):
+    part, sigma, *near, halo, transposed, out, half = refs
+    first = lax.rem(lax.axis_index("trow"), 2) == 0
+
     def finish(far_left):
         for row in range(count):
-            value = part[row, :, columns]
-            for left, block in ((not far_left, near), (far_left, halo)):
+            value = part[row, :, :COLUMNS]
+            for left, block in [(not far_left, ref) for ref in near] + [(far_left, halo)]:
                 term = outer(count, row, left, sigma, block)
                 value = value if term is None else value + term
             for t in range(PAIRS):
@@ -181,14 +213,17 @@
 
 def project(part, sigma, near, halo, transposed, split, piece):
     count = part.shape[0]
-    operands = (part, sigma, near, halo, transposed)
+    if piece:
+        operands = (prepare(part, sigma, near, piece), sigma, halo, transposed)
+    else:
+        operands = (part, sigma, near, halo, transposed)
     vmem = pl.BlockSpec(memory_space=pltpu.VMEM)
     if split:
         out_shape = pltpu.VMEM((NMO // 2, PAIRS * COLUMNS), jnp.bfloat16)
     else:
         out_shape = jax.ShapeDtypeStruct((NMO, PAIRS * COLUMNS), jnp.float32)
     return pl.pallas_call(
-        functools.partial(project_kernel, count, split, piece),
+        functools.partial(project_kernel, count, split),
         out_shape=(out_shape, pltpu.VMEM((count * TILE, PAIRS * COLUMNS), jnp.bfloat16)),
         in_specs=[vmem] * len(operands),
         out_specs=(vmem, vmem),

time: 41.7 us -> 41.5 us (level)
    pallas_call x1, Pallas kernels: 6.77 us -> 6.29 us  [tiles(): pl.pallas_call(functools.partial(tiles_kernel, count, split), out_shape=(...]
    pallas_call x2 -> x3, Pallas kernels: 1.91 us -> 2.11 us  [the longest x2 1.71 us: project(): pl.pallas_call(functools.partial(project_kernel, count, split), out_shape...]
  transfers between devices with their start and end apart: 12 -> 12, of which waited for: 4 -> 4; matrix products, arithmetic and copies ran while one was open for 1% -> 1% of each run, Pallas kernels for 23% -> 22%
where the time goes in v5:
time: 41.5 us; the launch traced here: 41.3 us
  starting transfers between devices  19.2 us (46%)
  Pallas kernels  15.1 us (36%)
  waiting for transfers between devices  5.32 us (13%)
  local copies, waits for them, and re-layouts  1.26 us (3%)
    ppermute x2, starting transfers between devices, local(): nears.append(lax.ppermute(inner, 'trow', partner))  7.31 us
    pallas_call x1, Pallas kernels, tiles(): pl.pallas_call(functools.partial(tiles_kernel, count, split), out_shape=(...  6.29 us
    pallas_call x1, Pallas kernels, frequency(): pl.pallas_call(functools.partial(frequency_kernel, len(terms)), out_shape...  6 us
    ppermute x2, starting transfers between devices, local(): lax.ppermute(jnp.stack(blocks).astype(jnp.bfloat16), 'trow', flip[1])  4.03 us
    ppermute x2, starting transfers between devices, local(): straight = [lax.ppermute(cast[k], 'trow', flip[k]) for k in (6, 7)]  3.57 us
    ppermute x2, starting transfers between devices, local(): lax.ppermute((sums[k] + beside[at]).astype(jnp.bfloat16), 'trow', flip[k])  2.33 us
    ppermute x2, waiting for transfers between devices, local(): straight = [lax.ppermute(cast[k], 'trow', flip[k]) for k in (6, 7)]  2.13 us
    ppermute x2, waiting for transfers between devices, local(): lax.ppermute(jnp.stack(blocks).astype(jnp.bfloat16), 'trow', flip[1])  1.71 us
  transfers between devices with their start and end apart: 12, of which 4 were waited for; matrix products, arithmetic and copies ran while one was open for 1% of the time, Pallas kernels for 22%

profile of v5, /device:TPU:0, one launch (start us, length us, event | category | flops | bytes accessed | tf_op | source)
XLA Modules:
  0.0 41.3 jit_solution(6124650081242700086)
XLA Ops:
  0.0 1.3 %constant_dynamic-slice_fusion = (bf16[512,256]{1,0:T(8,128)(2,1)S(1)}, bf16[512,256]{1,0:T(8,128)(2,1)S(1)}, bf16[512,256]{1,0:T(8,128)(2,1)S(1)}, bf16[512,256]{1,0:T(8,128)(2,1)S(1)}) fusion(bf16[768,512]{1,0:T(8,128)(2,1)} %coefficients.1, s32[]{:T(128)S(6)} %select_n.9, s32[]{:T(128)S(6)} %select_n.8), kind=kLoop, calls=%fused_computation.45 | loop fusion | bytes 2097160 | tf_op jit(solution)/shard_map/dynamic_slice | solution.py:329
  1.3 0.7 %collective-permute-start.1 = (bf16[512,256]{1,0:T(8,128)(2,1)S(1)}, bf16[512,256]{1,0:T(8,128)(2,1)S(1)}, u32[]{:S(2)}, u32[]{:S(2)}) collective-permute-start(bf16[512,256]{1,0:T(8,128)(2,1)S(1)} %get-tuple-element.40), channel_id=1, source_target_pairs={{1,2},{3,4},{5,6},{7,8},{9,10},{11,12},{13,14},{2,1},{4,3},{6,5},{... | collective-permute-start | bytes 786440 | tf_op jit(solution)/shard_map/ppermute | solution.py:330
  1.9 4.3 %collective-permute-start = (bf16[512,256]{1,0:T(8,128)(2,1)S(1)}, bf16[512,256]{1,0:T(8,128)(2,1)S(1)}, u32[]{:S(2)}, u32[]{:S(2)}) collective-permute-start(bf16[512,256]{1,0:T(8,128)(2,1)S(1)} %get-tuple-element.41), channel_id=1, source_target_pairs={{0,1},{1,0},{2,3},{3,2},{4,5},{5,4},{6,7},{7,6},{8,9},{9,8},{10,11... | collective-permute-start | bytes 786440 | tf_op jit(solution)/shard_map/ppermute | solution.py:332
  6.3 0.7 %collective-permute-start.4 = (bf16[512,256]{1,0:T(8,128)(2,1)S(1)}, bf16[512,256]{1,0:T(8,128)(2,1)S(1)}, u32[]{:S(2)}, u32[]{:S(2)}) collective-permute-start(bf16[512,256]{1,0:T(8,128)(2,1)S(1)} %get-tuple-element.39), channel_id=1, source_target_pairs={{1,2},{3,4},{5,6},{7,8},{9,10},{11,12},{13,14},{2,1},{4,3},{6,5},{... | collective-permute-start | bytes 786440 | tf_op jit(solution)/shard_map/ppermute | solution.py:330
  7.0 3.0 %collective-permute-start.3 = (bf16[512,256]{1,0:T(8,128)(2,1)S(1)}, bf16[512,256]{1,0:T(8,128)(2,1)S(1)}, u32[]{:S(2)}, u32[]{:S(2)}) collective-permute-start(bf16[512,256]{1,0:T(8,128)(2,1)S(1)} %get-tuple-element.42), channel_id=1, source_target_pairs={{0,1},{1,0},{2,3},{3,2},{4,5},{5,4},{6,7},{7,6},{8,9},{9,8},{10,11... | collective-permute-start | bytes 786440 | tf_op jit(solution)/shard_map/ppermute | solution.py:332
  9.9 6.3 %tiles.1 = (f32[6,256,512]{2,1,0:T(8,128)S(1)}, bf16[6,9,256,128]{3,2,1,0:T(8,128)(2,1)S(1)}, bf16[512,768]{1,0:T(8,128)(2,1)S(1)}) custom-call(s32[6,9]{1,0:T(8,128)} %mask.1, bf16[6,9,4,128,128]{4,3,2,1,0:T(8,128)(2,1)} %green.1, bf16[6,9,128,128]{3,2,1,0:T(8,128)(2,1)} %integrals.1, bf16[768,512]{1,0:T(8,128)(2,1)} %coefficients.1), custom_call_target="tpu_custom_call" | custom-call | flops 2000000000 | bytes 12000000 | tf_op jit(solution)/shard_map/tiles/pallas_call | solution.py:121
  16.3 1.0 %project.2 = (bf16[256,512]{1,0:T(8,128)(2,1)S(1)}, bf16[768,512]{1,0:T(8,128)(2,1)S(1)}) custom-call(f32[6,256,512]{2,1,0:T(8,128)S(1)} %get-tuple-element.14.refs_0_.part, bf16[6,9,256,128]{3,2,1,0:T(8,128)(2,1)S(1)} %get-tuple-element.15.refs_1_.sigma, bf16[512,256]{1,0:T(8,128)(2,1)S(1)} %collective-permute-done.refs_2_, ...), custom_call_target="tpu_custom_call" | custom-call | flops 500000000 | bytes 3000000 | tf_op jit(solution)/shard_map/project/pallas_call | solution.py:225
  17.3 0.4 prepare.1.refs_0_
  17.7 0.8 %project.3 = (bf16[256,512]{1,0:T(8,128)(2,1)S(1)}, bf16[768,512]{1,0:T(8,128)(2,1)S(1)}) custom-call(f32[6,256,256]{2,1,0:T(8,128)S(1)} %prepare.1.refs_0_, bf16[6,9,256,128]{3,2,1,0:T(8,128)(2,1)S(1)} %get-tuple-element.15.refs_1_.sigma, bf16[512,256]{1,0:T(8,128)(2,1)S(1)} %collective-permute-done.4.refs_2_, ...), custom_call_target="tpu_custom_call" | custom-call | flops 500000000 | bytes 3000000 | tf_op jit(solution)/shard_map/project/pallas_call | solution.py:225
  18.5 0.5 %collective-permute-start.5 = (bf16[256,512]{1,0:T(8,128)(2,1)S(1)}, bf16[256,512]{1,0:T(8,128)(2,1)S(1)}, u32[]{:S(2)}, u32[]{:S(2)}) collective-permute-start(bf16[256,512]{1,0:T(8,128)(2,1)S(1)} %get-tuple-element.20), channel_id=1, source_target_pairs={{0,1},{1,0},{2,3},{3,2},{4,5},{5,4},{6,7},{7,6},{8,9},{9,8},{10,11... | collective-permute-start | bytes 786440 | tf_op jit(solution)/shard_map/ppermute | solution.py:342
  19.0 0.4 project_own.3
  19.4 0.4 project_own.2
  19.8 0.1 slice_add_fusion.1
  19.9 2.2 %collective-permute-start.6 = (bf16[3,32,512]{2,1,0:T(8,128)(2,1)S(1)}, bf16[3,32,512]{2,1,0:T(8,128)(2,1)S(1)}, u32[]{:S(2)}, u32[]{:S(2)}) collective-permute-start(bf16[3,32,512]{2,1,0:T(8,128)(2,1)S(1)} %pad_maximum_fusion), channel_id=1, source_target_pairs={{0,2},{1,3},{2,0},{3,1},{4,6},{5,7},{6,4},{7,5},{8,10},{9,11},{10,... | collective-permute-start | bytes 294920 | tf_op jit(solution)/shard_map/ppermute | solution.py:360
  22.2 2.3 %collective-permute-start.8 = (bf16[32,1024]{1,0:T(8,128)(2,1)S(1)}, bf16[32,1024]{1,0:T(8,128)(2,1)S(1)}, u32[]{:S(2)}, u32[]{:S(2)}) collective-permute-start(bf16[32,1024]{1,0:T(8,128)(2,1)S(1)} %pad_maximum_fusion.2), channel_id=1, source_target_pairs={{0,12},{1,13},{2,14},{3,15},{4,8},{5,9},{6,10},{7,11},{8,4},{9,5},... | collective-permute-start | bytes 196616 | tf_op jit(solution)/shard_map/ppermute | solution.py:362
  24.5 1.8 %collective-permute-start.7 = (bf16[3,32,512]{2,1,0:T(8,128)(2,1)S(1)}, bf16[3,32,512]{2,1,0:T(8,128)(2,1)S(1)}, u32[]{:S(2)}, u32[]{:S(2)}) collective-permute-start(bf16[3,32,512]{2,1,0:T(8,128)(2,1)S(1)} %pad_maximum_fusion.1), channel_id=1, source_target_pairs={{0,2},{1,3},{2,0},{3,1},{4,6},{5,7},{6,4},{7,5},{8,10},{9,11},{10,... | collective-permute-start | bytes 294920 | tf_op jit(solution)/shard_map/ppermute | solution.py:360
  26.3 1.3 %collective-permute-start.9 = (bf16[32,1024]{1,0:T(8,128)(2,1)S(1)}, bf16[32,1024]{1,0:T(8,128)(2,1)S(1)}, u32[]{:S(2)}, u32[]{:S(2)}) collective-permute-start(bf16[32,1024]{1,0:T(8,128)(2,1)S(1)} %pad_maximum_fusion.3), channel_id=1, source_target_pairs={{0,14},{1,15},{2,12},{3,13},{4,10},{5,11},{6,8},{7,9},{8,6},{9,7},... | collective-permute-start | bytes 196616 | tf_op jit(solution)/shard_map/ppermute | solution.py:362
  27.6 1.7 %collective-permute-done.7 = bf16[3,32,512]{2,1,0:T(8,128)(2,1)S(1)} collective-permute-done((bf16[3,32,512]{2,1,0:T(8,128)(2,1)S(1)}, bf16[3,32,512]{2,1,0:T(8,128)(2,1)S(1)}, u32[]{:S(2)}, u32[]{:S(2)}) %collective-permute-start.7) | collective-permute-done | bytes 98336 | tf_op jit(solution)/shard_map/ppermute | solution.py:360
  29.4 1.3 %collective-permute-start.11 = (bf16[32,1024]{1,0:T(8,128)(2,1)S(1)}, bf16[32,1024]{1,0:T(8,128)(2,1)S(1)}, u32[]{:S(2)}, u32[]{:S(2)}) collective-permute-start(bf16[32,1024]{1,0:T(8,128)(2,1)S(1)} %get-tuple-element.43), channel_id=1, source_target_pairs={{0,8},{1,9},{2,10},{3,11},{4,12},{5,13},{6,14},{7,15},{8,0},{9,1},... | collective-permute-start | bytes 196616 | tf_op jit(solution)/shard_map/ppermute | solution.py:364
  30.7 1.0 %collective-permute-start.10 = (bf16[32,1024]{1,0:T(8,128)(2,1)S(1)}, bf16[32,1024]{1,0:T(8,128)(2,1)S(1)}, u32[]{:S(2)}, u32[]{:S(2)}) collective-permute-start(bf16[32,1024]{1,0:T(8,128)(2,1)S(1)} %get-tuple-element.44), channel_id=1, source_target_pairs={{0,4},{1,5},{2,6},{3,7},{4,0},{5,1},{6,2},{7,3},{8,12},{9,13},{10,... | collective-permute-start | bytes 196616 | tf_op jit(solution)/shard_map/ppermute | solution.py:364
  31.7 2.1 %collective-permute-done.9.refs_2_ = bf16[32,1024]{1,0:T(8,128)(2,1)S(1)} collective-permute-done((bf16[32,1024]{1,0:T(8,128)(2,1)S(1)}, bf16[32,1024]{1,0:T(8,128)(2,1)S(1)}, u32[]{:S(2)}, u32[]{:S(2)}) %collective-permute-start.9) | collective-permute-done | bytes 65568 | tf_op jit(solution)/shard_map/ppermute | solution.py:362
  33.9 0.8 %collective-permute-done.11.refs_4_ = bf16[32,1024]{1,0:T(8,128)(2,1)S(1)} collective-permute-done((bf16[32,1024]{1,0:T(8,128)(2,1)S(1)}, bf16[32,1024]{1,0:T(8,128)(2,1)S(1)}, u32[]{:S(2)}, u32[]{:S(2)}) %collective-permute-start.11) | collective-permute-done | bytes 65568 | tf_op jit(solution)/shard_map/ppermute | solution.py:364
  34.7 0.7 %collective-permute-done.10.refs_3_ = bf16[32,1024]{1,0:T(8,128)(2,1)S(1)} collective-permute-done((bf16[32,1024]{1,0:T(8,128)(2,1)S(1)}, bf16[32,1024]{1,0:T(8,128)(2,1)S(1)}, u32[]{:S(2)}, u32[]{:S(2)}) %collective-permute-start.10) | collective-permute-done | bytes 65568 | tf_op jit(solution)/shard_map/ppermute | solution.py:364
  35.3 6.0 %frequency.1 = f32[256,32,512]{2,1,0:T(8,128)} custom-call(f32[512,128]{1,0:T(8,128)S(1)} %copy-done, f32[32,1024]{1,0:T(8,128)S(1)} %get-tuple-element.45.refs_0_, bf16[32,1024]{1,0:T(8,128)(2,1)S(1)} %collective-permute-done.8.refs_1_, bf16[32,1024]{1,0:T(8,128)(2,1)S(1)} %collective-permute-done.9.refs_2_, ...), custom_call_target="tpu_custom_call" | custom-call | flops 50000000 | bytes 17000000 | tf_op jit(solution)/shard_map/frequency/pallas_call | solution.py:304
  (18 shorter events, 0.3 us)
Async XLA Ops:
  1.3 15.0 %collective-permute-start.1 = (bf16[512,256]{1,0:T(8,128)(2,1)S(1)}, bf16[512,256]{1,0:T(8,128)(2,1)S(1)}, u32[]{:S(2)}, u32[]{:S(2)}) collective-permute-start(bf16[512,256]{1,0:T(8,128)(2,1)S(1)} %get-tuple-element.40), channel_id=1, source_target_pairs={{1,2},{3,4},{5,6},{7,8},{9,10},{11,12},{13,14},{2,1},{4,3},{6,5},{... | collective-permute-start | bytes 786440 | tf_op jit(solution)/shard_map/ppermute | solution.py:330
  1.9 14.3 %collective-permute-start = (bf16[512,256]{1,0:T(8,128)(2,1)S(1)}, bf16[512,256]{1,0:T(8,128)(2,1)S(1)}, u32[]{:S(2)}, u32[]{:S(2)}) collective-permute-start(bf16[512,256]{1,0:T(8,128)(2,1)S(1)} %get-tuple-element.41), channel_id=1, source_target_pairs={{0,1},{1,0},{2,3},{3,2},{4,5},{5,4},{6,7},{7,6},{8,9},{9,8},{10,11... | collective-permute-start | bytes 786440 | tf_op jit(solution)/shard_map/ppermute | solution.py:332
  6.3 11.4 %collective-permute-start.4 = (bf16[512,256]{1,0:T(8,128)(2,1)S(1)}, bf16[512,256]{1,0:T(8,128)(2,1)S(1)}, u32[]{:S(2)}, u32[]{:S(2)}) collective-permute-start(bf16[512,256]{1,0:T(8,128)(2,1)S(1)} %get-tuple-element.39), channel_id=1, source_target_pairs={{1,2},{3,4},{5,6},{7,8},{9,10},{11,12},{13,14},{2,1},{4,3},{6,5},{... | collective-permute-start | bytes 786440 | tf_op jit(solution)/shard_map/ppermute | solution.py:330
  7.0 10.3 %collective-permute-start.3 = (bf16[512,256]{1,0:T(8,128)(2,1)S(1)}, bf16[512,256]{1,0:T(8,128)(2,1)S(1)}, u32[]{:S(2)}, u32[]{:S(2)}) collective-permute-start(bf16[512,256]{1,0:T(8,128)(2,1)S(1)} %get-tuple-element.42), channel_id=1, source_target_pairs={{0,1},{1,0},{2,3},{3,2},{4,5},{5,4},{6,7},{7,6},{8,9},{9,8},{10,11... | collective-permute-start | bytes 786440 | tf_op jit(solution)/shard_map/ppermute | solution.py:332
  17.2 2.6 %collective-permute-start.2 = (bf16[256,512]{1,0:T(8,128)(2,1)S(1)}, bf16[256,512]{1,0:T(8,128)(2,1)S(1)}, u32[]{:S(2)}, u32[]{:S(2)}) collective-permute-start(bf16[256,512]{1,0:T(8,128)(2,1)S(1)} %get-tuple-element.18), channel_id=1, source_target_pairs={{0,1},{1,0},{2,3},{3,2},{4,5},{5,4},{6,7},{7,6},{8,9},{9,8},{10,11... | collective-permute-start | bytes 786440 | tf_op jit(solution)/shard_map/ppermute | solution.py:342
  18.5 3.6 %collective-permute-start.5 = (bf16[256,512]{1,0:T(8,128)(2,1)S(1)}, bf16[256,512]{1,0:T(8,128)(2,1)S(1)}, u32[]{:S(2)}, u32[]{:S(2)}) collective-permute-start(bf16[256,512]{1,0:T(8,128)(2,1)S(1)} %get-tuple-element.20), channel_id=1, source_target_pairs={{0,1},{1,0},{2,3},{3,2},{4,5},{5,4},{6,7},{7,6},{8,9},{9,8},{10,11... | collective-permute-start | bytes 786440 | tf_op jit(solution)/shard_map/ppermute | solution.py:342
  19.4 15.9 %copy-start = (f32[512,128]{1,0:T(8,128)S(1)}, f32[512,128]{1,0:T(8,128)}, u32[]{:S(2)}) copy-start(f32[512,128]{1,0:T(8,128)} %constant.17.clone.table) | copy-start | bytes 786436
  19.9 7.7 %collective-permute-start.6 = (bf16[3,32,512]{2,1,0:T(8,128)(2,1)S(1)}, bf16[3,32,512]{2,1,0:T(8,128)(2,1)S(1)}, u32[]{:S(2)}, u32[]{:S(2)}) collective-permute-start(bf16[3,32,512]{2,1,0:T(8,128)(2,1)S(1)} %pad_maximum_fusion), channel_id=1, source_target_pairs={{0,2},{1,3},{2,0},{3,1},{4,6},{5,7},{6,4},{7,5},{8,10},{9,11},{10,... | collective-permute-start | bytes 294920 | tf_op jit(solution)/shard_map/ppermute | solution.py:360
  22.2 9.6 %collective-permute-start.8 = (bf16[32,1024]{1,0:T(8,128)(2,1)S(1)}, bf16[32,1024]{1,0:T(8,128)(2,1)S(1)}, u32[]{:S(2)}, u32[]{:S(2)}) collective-permute-start(bf16[32,1024]{1,0:T(8,128)(2,1)S(1)} %pad_maximum_fusion.2), channel_id=1, source_target_pairs={{0,12},{1,13},{2,14},{3,15},{4,8},{5,9},{6,10},{7,11},{8,4},{9,5},... | collective-permute-start | bytes 196616 | tf_op jit(solution)/shard_map/ppermute | solution.py:362
  24.5 4.8 %collective-permute-start.7 = (bf16[3,32,512]{2,1,0:T(8,128)(2,1)S(1)}, bf16[3,32,512]{2,1,0:T(8,128)(2,1)S(1)}, u32[]{:S(2)}, u32[]{:S(2)}) collective-permute-start(bf16[3,32,512]{2,1,0:T(8,128)(2,1)S(1)} %pad_maximum_fusion.1), channel_id=1, source_target_pairs={{0,2},{1,3},{2,0},{3,1},{4,6},{5,7},{6,4},{7,5},{8,10},{9,11},{10,... | collective-permute-start | bytes 294920 | tf_op jit(solution)/shard_map/ppermute | solution.py:360
  26.3 7.5 %collective-permute-start.9 = (bf16[32,1024]{1,0:T(8,128)(2,1)S(1)}, bf16[32,1024]{1,0:T(8,128)(2,1)S(1)}, u32[]{:S(2)}, u32[]{:S(2)}) collective-permute-start(bf16[32,1024]{1,0:T(8,128)(2,1)S(1)} %pad_maximum_fusion.3), channel_id=1, source_target_pairs={{0,14},{1,15},{2,12},{3,13},{4,10},{5,11},{6,8},{7,9},{8,6},{9,7},... | collective-permute-start | bytes 196616 | tf_op jit(solution)/shard_map/ppermute | solution.py:362
  29.4 5.3 %collective-permute-start.11 = (bf16[32,1024]{1,0:T(8,128)(2,1)S(1)}, bf16[32,1024]{1,0:T(8,128)(2,1)S(1)}, u32[]{:S(2)}, u32[]{:S(2)}) collective-permute-start(bf16[32,1024]{1,0:T(8,128)(2,1)S(1)} %get-tuple-element.43), channel_id=1, source_target_pairs={{0,8},{1,9},{2,10},{3,11},{4,12},{5,13},{6,14},{7,15},{8,0},{9,1},... | collective-permute-start | bytes 196616 | tf_op jit(solution)/shard_map/ppermute | solution.py:364
  30.7 4.6 %collective-permute-start.10 = (bf16[32,1024]{1,0:T(8,128)(2,1)S(1)}, bf16[32,1024]{1,0:T(8,128)(2,1)S(1)}, u32[]{:S(2)}, u32[]{:S(2)}) collective-permute-start(bf16[32,1024]{1,0:T(8,128)(2,1)S(1)} %get-tuple-element.44), channel_id=1, source_target_pairs={{0,4},{1,5},{2,6},{3,7},{4,0},{5,1},{6,2},{7,3},{8,12},{9,13},{10,... | collective-permute-start | bytes 196616 | tf_op jit(solution)/shard_map/ppermute | solution.py:364

commit v6 on v5

--- a/solution.py
+++ b/solution.py
@@ -18,7 +18,7 @@
 FREQ_STEP = 4
 FREQ_EDGES = [0, 2, 4, 8, 16, *range(32, 2 * NW + 1, 32)]
 FREQ_BLOCKS = list(zip(FREQ_EDGES, FREQ_EDGES[1:]))
-GROUP = 4
+GROUP = 6
 CHUNKS = 2
 COLUMNS = NMO // CHUNKS
 MIB = 1 << 20

time: 41.5 us -> 41.5 us (level)
  transfers between devices with their start and end apart: 12 -> 12, of which waited for: 4 -> 4; matrix products, arithmetic and copies ran while one was open for 1% -> 1% of each run, Pallas kernels for 22% -> 21%
where the time goes in v6:
time: 41.5 us; the launch traced here: 41.3 us
  starting transfers between devices  19.5 us (47%)
  Pallas kernels  14.9 us (36%)
  waiting for transfers between devices  5.32 us (13%)
  local copies, waits for them, and re-layouts  1.26 us (3%)
    ppermute x2, starting transfers between devices, local(): nears.append(lax.ppermute(inner, 'trow', partner))  7.31 us
    pallas_call x1, Pallas kernels, tiles(): pl.pallas_call(functools.partial(tiles_kernel, count, split), out_shape=(...  6.04 us
    pallas_call x1, Pallas kernels, frequency(): pl.pallas_call(functools.partial(frequency_kernel, len(terms)), out_shape...  6 us
    ppermute x2, starting transfers between devices, local(): lax.ppermute(jnp.stack(blocks).astype(jnp.bfloat16), 'trow', flip[1])  4.28 us
    ppermute x2, starting transfers between devices, local(): straight = [lax.ppermute(cast[k], 'trow', flip[k]) for k in (6, 7)]  3.57 us
    ppermute x2, starting transfers between devices, local(): lax.ppermute((sums[k] + beside[at]).astype(jnp.bfloat16), 'trow', flip[k])  2.33 us
    ppermute x2, waiting for transfers between devices, local(): straight = [lax.ppermute(cast[k], 'trow', flip[k]) for k in (6, 7)]  2.13 us
    ppermute x2, waiting for transfers between devices, local(): lax.ppermute(jnp.stack(blocks).astype(jnp.bfloat16), 'trow', flip[1])  1.71 us
  transfers between devices with their start and end apart: 12, of which 4 were waited for; matrix products, arithmetic and copies ran while one was open for 1% of the time, Pallas kernels for 21%

profile of v6, /device:TPU:0, one launch (start us, length us, event | category | flops | bytes accessed | tf_op | source)
XLA Modules:
  0.0 41.3 jit_solution(6097018296858180281)
XLA Ops:
  0.0 1.3 %constant_dynamic-slice_fusion = (bf16[512,256]{1,0:T(8,128)(2,1)S(1)}, bf16[512,256]{1,0:T(8,128)(2,1)S(1)}, bf16[512,256]{1,0:T(8,128)(2,1)S(1)}, bf16[512,256]{1,0:T(8,128)(2,1)S(1)}) fusion(bf16[768,512]{1,0:T(8,128)(2,1)} %coefficients.1, s32[]{:T(128)S(6)} %select_n.9, s32[]{:T(128)S(6)} %select_n.8), kind=kLoop, calls=%fused_computation.45 | loop fusion | bytes 2097160 | tf_op jit(solution)/shard_map/dynamic_slice | solution.py:329
  1.3 0.7 %collective-permute-start.1 = (bf16[512,256]{1,0:T(8,128)(2,1)S(1)}, bf16[512,256]{1,0:T(8,128)(2,1)S(1)}, u32[]{:S(2)}, u32[]{:S(2)}) collective-permute-start(bf16[512,256]{1,0:T(8,128)(2,1)S(1)} %get-tuple-element.40), channel_id=1, source_target_pairs={{1,2},{3,4},{5,6},{7,8},{9,10},{11,12},{13,14},{2,1},{4,3},{6,5},{... | collective-permute-start | bytes 786440 | tf_op jit(solution)/shard_map/ppermute | solution.py:330
  1.9 4.3 %collective-permute-start = (bf16[512,256]{1,0:T(8,128)(2,1)S(1)}, bf16[512,256]{1,0:T(8,128)(2,1)S(1)}, u32[]{:S(2)}, u32[]{:S(2)}) collective-permute-start(bf16[512,256]{1,0:T(8,128)(2,1)S(1)} %get-tuple-element.41), channel_id=1, source_target_pairs={{0,1},{1,0},{2,3},{3,2},{4,5},{5,4},{6,7},{7,6},{8,9},{9,8},{10,11... | collective-permute-start | bytes 786440 | tf_op jit(solution)/shard_map/ppermute | solution.py:332
  6.3 0.7 %collective-permute-start.4 = (bf16[512,256]{1,0:T(8,128)(2,1)S(1)}, bf16[512,256]{1,0:T(8,128)(2,1)S(1)}, u32[]{:S(2)}, u32[]{:S(2)}) collective-permute-start(bf16[512,256]{1,0:T(8,128)(2,1)S(1)} %get-tuple-element.39), channel_id=1, source_target_pairs={{1,2},{3,4},{5,6},{7,8},{9,10},{11,12},{13,14},{2,1},{4,3},{6,5},{... | collective-permute-start | bytes 786440 | tf_op jit(solution)/shard_map/ppermute | solution.py:330
  7.0 3.0 %collective-permute-start.3 = (bf16[512,256]{1,0:T(8,128)(2,1)S(1)}, bf16[512,256]{1,0:T(8,128)(2,1)S(1)}, u32[]{:S(2)}, u32[]{:S(2)}) collective-permute-start(bf16[512,256]{1,0:T(8,128)(2,1)S(1)} %get-tuple-element.42), channel_id=1, source_target_pairs={{0,1},{1,0},{2,3},{3,2},{4,5},{5,4},{6,7},{7,6},{8,9},{9,8},{10,11... | collective-permute-start | bytes 786440 | tf_op jit(solution)/shard_map/ppermute | solution.py:332
  9.9 6.0 %tiles.1 = (f32[6,256,512]{2,1,0:T(8,128)S(1)}, bf16[6,9,256,128]{3,2,1,0:T(8,128)(2,1)S(1)}, bf16[512,768]{1,0:T(8,128)(2,1)S(1)}) custom-call(s32[6,9]{1,0:T(8,128)} %mask.1, bf16[6,9,4,128,128]{4,3,2,1,0:T(8,128)(2,1)} %green.1, bf16[6,9,128,128]{3,2,1,0:T(8,128)(2,1)} %integrals.1, bf16[768,512]{1,0:T(8,128)(2,1)} %coefficients.1), custom_call_target="tpu_custom_call" | custom-call | flops 2000000000 | bytes 12000000 | tf_op jit(solution)/shard_map/tiles/pallas_call | solution.py:121
  16.0 1.0 %project.2 = (bf16[256,512]{1,0:T(8,128)(2,1)S(1)}, bf16[768,512]{1,0:T(8,128)(2,1)S(1)}) custom-call(f32[6,256,512]{2,1,0:T(8,128)S(1)} %get-tuple-element.14.refs_0_.part, bf16[6,9,256,128]{3,2,1,0:T(8,128)(2,1)S(1)} %get-tuple-element.15.refs_1_.sigma, bf16[512,256]{1,0:T(8,128)(2,1)S(1)} %collective-permute-done.refs_2_, ...), custom_call_target="tpu_custom_call" | custom-call | flops 500000000 | bytes 3000000 | tf_op jit(solution)/shard_map/project/pallas_call | solution.py:225
  17.0 0.4 prepare.1.refs_0_
  17.5 0.7 %project.3 = (bf16[256,512]{1,0:T(8,128)(2,1)S(1)}, bf16[768,512]{1,0:T(8,128)(2,1)S(1)}) custom-call(f32[6,256,256]{2,1,0:T(8,128)S(1)} %prepare.1.refs_0_, bf16[6,9,256,128]{3,2,1,0:T(8,128)(2,1)S(1)} %get-tuple-element.15.refs_1_.sigma, bf16[512,256]{1,0:T(8,128)(2,1)S(1)} %collective-permute-done.4.refs_2_, ...), custom_call_target="tpu_custom_call" | custom-call | flops 500000000 | bytes 3000000 | tf_op jit(solution)/shard_map/project/pallas_call | solution.py:225
  18.2 0.6 %collective-permute-start.5 = (bf16[256,512]{1,0:T(8,128)(2,1)S(1)}, bf16[256,512]{1,0:T(8,128)(2,1)S(1)}, u32[]{:S(2)}, u32[]{:S(2)}) collective-permute-start(bf16[256,512]{1,0:T(8,128)(2,1)S(1)} %get-tuple-element.20), channel_id=1, source_target_pairs={{0,1},{1,0},{2,3},{3,2},{4,5},{5,4},{6,7},{7,6},{8,9},{9,8},{10,11... | collective-permute-start | bytes 786440 | tf_op jit(solution)/shard_map/ppermute | solution.py:342
  18.8 0.4 project_own.3
  19.2 0.4 project_own.2
  19.5 0.1 slice_add_fusion.1
  19.6 2.4 %collective-permute-start.6 = (bf16[3,32,512]{2,1,0:T(8,128)(2,1)S(1)}, bf16[3,32,512]{2,1,0:T(8,128)(2,1)S(1)}, u32[]{:S(2)}, u32[]{:S(2)}) collective-permute-start(bf16[3,32,512]{2,1,0:T(8,128)(2,1)S(1)} %pad_maximum_fusion), channel_id=1, source_target_pairs={{0,2},{1,3},{2,0},{3,1},{4,6},{5,7},{6,4},{7,5},{8,10},{9,11},{10,... | collective-permute-start | bytes 294920 | tf_op jit(solution)/shard_map/ppermute | solution.py:360
  22.2 2.3 %collective-permute-start.8 = (bf16[32,1024]{1,0:T(8,128)(2,1)S(1)}, bf16[32,1024]{1,0:T(8,128)(2,1)S(1)}, u32[]{:S(2)}, u32[]{:S(2)}) collective-permute-start(bf16[32,1024]{1,0:T(8,128)(2,1)S(1)} %pad_maximum_fusion.2), channel_id=1, source_target_pairs={{0,12},{1,13},{2,14},{3,15},{4,8},{5,9},{6,10},{7,11},{8,4},{9,5},... | collective-permute-start | bytes 196616 | tf_op jit(solution)/shard_map/ppermute | solution.py:362
  24.5 1.8 %collective-permute-start.7 = (bf16[3,32,512]{2,1,0:T(8,128)(2,1)S(1)}, bf16[3,32,512]{2,1,0:T(8,128)(2,1)S(1)}, u32[]{:S(2)}, u32[]{:S(2)}) collective-permute-start(bf16[3,32,512]{2,1,0:T(8,128)(2,1)S(1)} %pad_maximum_fusion.1), channel_id=1, source_target_pairs={{0,2},{1,3},{2,0},{3,1},{4,6},{5,7},{6,4},{7,5},{8,10},{9,11},{10,... | collective-permute-start | bytes 294920 | tf_op jit(solution)/shard_map/ppermute | solution.py:360
  26.3 1.3 %collective-permute-start.9 = (bf16[32,1024]{1,0:T(8,128)(2,1)S(1)}, bf16[32,1024]{1,0:T(8,128)(2,1)S(1)}, u32[]{:S(2)}, u32[]{:S(2)}) collective-permute-start(bf16[32,1024]{1,0:T(8,128)(2,1)S(1)} %pad_maximum_fusion.3), channel_id=1, source_target_pairs={{0,14},{1,15},{2,12},{3,13},{4,10},{5,11},{6,8},{7,9},{8,6},{9,7},... | collective-permute-start | bytes 196616 | tf_op jit(solution)/shard_map/ppermute | solution.py:362
  27.6 1.7 %collective-permute-done.7 = bf16[3,32,512]{2,1,0:T(8,128)(2,1)S(1)} collective-permute-done((bf16[3,32,512]{2,1,0:T(8,128)(2,1)S(1)}, bf16[3,32,512]{2,1,0:T(8,128)(2,1)S(1)}, u32[]{:S(2)}, u32[]{:S(2)}) %collective-permute-start.7) | collective-permute-done | bytes 98336 | tf_op jit(solution)/shard_map/ppermute | solution.py:360
  29.4 1.3 %collective-permute-start.11 = (bf16[32,1024]{1,0:T(8,128)(2,1)S(1)}, bf16[32,1024]{1,0:T(8,128)(2,1)S(1)}, u32[]{:S(2)}, u32[]{:S(2)}) collective-permute-start(bf16[32,1024]{1,0:T(8,128)(2,1)S(1)} %get-tuple-element.43), channel_id=1, source_target_pairs={{0,8},{1,9},{2,10},{3,11},{4,12},{5,13},{6,14},{7,15},{8,0},{9,1},... | collective-permute-start | bytes 196616 | tf_op jit(solution)/shard_map/ppermute | solution.py:364
  30.7 1.0 %collective-permute-start.10 = (bf16[32,1024]{1,0:T(8,128)(2,1)S(1)}, bf16[32,1024]{1,0:T(8,128)(2,1)S(1)}, u32[]{:S(2)}, u32[]{:S(2)}) collective-permute-start(bf16[32,1024]{1,0:T(8,128)(2,1)S(1)} %get-tuple-element.44), channel_id=1, source_target_pairs={{0,4},{1,5},{2,6},{3,7},{4,0},{5,1},{6,2},{7,3},{8,12},{9,13},{10,... | collective-permute-start | bytes 196616 | tf_op jit(solution)/shard_map/ppermute | solution.py:364
  31.7 2.1 %collective-permute-done.9.refs_2_ = bf16[32,1024]{1,0:T(8,128)(2,1)S(1)} collective-permute-done((bf16[32,1024]{1,0:T(8,128)(2,1)S(1)}, bf16[32,1024]{1,0:T(8,128)(2,1)S(1)}, u32[]{:S(2)}, u32[]{:S(2)}) %collective-permute-start.9) | collective-permute-done | bytes 65568 | tf_op jit(solution)/shard_map/ppermute | solution.py:362
  33.9 0.8 %collective-permute-done.11.refs_4_ = bf16[32,1024]{1,0:T(8,128)(2,1)S(1)} collective-permute-done((bf16[32,1024]{1,0:T(8,128)(2,1)S(1)}, bf16[32,1024]{1,0:T(8,128)(2,1)S(1)}, u32[]{:S(2)}, u32[]{:S(2)}) %collective-permute-start.11) | collective-permute-done | bytes 65568 | tf_op jit(solution)/shard_map/ppermute | solution.py:364
  34.7 0.7 %collective-permute-done.10.refs_3_ = bf16[32,1024]{1,0:T(8,128)(2,1)S(1)} collective-permute-done((bf16[32,1024]{1,0:T(8,128)(2,1)S(1)}, bf16[32,1024]{1,0:T(8,128)(2,1)S(1)}, u32[]{:S(2)}, u32[]{:S(2)}) %collective-permute-start.10) | collective-permute-done | bytes 65568 | tf_op jit(solution)/shard_map/ppermute | solution.py:364
  35.3 6.0 %frequency.1 = f32[256,32,512]{2,1,0:T(8,128)} custom-call(f32[512,128]{1,0:T(8,128)S(1)} %copy-done, f32[32,1024]{1,0:T(8,128)S(1)} %get-tuple-element.45.refs_0_, bf16[32,1024]{1,0:T(8,128)(2,1)S(1)} %collective-permute-done.8.refs_1_, bf16[32,1024]{1,0:T(8,128)(2,1)S(1)} %collective-permute-done.9.refs_2_, ...), custom_call_target="tpu_custom_call" | custom-call | flops 50000000 | bytes 17000000 | tf_op jit(solution)/shard_map/frequency/pallas_call | solution.py:304
  (18 shorter events, 0.3 us)
Async XLA Ops:
  1.3 14.7 %collective-permute-start.1 = (bf16[512,256]{1,0:T(8,128)(2,1)S(1)}, bf16[512,256]{1,0:T(8,128)(2,1)S(1)}, u32[]{:S(2)}, u32[]{:S(2)}) collective-permute-start(bf16[512,256]{1,0:T(8,128)(2,1)S(1)} %get-tuple-element.40), channel_id=1, source_target_pairs={{1,2},{3,4},{5,6},{7,8},{9,10},{11,12},{13,14},{2,1},{4,3},{6,5},{... | collective-permute-start | bytes 786440 | tf_op jit(solution)/shard_map/ppermute | solution.py:330
  1.9 14.0 %collective-permute-start = (bf16[512,256]{1,0:T(8,128)(2,1)S(1)}, bf16[512,256]{1,0:T(8,128)(2,1)S(1)}, u32[]{:S(2)}, u32[]{:S(2)}) collective-permute-start(bf16[512,256]{1,0:T(8,128)(2,1)S(1)} %get-tuple-element.41), channel_id=1, source_target_pairs={{0,1},{1,0},{2,3},{3,2},{4,5},{5,4},{6,7},{7,6},{8,9},{9,8},{10,11... | collective-permute-start | bytes 786440 | tf_op jit(solution)/shard_map/ppermute | solution.py:332
  6.3 11.2 %collective-permute-start.4 = (bf16[512,256]{1,0:T(8,128)(2,1)S(1)}, bf16[512,256]{1,0:T(8,128)(2,1)S(1)}, u32[]{:S(2)}, u32[]{:S(2)}) collective-permute-start(bf16[512,256]{1,0:T(8,128)(2,1)S(1)} %get-tuple-element.39), channel_id=1, source_target_pairs={{1,2},{3,4},{5,6},{7,8},{9,10},{11,12},{13,14},{2,1},{4,3},{6,5},{... | collective-permute-start | bytes 786440 | tf_op jit(solution)/shard_map/ppermute | solution.py:330
  7.0 10.1 %collective-permute-start.3 = (bf16[512,256]{1,0:T(8,128)(2,1)S(1)}, bf16[512,256]{1,0:T(8,128)(2,1)S(1)}, u32[]{:S(2)}, u32[]{:S(2)}) collective-permute-start(bf16[512,256]{1,0:T(8,128)(2,1)S(1)} %get-tuple-element.42), channel_id=1, source_target_pairs={{0,1},{1,0},{2,3},{3,2},{4,5},{5,4},{6,7},{7,6},{8,9},{9,8},{10,11... | collective-permute-start | bytes 786440 | tf_op jit(solution)/shard_map/ppermute | solution.py:332
  17.0 2.6 %collective-permute-start.2 = (bf16[256,512]{1,0:T(8,128)(2,1)S(1)}, bf16[256,512]{1,0:T(8,128)(2,1)S(1)}, u32[]{:S(2)}, u32[]{:S(2)}) collective-permute-start(bf16[256,512]{1,0:T(8,128)(2,1)S(1)} %get-tuple-element.18), channel_id=1, source_target_pairs={{0,1},{1,0},{2,3},{3,2},{4,5},{5,4},{6,7},{7,6},{8,9},{9,8},{10,11... | collective-permute-start | bytes 786440 | tf_op jit(solution)/shard_map/ppermute | solution.py:342
  18.2 3.8 %collective-permute-start.5 = (bf16[256,512]{1,0:T(8,128)(2,1)S(1)}, bf16[256,512]{1,0:T(8,128)(2,1)S(1)}, u32[]{:S(2)}, u32[]{:S(2)}) collective-permute-start(bf16[256,512]{1,0:T(8,128)(2,1)S(1)} %get-tuple-element.20), channel_id=1, source_target_pairs={{0,1},{1,0},{2,3},{3,2},{4,5},{5,4},{6,7},{7,6},{8,9},{9,8},{10,11... | collective-permute-start | bytes 786440 | tf_op jit(solution)/shard_map/ppermute | solution.py:342
  19.1 16.2 %copy-start = (f32[512,128]{1,0:T(8,128)S(1)}, f32[512,128]{1,0:T(8,128)}, u32[]{:S(2)}) copy-start(f32[512,128]{1,0:T(8,128)} %constant.17.clone.table) | copy-start | bytes 786436
  19.6 8.0 %collective-permute-start.6 = (bf16[3,32,512]{2,1,0:T(8,128)(2,1)S(1)}, bf16[3,32,512]{2,1,0:T(8,128)(2,1)S(1)}, u32[]{:S(2)}, u32[]{:S(2)}) collective-permute-start(bf16[3,32,512]{2,1,0:T(8,128)(2,1)S(1)} %pad_maximum_fusion), channel_id=1, source_target_pairs={{0,2},{1,3},{2,0},{3,1},{4,6},{5,7},{6,4},{7,5},{8,10},{9,11},{10,... | collective-permute-start | bytes 294920 | tf_op jit(solution)/shard_map/ppermute | solution.py:360
  22.2 9.6 %collective-permute-start.8 = (bf16[32,1024]{1,0:T(8,128)(2,1)S(1)}, bf16[32,1024]{1,0:T(8,128)(2,1)S(1)}, u32[]{:S(2)}, u32[]{:S(2)}) collective-permute-start(bf16[32,1024]{1,0:T(8,128)(2,1)S(1)} %pad_maximum_fusion.2), channel_id=1, source_target_pairs={{0,12},{1,13},{2,14},{3,15},{4,8},{5,9},{6,10},{7,11},{8,4},{9,5},... | collective-permute-start | bytes 196616 | tf_op jit(solution)/shard_map/ppermute | solution.py:362
  24.5 4.8 %collective-permute-start.7 = (bf16[3,32,512]{2,1,0:T(8,128)(2,1)S(1)}, bf16[3,32,512]{2,1,0:T(8,128)(2,1)S(1)}, u32[]{:S(2)}, u32[]{:S(2)}) collective-permute-start(bf16[3,32,512]{2,1,0:T(8,128)(2,1)S(1)} %pad_maximum_fusion.1), channel_id=1, source_target_pairs={{0,2},{1,3},{2,0},{3,1},{4,6},{5,7},{6,4},{7,5},{8,10},{9,11},{10,... | collective-permute-start | bytes 294920 | tf_op jit(solution)/shard_map/ppermute | solution.py:360
  26.3 7.5 %collective-permute-start.9 = (bf16[32,1024]{1,0:T(8,128)(2,1)S(1)}, bf16[32,1024]{1,0:T(8,128)(2,1)S(1)}, u32[]{:S(2)}, u32[]{:S(2)}) collective-permute-start(bf16[32,1024]{1,0:T(8,128)(2,1)S(1)} %pad_maximum_fusion.3), channel_id=1, source_target_pairs={{0,14},{1,15},{2,12},{3,13},{4,10},{5,11},{6,8},{7,9},{8,6},{9,7},... | collective-permute-start | bytes 196616 | tf_op jit(solution)/shard_map/ppermute | solution.py:362
  29.4 5.3 %collective-permute-start.11 = (bf16[32,1024]{1,0:T(8,128)(2,1)S(1)}, bf16[32,1024]{1,0:T(8,128)(2,1)S(1)}, u32[]{:S(2)}, u32[]{:S(2)}) collective-permute-start(bf16[32,1024]{1,0:T(8,128)(2,1)S(1)} %get-tuple-element.43), channel_id=1, source_target_pairs={{0,8},{1,9},{2,10},{3,11},{4,12},{5,13},{6,14},{7,15},{8,0},{9,1},... | collective-permute-start | bytes 196616 | tf_op jit(solution)/shard_map/ppermute | solution.py:364
  30.7 4.6 %collective-permute-start.10 = (bf16[32,1024]{1,0:T(8,128)(2,1)S(1)}, bf16[32,1024]{1,0:T(8,128)(2,1)S(1)}, u32[]{:S(2)}, u32[]{:S(2)}) collective-permute-start(bf16[32,1024]{1,0:T(8,128)(2,1)S(1)} %get-tuple-element.44), channel_id=1, source_target_pairs={{0,4},{1,5},{2,6},{3,7},{4,0},{5,1},{6,2},{7,3},{8,12},{9,13},{10,... | collective-permute-start | bytes 196616 | tf_op jit(solution)/shard_map/ppermute | solution.py:364

commit v7 on v6

--- a/solution.py
+++ b/solution.py
@@ -158,7 +158,7 @@
     def add(left):
         for row in range(count):
             value = part[row, :, columns]
-            term = outer(count, row, left, sigma, near)
+            term = outer(count, row, left, sigma, near.at[:, columns])
             total[row] = value if term is None else value + term
 
     @pl.when(first)
@@ -191,7 +191,7 @@
     def finish(far_left):
         for row in range(count):
             value = part[row, :, :COLUMNS]
-            for left, block in [(not far_left, ref) for ref in near] + [(far_left, halo)]:
+            for left, block in [(not far_left, ref.at[:, :COLUMNS]) for ref in near] + [(far_left, halo)]:
                 term = outer(count, row, left, sigma, block)
                 value = value if term is None else value + term
             for t in range(PAIRS):
@@ -324,12 +324,13 @@
     partner = [(i, i ^ 1) for i in range(devices)]
     pairs = [(i, i + 1) for i in range(1, devices - 1, 2)]
     pairs += [(b, a) for a, b in pairs]
-    halos, nears = [], []
+    halos = []
     for piece in range(CHUNKS):
         away = lax.dynamic_slice(coefficients, (core * (rows - width), piece * COLUMNS), (width, COLUMNS))
         halos.append(lax.ppermute(away, "trow", pairs))
-        inner = lax.dynamic_slice(coefficients, ((1 - core) * (rows - width), piece * COLUMNS), (width, COLUMNS))
-        nears.append(lax.ppermute(inner, "trow", partner))
+    inner = lax.dynamic_slice_in_dim(coefficients, (1 - core) * (rows - width), width, axis=0)
+    near = lax.ppermute(inner, "trow", partner)
+    nears = [near] * CHUNKS
     part, sigma, transposed = tiles(green, integrals, pattern, coefficients, devices == 16)
     if devices != 16:
         summed = jnp.concatenate(

time: 41.5 us -> 43.2 us (1.041)
  local copies, waits for them, and re-layouts: 1.26 us -> 2.15 us
  waiting for transfers between devices: 5.32 us -> 6.08 us
    ppermute x2, starting transfers between devices: 0.62 us -> 7.52 us  [local(): arrived.append(lax.ppermute(send, 'trow', partner))]
    ppermute x2 -> x1, starting transfers between devices: 7.31 us -> 0.52 us  [local(): near = lax.ppermute(inner, 'trow', partner)]
    dynamic_slice x0 -> x1, local copies, waits for them, and re-layouts: none -> 1.08 us  [local(): lax.dynamic_slice_in_dim(coefficients, (1 - core) * (rows - width), width...]
    ppermute x2, waiting for transfers between devices: 1.71 us -> 2.32 us  [local(): lax.ppermute(jnp.stack(blocks).astype(jnp.bfloat16), 'trow', flip[1])]
  transfers between devices with their start and end apart: 12 -> 11, of which waited for: 4 -> 3; matrix products, arithmetic and copies ran while one was open for 1% -> 3% of each run, Pallas kernels for 21% -> 21%
where the time goes in v7:
time: 43.2 us; the launch traced here: 42.9 us
  starting transfers between devices  19.4 us (45%)
  Pallas kernels  14.9 us (34%)
  waiting for transfers between devices  6.08 us (14%)
  local copies, waits for them, and re-layouts  2.15 us (5%)
    ppermute x2, starting transfers between devices, local(): arrived.append(lax.ppermute(send, 'trow', partner))  7.52 us
    pallas_call x1, Pallas kernels, tiles(): pl.pallas_call(functools.partial(tiles_kernel, count, split), out_shape=(...  6.03 us
    pallas_call x1, Pallas kernels, frequency(): pl.pallas_call(functools.partial(frequency_kernel, len(terms)), out_shape...  6.01 us
    ppermute x2, starting transfers between devices, local(): lax.ppermute(jnp.stack(blocks).astype(jnp.bfloat16), 'trow', flip[1])  4.28 us
    ppermute x2, starting transfers between devices, local(): straight = [lax.ppermute(cast[k], 'trow', flip[k]) for k in (6, 7)]  3.57 us
    ppermute x2, waiting for transfers between devices, local(): lax.ppermute(jnp.stack(blocks).astype(jnp.bfloat16), 'trow', flip[1])  2.32 us
    ppermute x2, starting transfers between devices, local(): lax.ppermute((sums[k] + beside[at]).astype(jnp.bfloat16), 'trow', flip[k])  2.19 us
    ppermute x2, waiting for transfers between devices, local(): straight = [lax.ppermute(cast[k], 'trow', flip[k]) for k in (6, 7)]  1.87 us
  transfers between devices with their start and end apart: 11, of which 3 were waited for; matrix products, arithmetic and copies ran while one was open for 3% of the time, Pallas kernels for 21%

profile of v7, /device:TPU:0, one launch (start us, length us, event | category | flops | bytes accessed | tf_op | source)
XLA Modules:
  0.0 42.9 jit_solution(11335335788402613116)
XLA Ops:
  0.0 1.1 %constant_dynamic-slice_fusion.1 = bf16[512,512]{1,0:T(8,128)(2,1)S(1)} fusion(bf16[768,512]{1,0:T(8,128)(2,1)} %coefficients.1, s32[]{:T(128)S(6)} %select_n.7), kind=kLoop, calls=%fused_computation.46 | loop fusion | bytes 1048580 | tf_op jit(solution)/shard_map/dynamic_slice | solution.py:331
  1.1 0.5 %collective-permute-start = (bf16[512,512]{1,0:T(8,128)(2,1)S(1)}, bf16[512,512]{1,0:T(8,128)(2,1)S(1)}, u32[]{:S(2)}, u32[]{:S(2)}) collective-permute-start(bf16[512,512]{1,0:T(8,128)(2,1)S(1)} %constant_dynamic-slice_fusion.1), channel_id=1, source_target_pairs={{0,1},{1,0},{2,3},{3,2},{4,5},{5,4},{6,7},{7,6},{8,9},{9,8},{10,11... | collective-permute-start | bytes 1572872 | tf_op jit(solution)/shard_map/ppermute | solution.py:332
  1.6 1.1 %constant_dynamic-slice_fusion.2 = (bf16[512,256]{1,0:T(8,128)(2,1)S(1)}, bf16[512,256]{1,0:T(8,128)(2,1)S(1)}) fusion(bf16[768,512]{1,0:T(8,128)(2,1)} %coefficients.1, s32[]{:T(128)S(6)} %select_n.8), kind=kLoop, calls=%fused_computation.47 | loop fusion | bytes 1048580 | tf_op jit(solution)/shard_map/dynamic_slice | solution.py:329
  2.7 0.7 %collective-permute-start.1 = (bf16[512,256]{1,0:T(8,128)(2,1)S(1)}, bf16[512,256]{1,0:T(8,128)(2,1)S(1)}, u32[]{:S(2)}, u32[]{:S(2)}) collective-permute-start(bf16[512,256]{1,0:T(8,128)(2,1)S(1)} %get-tuple-element.40), channel_id=1, source_target_pairs={{1,2},{3,4},{5,6},{7,8},{9,10},{11,12},{13,14},{2,1},{4,3},{6,5},{... | collective-permute-start | bytes 786440 | tf_op jit(solution)/shard_map/ppermute | solution.py:330
  3.3 0.7 %collective-permute-start.3 = (bf16[512,256]{1,0:T(8,128)(2,1)S(1)}, bf16[512,256]{1,0:T(8,128)(2,1)S(1)}, u32[]{:S(2)}, u32[]{:S(2)}) collective-permute-start(bf16[512,256]{1,0:T(8,128)(2,1)S(1)} %get-tuple-element.39), channel_id=1, source_target_pairs={{1,2},{3,4},{5,6},{7,8},{9,10},{11,12},{13,14},{2,1},{4,3},{6,5},{... | collective-permute-start | bytes 786440 | tf_op jit(solution)/shard_map/ppermute | solution.py:330
  4.0 6.0 %tiles.1 = (f32[6,256,512]{2,1,0:T(8,128)S(1)}, bf16[6,9,256,128]{3,2,1,0:T(8,128)(2,1)S(1)}, bf16[512,768]{1,0:T(8,128)(2,1)S(1)}) custom-call(s32[6,9]{1,0:T(8,128)} %mask.1, bf16[6,9,4,128,128]{4,3,2,1,0:T(8,128)(2,1)} %green.1, bf16[6,9,128,128]{3,2,1,0:T(8,128)(2,1)} %integrals.1, bf16[768,512]{1,0:T(8,128)(2,1)} %coefficients.1), custom_call_target="tpu_custom_call" | custom-call | flops 2000000000 | bytes 12000000 | tf_op jit(solution)/shard_map/tiles/pallas_call | solution.py:121
  10.1 1.0 %project.2 = (bf16[256,512]{1,0:T(8,128)(2,1)S(1)}, bf16[768,512]{1,0:T(8,128)(2,1)S(1)}) custom-call(f32[6,256,512]{2,1,0:T(8,128)S(1)} %get-tuple-element.14.refs_0_.part, bf16[6,9,256,128]{3,2,1,0:T(8,128)(2,1)S(1)} %get-tuple-element.15.refs_1_.sigma, bf16[512,512]{1,0:T(8,128)(2,1)S(1)} %collective-permute-done.refs_2_.near, ...), custom_call_target="tpu_custom_call" | custom-call | flops 500000000 | bytes 3000000 | tf_op jit(solution)/shard_map/project/pallas_call | solution.py:225
  11.1 6.1 %collective-permute-start.2 = (bf16[256,512]{1,0:T(8,128)(2,1)S(1)}, bf16[256,512]{1,0:T(8,128)(2,1)S(1)}, u32[]{:S(2)}, u32[]{:S(2)}) collective-permute-start(bf16[256,512]{1,0:T(8,128)(2,1)S(1)} %get-tuple-element.18), channel_id=1, source_target_pairs={{0,1},{1,0},{2,3},{3,2},{4,5},{5,4},{6,7},{7,6},{8,9},{9,8},{10,11... | collective-permute-start | bytes 786440 | tf_op jit(solution)/shard_map/ppermute | solution.py:343
  17.1 0.4 prepare.1.refs_0_
  17.6 0.8 %project.3 = (bf16[256,512]{1,0:T(8,128)(2,1)S(1)}, bf16[768,512]{1,0:T(8,128)(2,1)S(1)}) custom-call(f32[6,256,256]{2,1,0:T(8,128)S(1)} %prepare.1.refs_0_, bf16[6,9,256,128]{3,2,1,0:T(8,128)(2,1)S(1)} %get-tuple-element.15.refs_1_.sigma, bf16[512,256]{1,0:T(8,128)(2,1)S(1)} %collective-permute-done.3.refs_2_, ...), custom_call_target="tpu_custom_call" | custom-call | flops 500000000 | bytes 3000000 | tf_op jit(solution)/shard_map/project/pallas_call | solution.py:225
  18.3 1.4 %collective-permute-start.4 = (bf16[256,512]{1,0:T(8,128)(2,1)S(1)}, bf16[256,512]{1,0:T(8,128)(2,1)S(1)}, u32[]{:S(2)}, u32[]{:S(2)}) collective-permute-start(bf16[256,512]{1,0:T(8,128)(2,1)S(1)} %get-tuple-element.20), channel_id=1, source_target_pairs={{0,1},{1,0},{2,3},{3,2},{4,5},{5,4},{6,7},{7,6},{8,9},{9,8},{10,11... | collective-permute-start | bytes 786440 | tf_op jit(solution)/shard_map/ppermute | solution.py:343
  19.8 0.4 project_own.3
  20.1 0.4 project_own.2
  20.5 0.1 slice_add_fusion.1
  20.6 2.4 %collective-permute-start.5 = (bf16[3,32,512]{2,1,0:T(8,128)(2,1)S(1)}, bf16[3,32,512]{2,1,0:T(8,128)(2,1)S(1)}, u32[]{:S(2)}, u32[]{:S(2)}) collective-permute-start(bf16[3,32,512]{2,1,0:T(8,128)(2,1)S(1)} %pad_maximum_fusion), channel_id=1, source_target_pairs={{0,2},{1,3},{2,0},{3,1},{4,6},{5,7},{6,4},{7,5},{8,10},{9,11},{10,... | collective-permute-start | bytes 294920 | tf_op jit(solution)/shard_map/ppermute | solution.py:361
  23.1 2.9 %collective-permute-start.7 = (bf16[32,1024]{1,0:T(8,128)(2,1)S(1)}, bf16[32,1024]{1,0:T(8,128)(2,1)S(1)}, u32[]{:S(2)}, u32[]{:S(2)}) collective-permute-start(bf16[32,1024]{1,0:T(8,128)(2,1)S(1)} %pad_maximum_fusion.2), channel_id=1, source_target_pairs={{0,12},{1,13},{2,14},{3,15},{4,8},{5,9},{6,10},{7,11},{8,4},{9,5},... | collective-permute-start | bytes 196616 | tf_op jit(solution)/shard_map/ppermute | solution.py:363
  26.1 1.8 %collective-permute-start.6 = (bf16[3,32,512]{2,1,0:T(8,128)(2,1)S(1)}, bf16[3,32,512]{2,1,0:T(8,128)(2,1)S(1)}, u32[]{:S(2)}, u32[]{:S(2)}) collective-permute-start(bf16[3,32,512]{2,1,0:T(8,128)(2,1)S(1)} %pad_maximum_fusion.1), channel_id=1, source_target_pairs={{0,2},{1,3},{2,0},{3,1},{4,6},{5,7},{6,4},{7,5},{8,10},{9,11},{10,... | collective-permute-start | bytes 294920 | tf_op jit(solution)/shard_map/ppermute | solution.py:361
  27.9 0.7 %collective-permute-start.8 = (bf16[32,1024]{1,0:T(8,128)(2,1)S(1)}, bf16[32,1024]{1,0:T(8,128)(2,1)S(1)}, u32[]{:S(2)}, u32[]{:S(2)}) collective-permute-start(bf16[32,1024]{1,0:T(8,128)(2,1)S(1)} %pad_maximum_fusion.3), channel_id=1, source_target_pairs={{0,14},{1,15},{2,12},{3,13},{4,10},{5,11},{6,8},{7,9},{8,6},{9,7},... | collective-permute-start | bytes 196616 | tf_op jit(solution)/shard_map/ppermute | solution.py:363
  28.6 2.3 %collective-permute-done.6 = bf16[3,32,512]{2,1,0:T(8,128)(2,1)S(1)} collective-permute-done((bf16[3,32,512]{2,1,0:T(8,128)(2,1)S(1)}, bf16[3,32,512]{2,1,0:T(8,128)(2,1)S(1)}, u32[]{:S(2)}, u32[]{:S(2)}) %collective-permute-start.6) | collective-permute-done | bytes 98336 | tf_op jit(solution)/shard_map/ppermute | solution.py:361
  31.0 1.1 %collective-permute-start.10 = (bf16[32,1024]{1,0:T(8,128)(2,1)S(1)}, bf16[32,1024]{1,0:T(8,128)(2,1)S(1)}, u32[]{:S(2)}, u32[]{:S(2)}) collective-permute-start(bf16[32,1024]{1,0:T(8,128)(2,1)S(1)} %get-tuple-element.41), channel_id=1, source_target_pairs={{0,8},{1,9},{2,10},{3,11},{4,12},{5,13},{6,14},{7,15},{8,0},{9,1},... | collective-permute-start | bytes 196616 | tf_op jit(solution)/shard_map/ppermute | solution.py:365
  32.1 1.1 %collective-permute-start.9 = (bf16[32,1024]{1,0:T(8,128)(2,1)S(1)}, bf16[32,1024]{1,0:T(8,128)(2,1)S(1)}, u32[]{:S(2)}, u32[]{:S(2)}) collective-permute-start(bf16[32,1024]{1,0:T(8,128)(2,1)S(1)} %get-tuple-element.42), channel_id=1, source_target_pairs={{0,4},{1,5},{2,6},{3,7},{4,0},{5,1},{6,2},{7,3},{8,12},{9,13},{10,... | collective-permute-start | bytes 196616 | tf_op jit(solution)/shard_map/ppermute | solution.py:365
  33.2 1.9 %collective-permute-done.8.refs_2_ = bf16[32,1024]{1,0:T(8,128)(2,1)S(1)} collective-permute-done((bf16[32,1024]{1,0:T(8,128)(2,1)S(1)}, bf16[32,1024]{1,0:T(8,128)(2,1)S(1)}, u32[]{:S(2)}, u32[]{:S(2)}) %collective-permute-start.8) | collective-permute-done | bytes 65568 | tf_op jit(solution)/shard_map/ppermute | solution.py:363
  35.1 1.9 %collective-permute-done.10.refs_4_ = bf16[32,1024]{1,0:T(8,128)(2,1)S(1)} collective-permute-done((bf16[32,1024]{1,0:T(8,128)(2,1)S(1)}, bf16[32,1024]{1,0:T(8,128)(2,1)S(1)}, u32[]{:S(2)}, u32[]{:S(2)}) %collective-permute-start.10) | collective-permute-done | bytes 65568 | tf_op jit(solution)/shard_map/ppermute | solution.py:365
  36.9 6.0 %frequency.1 = f32[256,32,512]{2,1,0:T(8,128)} custom-call(f32[512,128]{1,0:T(8,128)S(1)} %copy-done, f32[32,1024]{1,0:T(8,128)S(1)} %get-tuple-element.43.refs_0_, bf16[32,1024]{1,0:T(8,128)(2,1)S(1)} %collective-permute-done.7.refs_1_, bf16[32,1024]{1,0:T(8,128)(2,1)S(1)} %collective-permute-done.8.refs_2_, ...), custom_call_target="tpu_custom_call" | custom-call | flops 50000000 | bytes 17000000 | tf_op jit(solution)/shard_map/frequency/pallas_call | solution.py:304
  (17 shorter events, 0.2 us)
Async XLA Ops:
  1.1 9.0 %collective-permute-start = (bf16[512,512]{1,0:T(8,128)(2,1)S(1)}, bf16[512,512]{1,0:T(8,128)(2,1)S(1)}, u32[]{:S(2)}, u32[]{:S(2)}) collective-permute-start(bf16[512,512]{1,0:T(8,128)(2,1)S(1)} %constant_dynamic-slice_fusion.1), channel_id=1, source_target_pairs={{0,1},{1,0},{2,3},{3,2},{4,5},{5,4},{6,7},{7,6},{8,9},{9,8},{10,11... | collective-permute-start | bytes 1572872 | tf_op jit(solution)/shard_map/ppermute | solution.py:332
  2.7 7.4 %collective-permute-start.1 = (bf16[512,256]{1,0:T(8,128)(2,1)S(1)}, bf16[512,256]{1,0:T(8,128)(2,1)S(1)}, u32[]{:S(2)}, u32[]{:S(2)}) collective-permute-start(bf16[512,256]{1,0:T(8,128)(2,1)S(1)} %get-tuple-element.40), channel_id=1, source_target_pairs={{1,2},{3,4},{5,6},{7,8},{9,10},{11,12},{13,14},{2,1},{4,3},{6,5},{... | collective-permute-start | bytes 786440 | tf_op jit(solution)/shard_map/ppermute | solution.py:330
  3.3 14.2 %collective-permute-start.3 = (bf16[512,256]{1,0:T(8,128)(2,1)S(1)}, bf16[512,256]{1,0:T(8,128)(2,1)S(1)}, u32[]{:S(2)}, u32[]{:S(2)}) collective-permute-start(bf16[512,256]{1,0:T(8,128)(2,1)S(1)} %get-tuple-element.39), channel_id=1, source_target_pairs={{1,2},{3,4},{5,6},{7,8},{9,10},{11,12},{13,14},{2,1},{4,3},{6,5},{... | collective-permute-start | bytes 786440 | tf_op jit(solution)/shard_map/ppermute | solution.py:330
  11.1 9.4 %collective-permute-start.2 = (bf16[256,512]{1,0:T(8,128)(2,1)S(1)}, bf16[256,512]{1,0:T(8,128)(2,1)S(1)}, u32[]{:S(2)}, u32[]{:S(2)}) collective-permute-start(bf16[256,512]{1,0:T(8,128)(2,1)S(1)} %get-tuple-element.18), channel_id=1, source_target_pairs={{0,1},{1,0},{2,3},{3,2},{4,5},{5,4},{6,7},{7,6},{8,9},{9,8},{10,11... | collective-permute-start | bytes 786440 | tf_op jit(solution)/shard_map/ppermute | solution.py:343
  18.3 4.7 %collective-permute-start.4 = (bf16[256,512]{1,0:T(8,128)(2,1)S(1)}, bf16[256,512]{1,0:T(8,128)(2,1)S(1)}, u32[]{:S(2)}, u32[]{:S(2)}) collective-permute-start(bf16[256,512]{1,0:T(8,128)(2,1)S(1)} %get-tuple-element.20), channel_id=1, source_target_pairs={{0,1},{1,0},{2,3},{3,2},{4,5},{5,4},{6,7},{7,6},{8,9},{9,8},{10,11... | collective-permute-start | bytes 786440 | tf_op jit(solution)/shard_map/ppermute | solution.py:343
  20.1 16.8 %copy-start = (f32[512,128]{1,0:T(8,128)S(1)}, f32[512,128]{1,0:T(8,128)}, u32[]{:S(2)}) copy-start(f32[512,128]{1,0:T(8,128)} %constant.17.clone.table) | copy-start | bytes 786436
  20.6 8.0 %collective-permute-start.5 = (bf16[3,32,512]{2,1,0:T(8,128)(2,1)S(1)}, bf16[3,32,512]{2,1,0:T(8,128)(2,1)S(1)}, u32[]{:S(2)}, u32[]{:S(2)}) collective-permute-start(bf16[3,32,512]{2,1,0:T(8,128)(2,1)S(1)} %pad_maximum_fusion), channel_id=1, source_target_pairs={{0,2},{1,3},{2,0},{3,1},{4,6},{5,7},{6,4},{7,5},{8,10},{9,11},{10,... | collective-permute-start | bytes 294920 | tf_op jit(solution)/shard_map/ppermute | solution.py:361
  23.1 10.0 %collective-permute-start.7 = (bf16[32,1024]{1,0:T(8,128)(2,1)S(1)}, bf16[32,1024]{1,0:T(8,128)(2,1)S(1)}, u32[]{:S(2)}, u32[]{:S(2)}) collective-permute-start(bf16[32,1024]{1,0:T(8,128)(2,1)S(1)} %pad_maximum_fusion.2), channel_id=1, source_target_pairs={{0,12},{1,13},{2,14},{3,15},{4,8},{5,9},{6,10},{7,11},{8,4},{9,5},... | collective-permute-start | bytes 196616 | tf_op jit(solution)/shard_map/ppermute | solution.py:363
  26.1 4.8 %collective-permute-start.6 = (bf16[3,32,512]{2,1,0:T(8,128)(2,1)S(1)}, bf16[3,32,512]{2,1,0:T(8,128)(2,1)S(1)}, u32[]{:S(2)}, u32[]{:S(2)}) collective-permute-start(bf16[3,32,512]{2,1,0:T(8,128)(2,1)S(1)} %pad_maximum_fusion.1), channel_id=1, source_target_pairs={{0,2},{1,3},{2,0},{3,1},{4,6},{5,7},{6,4},{7,5},{8,10},{9,11},{10,... | collective-permute-start | bytes 294920 | tf_op jit(solution)/shard_map/ppermute | solution.py:361
  27.9 7.1 %collective-permute-start.8 = (bf16[32,1024]{1,0:T(8,128)(2,1)S(1)}, bf16[32,1024]{1,0:T(8,128)(2,1)S(1)}, u32[]{:S(2)}, u32[]{:S(2)}) collective-permute-start(bf16[32,1024]{1,0:T(8,128)(2,1)S(1)} %pad_maximum_fusion.3), channel_id=1, source_target_pairs={{0,14},{1,15},{2,12},{3,13},{4,10},{5,11},{6,8},{7,9},{8,6},{9,7},... | collective-permute-start | bytes 196616 | tf_op jit(solution)/shard_map/ppermute | solution.py:363
  31.0 5.9 %collective-permute-start.10 = (bf16[32,1024]{1,0:T(8,128)(2,1)S(1)}, bf16[32,1024]{1,0:T(8,128)(2,1)S(1)}, u32[]{:S(2)}, u32[]{:S(2)}) collective-permute-start(bf16[32,1024]{1,0:T(8,128)(2,1)S(1)} %get-tuple-element.41), channel_id=1, source_target_pairs={{0,8},{1,9},{2,10},{3,11},{4,12},{5,13},{6,14},{7,15},{8,0},{9,1},... | collective-permute-start | bytes 196616 | tf_op jit(solution)/shard_map/ppermute | solution.py:365
  32.1 4.8 %collective-permute-start.9 = (bf16[32,1024]{1,0:T(8,128)(2,1)S(1)}, bf16[32,1024]{1,0:T(8,128)(2,1)S(1)}, u32[]{:S(2)}, u32[]{:S(2)}) collective-permute-start(bf16[32,1024]{1,0:T(8,128)(2,1)S(1)} %get-tuple-element.42), channel_id=1, source_target_pairs={{0,4},{1,5},{2,6},{3,7},{4,0},{5,1},{6,2},{7,3},{8,12},{9,13},{10,... | collective-permute-start | bytes 196616 | tf_op jit(solution)/shard_map/ppermute | solution.py:365

commit v8 on v6

--- a/solution.py
+++ b/solution.py
@@ -18,7 +18,7 @@
 FREQ_STEP = 4
 FREQ_EDGES = [0, 2, 4, 8, 16, *range(32, 2 * NW + 1, 32)]
 FREQ_BLOCKS = list(zip(FREQ_EDGES, FREQ_EDGES[1:]))
-GROUP = 6
+GROUP = 9
 CHUNKS = 2
 COLUMNS = NMO // CHUNKS
 MIB = 1 << 20

time: 41.5 us -> 41.5 us (level)
  no operation moved by 1% of the time
where the time goes in v8:
time: 41.5 us; the launch traced here: 41.3 us
  starting transfers between devices  19.6 us (47%)
  Pallas kernels  14.7 us (35%)
  waiting for transfers between devices  5.32 us (13%)
  local copies, waits for them, and re-layouts  1.26 us (3%)
    ppermute x2, starting transfers between devices, local(): nears.append(lax.ppermute(inner, 'trow', partner))  7.31 us
    pallas_call x1, Pallas kernels, frequency(): pl.pallas_call(functools.partial(frequency_kernel, len(terms)), out_shape...  6 us
    pallas_call x1, Pallas kernels, tiles(): pl.pallas_call(functools.partial(tiles_kernel, count, split), out_shape=(...  5.9 us
    ppermute x2, starting transfers between devices, local(): lax.ppermute(jnp.stack(blocks).astype(jnp.bfloat16), 'trow', flip[1])  4.28 us
    ppermute x2, starting transfers between devices, local(): straight = [lax.ppermute(cast[k], 'trow', flip[k]) for k in (6, 7)]  3.57 us
    ppermute x2, starting transfers between devices, local(): lax.ppermute((sums[k] + beside[at]).astype(jnp.bfloat16), 'trow', flip[k])  2.33 us
    ppermute x2, waiting for transfers between devices, local(): straight = [lax.ppermute(cast[k], 'trow', flip[k]) for k in (6, 7)]  2.13 us
    ppermute x2, waiting for transfers between devices, local(): lax.ppermute(jnp.stack(blocks).astype(jnp.bfloat16), 'trow', flip[1])  1.71 us
  transfers between devices with their start and end apart: 12, of which 4 were waited for; matrix products, arithmetic and copies ran while one was open for 1% of the time, Pallas kernels for 21%

profile of v8, /device:TPU:0, one launch (start us, length us, event | category | flops | bytes accessed | tf_op | source)
XLA Modules:
  0.0 41.3 jit_solution(13768773125623867464)
XLA Ops:
  0.0 1.3 %constant_dynamic-slice_fusion = (bf16[512,256]{1,0:T(8,128)(2,1)S(1)}, bf16[512,256]{1,0:T(8,128)(2,1)S(1)}, bf16[512,256]{1,0:T(8,128)(2,1)S(1)}, bf16[512,256]{1,0:T(8,128)(2,1)S(1)}) fusion(bf16[768,512]{1,0:T(8,128)(2,1)} %coefficients.1, s32[]{:T(128)S(6)} %select_n.9, s32[]{:T(128)S(6)} %select_n.8), kind=kLoop, calls=%fused_computation.45 | loop fusion | bytes 2097160 | tf_op jit(solution)/shard_map/dynamic_slice | solution.py:329
  1.3 0.7 %collective-permute-start.1 = (bf16[512,256]{1,0:T(8,128)(2,1)S(1)}, bf16[512,256]{1,0:T(8,128)(2,1)S(1)}, u32[]{:S(2)}, u32[]{:S(2)}) collective-permute-start(bf16[512,256]{1,0:T(8,128)(2,1)S(1)} %get-tuple-element.40), channel_id=1, source_target_pairs={{1,2},{3,4},{5,6},{7,8},{9,10},{11,12},{13,14},{2,1},{4,3},{6,5},{... | collective-permute-start | bytes 786440 | tf_op jit(solution)/shard_map/ppermute | solution.py:330
  1.9 4.3 %collective-permute-start = (bf16[512,256]{1,0:T(8,128)(2,1)S(1)}, bf16[512,256]{1,0:T(8,128)(2,1)S(1)}, u32[]{:S(2)}, u32[]{:S(2)}) collective-permute-start(bf16[512,256]{1,0:T(8,128)(2,1)S(1)} %get-tuple-element.41), channel_id=1, source_target_pairs={{0,1},{1,0},{2,3},{3,2},{4,5},{5,4},{6,7},{7,6},{8,9},{9,8},{10,11... | collective-permute-start | bytes 786440 | tf_op jit(solution)/shard_map/ppermute | solution.py:332
  6.3 0.7 %collective-permute-start.4 = (bf16[512,256]{1,0:T(8,128)(2,1)S(1)}, bf16[512,256]{1,0:T(8,128)(2,1)S(1)}, u32[]{:S(2)}, u32[]{:S(2)}) collective-permute-start(bf16[512,256]{1,0:T(8,128)(2,1)S(1)} %get-tuple-element.39), channel_id=1, source_target_pairs={{1,2},{3,4},{5,6},{7,8},{9,10},{11,12},{13,14},{2,1},{4,3},{6,5},{... | collective-permute-start | bytes 786440 | tf_op jit(solution)/shard_map/ppermute | solution.py:330
  7.0 3.0 %collective-permute-start.3 = (bf16[512,256]{1,0:T(8,128)(2,1)S(1)}, bf16[512,256]{1,0:T(8,128)(2,1)S(1)}, u32[]{:S(2)}, u32[]{:S(2)}) collective-permute-start(bf16[512,256]{1,0:T(8,128)(2,1)S(1)} %get-tuple-element.42), channel_id=1, source_target_pairs={{0,1},{1,0},{2,3},{3,2},{4,5},{5,4},{6,7},{7,6},{8,9},{9,8},{10,11... | collective-permute-start | bytes 786440 | tf_op jit(solution)/shard_map/ppermute | solution.py:332
  9.9 5.9 %tiles.1 = (f32[6,256,512]{2,1,0:T(8,128)S(1)}, bf16[6,9,256,128]{3,2,1,0:T(8,128)(2,1)S(1)}, bf16[512,768]{1,0:T(8,128)(2,1)S(1)}) custom-call(s32[6,9]{1,0:T(8,128)} %mask.1, bf16[6,9,4,128,128]{4,3,2,1,0:T(8,128)(2,1)} %green.1, bf16[6,9,128,128]{3,2,1,0:T(8,128)(2,1)} %integrals.1, bf16[768,512]{1,0:T(8,128)(2,1)} %coefficients.1), custom_call_target="tpu_custom_call" | custom-call | flops 2000000000 | bytes 12000000 | tf_op jit(solution)/shard_map/tiles/pallas_call | solution.py:121
  15.9 1.0 %project.2 = (bf16[256,512]{1,0:T(8,128)(2,1)S(1)}, bf16[768,512]{1,0:T(8,128)(2,1)S(1)}) custom-call(f32[6,256,512]{2,1,0:T(8,128)S(1)} %get-tuple-element.14.refs_0_.part, bf16[6,9,256,128]{3,2,1,0:T(8,128)(2,1)S(1)} %get-tuple-element.15.refs_1_.sigma, bf16[512,256]{1,0:T(8,128)(2,1)S(1)} %collective-permute-done.refs_2_, ...), custom_call_target="tpu_custom_call" | custom-call | flops 500000000 | bytes 3000000 | tf_op jit(solution)/shard_map/project/pallas_call | solution.py:225
  16.8 0.3 collective-permute-start.2
  17.1 0.4 prepare.1.refs_0_
  17.5 0.8 %project.3 = (bf16[256,512]{1,0:T(8,128)(2,1)S(1)}, bf16[768,512]{1,0:T(8,128)(2,1)S(1)}) custom-call(f32[6,256,256]{2,1,0:T(8,128)S(1)} %prepare.1.refs_0_, bf16[6,9,256,128]{3,2,1,0:T(8,128)(2,1)S(1)} %get-tuple-element.15.refs_1_.sigma, bf16[512,256]{1,0:T(8,128)(2,1)S(1)} %collective-permute-done.4.refs_2_, ...), custom_call_target="tpu_custom_call" | custom-call | flops 500000000 | bytes 3000000 | tf_op jit(solution)/shard_map/project/pallas_call | solution.py:225
  18.3 0.5 %collective-permute-start.5 = (bf16[256,512]{1,0:T(8,128)(2,1)S(1)}, bf16[256,512]{1,0:T(8,128)(2,1)S(1)}, u32[]{:S(2)}, u32[]{:S(2)}) collective-permute-start(bf16[256,512]{1,0:T(8,128)(2,1)S(1)} %get-tuple-element.20), channel_id=1, source_target_pairs={{0,1},{1,0},{2,3},{3,2},{4,5},{5,4},{6,7},{7,6},{8,9},{9,8},{10,11... | collective-permute-start | bytes 786440 | tf_op jit(solution)/shard_map/ppermute | solution.py:342
  18.8 0.4 project_own.3
  19.2 0.4 project_own.2
  19.6 2.4 %collective-permute-start.6 = (bf16[3,32,512]{2,1,0:T(8,128)(2,1)S(1)}, bf16[3,32,512]{2,1,0:T(8,128)(2,1)S(1)}, u32[]{:S(2)}, u32[]{:S(2)}) collective-permute-start(bf16[3,32,512]{2,1,0:T(8,128)(2,1)S(1)} %pad_maximum_fusion), channel_id=1, source_target_pairs={{0,2},{1,3},{2,0},{3,1},{4,6},{5,7},{6,4},{7,5},{8,10},{9,11},{10,... | collective-permute-start | bytes 294920 | tf_op jit(solution)/shard_map/ppermute | solution.py:360
  22.2 2.3 %collective-permute-start.8 = (bf16[32,1024]{1,0:T(8,128)(2,1)S(1)}, bf16[32,1024]{1,0:T(8,128)(2,1)S(1)}, u32[]{:S(2)}, u32[]{:S(2)}) collective-permute-start(bf16[32,1024]{1,0:T(8,128)(2,1)S(1)} %pad_maximum_fusion.2), channel_id=1, source_target_pairs={{0,12},{1,13},{2,14},{3,15},{4,8},{5,9},{6,10},{7,11},{8,4},{9,5},... | collective-permute-start | bytes 196616 | tf_op jit(solution)/shard_map/ppermute | solution.py:362
  24.5 1.8 %collective-permute-start.7 = (bf16[3,32,512]{2,1,0:T(8,128)(2,1)S(1)}, bf16[3,32,512]{2,1,0:T(8,128)(2,1)S(1)}, u32[]{:S(2)}, u32[]{:S(2)}) collective-permute-start(bf16[3,32,512]{2,1,0:T(8,128)(2,1)S(1)} %pad_maximum_fusion.1), channel_id=1, source_target_pairs={{0,2},{1,3},{2,0},{3,1},{4,6},{5,7},{6,4},{7,5},{8,10},{9,11},{10,... | collective-permute-start | bytes 294920 | tf_op jit(solution)/shard_map/ppermute | solution.py:360
  26.3 1.3 %collective-permute-start.9 = (bf16[32,1024]{1,0:T(8,128)(2,1)S(1)}, bf16[32,1024]{1,0:T(8,128)(2,1)S(1)}, u32[]{:S(2)}, u32[]{:S(2)}) collective-permute-start(bf16[32,1024]{1,0:T(8,128)(2,1)S(1)} %pad_maximum_fusion.3), channel_id=1, source_target_pairs={{0,14},{1,15},{2,12},{3,13},{4,10},{5,11},{6,8},{7,9},{8,6},{9,7},... | collective-permute-start | bytes 196616 | tf_op jit(solution)/shard_map/ppermute | solution.py:362
  27.6 1.7 %collective-permute-done.7 = bf16[3,32,512]{2,1,0:T(8,128)(2,1)S(1)} collective-permute-done((bf16[3,32,512]{2,1,0:T(8,128)(2,1)S(1)}, bf16[3,32,512]{2,1,0:T(8,128)(2,1)S(1)}, u32[]{:S(2)}, u32[]{:S(2)}) %collective-permute-start.7) | collective-permute-done | bytes 98336 | tf_op jit(solution)/shard_map/ppermute | solution.py:360
  29.4 1.3 %collective-permute-start.11 = (bf16[32,1024]{1,0:T(8,128)(2,1)S(1)}, bf16[32,1024]{1,0:T(8,128)(2,1)S(1)}, u32[]{:S(2)}, u32[]{:S(2)}) collective-permute-start(bf16[32,1024]{1,0:T(8,128)(2,1)S(1)} %get-tuple-element.43), channel_id=1, source_target_pairs={{0,8},{1,9},{2,10},{3,11},{4,12},{5,13},{6,14},{7,15},{8,0},{9,1},... | collective-permute-start | bytes 196616 | tf_op jit(solution)/shard_map/ppermute | solution.py:364
  30.7 1.0 %collective-permute-start.10 = (bf16[32,1024]{1,0:T(8,128)(2,1)S(1)}, bf16[32,1024]{1,0:T(8,128)(2,1)S(1)}, u32[]{:S(2)}, u32[]{:S(2)}) collective-permute-start(bf16[32,1024]{1,0:T(8,128)(2,1)S(1)} %get-tuple-element.44), channel_id=1, source_target_pairs={{0,4},{1,5},{2,6},{3,7},{4,0},{5,1},{6,2},{7,3},{8,12},{9,13},{10,... | collective-permute-start | bytes 196616 | tf_op jit(solution)/shard_map/ppermute | solution.py:364
  31.7 2.1 %collective-permute-done.9.refs_2_ = bf16[32,1024]{1,0:T(8,128)(2,1)S(1)} collective-permute-done((bf16[32,1024]{1,0:T(8,128)(2,1)S(1)}, bf16[32,1024]{1,0:T(8,128)(2,1)S(1)}, u32[]{:S(2)}, u32[]{:S(2)}) %collective-permute-start.9) | collective-permute-done | bytes 65568 | tf_op jit(solution)/shard_map/ppermute | solution.py:362
  33.9 0.8 %collective-permute-done.11.refs_4_ = bf16[32,1024]{1,0:T(8,128)(2,1)S(1)} collective-permute-done((bf16[32,1024]{1,0:T(8,128)(2,1)S(1)}, bf16[32,1024]{1,0:T(8,128)(2,1)S(1)}, u32[]{:S(2)}, u32[]{:S(2)}) %collective-permute-start.11) | collective-permute-done | bytes 65568 | tf_op jit(solution)/shard_map/ppermute | solution.py:364
  34.7 0.7 %collective-permute-done.10.refs_3_ = bf16[32,1024]{1,0:T(8,128)(2,1)S(1)} collective-permute-done((bf16[32,1024]{1,0:T(8,128)(2,1)S(1)}, bf16[32,1024]{1,0:T(8,128)(2,1)S(1)}, u32[]{:S(2)}, u32[]{:S(2)}) %collective-permute-start.10) | collective-permute-done | bytes 65568 | tf_op jit(solution)/shard_map/ppermute | solution.py:364
  35.3 6.0 %frequency.1 = f32[256,32,512]{2,1,0:T(8,128)} custom-call(f32[512,128]{1,0:T(8,128)S(1)} %copy-done, f32[32,1024]{1,0:T(8,128)S(1)} %get-tuple-element.45.refs_0_, bf16[32,1024]{1,0:T(8,128)(2,1)S(1)} %collective-permute-done.8.refs_1_, bf16[32,1024]{1,0:T(8,128)(2,1)S(1)} %collective-permute-done.9.refs_2_, ...), custom_call_target="tpu_custom_call" | custom-call | flops 50000000 | bytes 17000000 | tf_op jit(solution)/shard_map/frequency/pallas_call | solution.py:304
  (18 shorter events, 0.3 us)
Async XLA Ops:
  1.3 14.6 %collective-permute-start.1 = (bf16[512,256]{1,0:T(8,128)(2,1)S(1)}, bf16[512,256]{1,0:T(8,128)(2,1)S(1)}, u32[]{:S(2)}, u32[]{:S(2)}) collective-permute-start(bf16[512,256]{1,0:T(8,128)(2,1)S(1)} %get-tuple-element.40), channel_id=1, source_target_pairs={{1,2},{3,4},{5,6},{7,8},{9,10},{11,12},{13,14},{2,1},{4,3},{6,5},{... | collective-permute-start | bytes 786440 | tf_op jit(solution)/shard_map/ppermute | solution.py:330
  1.9 13.9 %collective-permute-start = (bf16[512,256]{1,0:T(8,128)(2,1)S(1)}, bf16[512,256]{1,0:T(8,128)(2,1)S(1)}, u32[]{:S(2)}, u32[]{:S(2)}) collective-permute-start(bf16[512,256]{1,0:T(8,128)(2,1)S(1)} %get-tuple-element.41), channel_id=1, source_target_pairs={{0,1},{1,0},{2,3},{3,2},{4,5},{5,4},{6,7},{7,6},{8,9},{9,8},{10,11... | collective-permute-start | bytes 786440 | tf_op jit(solution)/shard_map/ppermute | solution.py:332
  6.3 11.2 %collective-permute-start.4 = (bf16[512,256]{1,0:T(8,128)(2,1)S(1)}, bf16[512,256]{1,0:T(8,128)(2,1)S(1)}, u32[]{:S(2)}, u32[]{:S(2)}) collective-permute-start(bf16[512,256]{1,0:T(8,128)(2,1)S(1)} %get-tuple-element.39), channel_id=1, source_target_pairs={{1,2},{3,4},{5,6},{7,8},{9,10},{11,12},{13,14},{2,1},{4,3},{6,5},{... | collective-permute-start | bytes 786440 | tf_op jit(solution)/shard_map/ppermute | solution.py:330
  7.0 10.2 %collective-permute-start.3 = (bf16[512,256]{1,0:T(8,128)(2,1)S(1)}, bf16[512,256]{1,0:T(8,128)(2,1)S(1)}, u32[]{:S(2)}, u32[]{:S(2)}) collective-permute-start(bf16[512,256]{1,0:T(8,128)(2,1)S(1)} %get-tuple-element.42), channel_id=1, source_target_pairs={{0,1},{1,0},{2,3},{3,2},{4,5},{5,4},{6,7},{7,6},{8,9},{9,8},{10,11... | collective-permute-start | bytes 786440 | tf_op jit(solution)/shard_map/ppermute | solution.py:332
  16.8 2.7 %collective-permute-start.2 = (bf16[256,512]{1,0:T(8,128)(2,1)S(1)}, bf16[256,512]{1,0:T(8,128)(2,1)S(1)}, u32[]{:S(2)}, u32[]{:S(2)}) collective-permute-start(bf16[256,512]{1,0:T(8,128)(2,1)S(1)} %get-tuple-element.18), channel_id=1, source_target_pairs={{0,1},{1,0},{2,3},{3,2},{4,5},{5,4},{6,7},{7,6},{8,9},{9,8},{10,11... | collective-permute-start | bytes 786440 | tf_op jit(solution)/shard_map/ppermute | solution.py:342
  18.3 3.8 %collective-permute-start.5 = (bf16[256,512]{1,0:T(8,128)(2,1)S(1)}, bf16[256,512]{1,0:T(8,128)(2,1)S(1)}, u32[]{:S(2)}, u32[]{:S(2)}) collective-permute-start(bf16[256,512]{1,0:T(8,128)(2,1)S(1)} %get-tuple-element.20), channel_id=1, source_target_pairs={{0,1},{1,0},{2,3},{3,2},{4,5},{5,4},{6,7},{7,6},{8,9},{9,8},{10,11... | collective-permute-start | bytes 786440 | tf_op jit(solution)/shard_map/ppermute | solution.py:342
  19.1 16.2 %copy-start = (f32[512,128]{1,0:T(8,128)S(1)}, f32[512,128]{1,0:T(8,128)}, u32[]{:S(2)}) copy-start(f32[512,128]{1,0:T(8,128)} %constant.17.clone.table) | copy-start | bytes 786436
  19.6 8.0 %collective-permute-start.6 = (bf16[3,32,512]{2,1,0:T(8,128)(2,1)S(1)}, bf16[3,32,512]{2,1,0:T(8,128)(2,1)S(1)}, u32[]{:S(2)}, u32[]{:S(2)}) collective-permute-start(bf16[3,32,512]{2,1,0:T(8,128)(2,1)S(1)} %pad_maximum_fusion), channel_id=1, source_target_pairs={{0,2},{1,3},{2,0},{3,1},{4,6},{5,7},{6,4},{7,5},{8,10},{9,11},{10,... | collective-permute-start | bytes 294920 | tf_op jit(solution)/shard_map/ppermute | solution.py:360
  22.2 9.6 %collective-permute-start.8 = (bf16[32,1024]{1,0:T(8,128)(2,1)S(1)}, bf16[32,1024]{1,0:T(8,128)(2,1)S(1)}, u32[]{:S(2)}, u32[]{:S(2)}) collective-permute-start(bf16[32,1024]{1,0:T(8,128)(2,1)S(1)} %pad_maximum_fusion.2), channel_id=1, source_target_pairs={{0,12},{1,13},{2,14},{3,15},{4,8},{5,9},{6,10},{7,11},{8,4},{9,5},... | collective-permute-start | bytes 196616 | tf_op jit(solution)/shard_map/ppermute | solution.py:362
  24.5 4.8 %collective-permute-start.7 = (bf16[3,32,512]{2,1,0:T(8,128)(2,1)S(1)}, bf16[3,32,512]{2,1,0:T(8,128)(2,1)S(1)}, u32[]{:S(2)}, u32[]{:S(2)}) collective-permute-start(bf16[3,32,512]{2,1,0:T(8,128)(2,1)S(1)} %pad_maximum_fusion.1), channel_id=1, source_target_pairs={{0,2},{1,3},{2,0},{3,1},{4,6},{5,7},{6,4},{7,5},{8,10},{9,11},{10,... | collective-permute-start | bytes 294920 | tf_op jit(solution)/shard_map/ppermute | solution.py:360
  26.3 7.5 %collective-permute-start.9 = (bf16[32,1024]{1,0:T(8,128)(2,1)S(1)}, bf16[32,1024]{1,0:T(8,128)(2,1)S(1)}, u32[]{:S(2)}, u32[]{:S(2)}) collective-permute-start(bf16[32,1024]{1,0:T(8,128)(2,1)S(1)} %pad_maximum_fusion.3), channel_id=1, source_target_pairs={{0,14},{1,15},{2,12},{3,13},{4,10},{5,11},{6,8},{7,9},{8,6},{9,7},... | collective-permute-start | bytes 196616 | tf_op jit(solution)/shard_map/ppermute | solution.py:362
  29.4 5.3 %collective-permute-start.11 = (bf16[32,1024]{1,0:T(8,128)(2,1)S(1)}, bf16[32,1024]{1,0:T(8,128)(2,1)S(1)}, u32[]{:S(2)}, u32[]{:S(2)}) collective-permute-start(bf16[32,1024]{1,0:T(8,128)(2,1)S(1)} %get-tuple-element.43), channel_id=1, source_target_pairs={{0,8},{1,9},{2,10},{3,11},{4,12},{5,13},{6,14},{7,15},{8,0},{9,1},... | collective-permute-start | bytes 196616 | tf_op jit(solution)/shard_map/ppermute | solution.py:364
  30.7 4.6 %collective-permute-start.10 = (bf16[32,1024]{1,0:T(8,128)(2,1)S(1)}, bf16[32,1024]{1,0:T(8,128)(2,1)S(1)}, u32[]{:S(2)}, u32[]{:S(2)}) collective-permute-start(bf16[32,1024]{1,0:T(8,128)(2,1)S(1)} %get-tuple-element.44), channel_id=1, source_target_pairs={{0,4},{1,5},{2,6},{3,7},{4,0},{5,1},{6,2},{7,3},{8,12},{9,13},{10,... | collective-permute-start | bytes 196616 | tf_op jit(solution)/shard_map/ppermute | solution.py:364
